TPU v7x, 32 devices: a whole 2x2x4 slice. The times are simulated.
32 devices in a mesh: section: 4 (over y, x), zone: 8 (over z, core).
Axes of the slice: x: 2, y: 2, z: 4, core: 2. Of those that a mesh axis runs over, the one named last changes fastest.
Arguments:
- tiles: bfloat16 [4, 256, 128, 128], P('section', 'zone'), may hold values from -0.5 to 0.5
- tile_row: int32 [4, 256], P('section', 'zone'), may hold values from 0 to 19
- tile_col: int32 [4, 256], P('section', 'zone'), may hold values from 0 to 15, as said below
- tile_live: int32 [4, 256], P('section', 'zone'), may hold values from 0 to 1, as said below
- block_place: int32 [16], replicated, may hold values from 0 to 15, as said below
- demand: int32 [4, 20480, 128], P('section', 'zone'), may hold values from 0 to 15
- flow_cost: float32 [4, 2048], P('section', 'zone'), may hold values from -6 to 6
- stock_cost: float32 [4, 20480], P('section', 'zone'), may hold values from 0.1 to 1
- flows: float32 [4, 2048, 128], P('section', 'zone'), may hold values from 0 to 1
- stock: float32 [4, 20480, 128], P('section', 'zone'), may hold values from 0 to 2
- duals: float32 [4, 20480, 128], P('section', 'zone'), may hold values from -6 to 6
Outputs:
- flows_out: float32 [4, 2048, 128], P('section', 'zone')
- stock_out: float32 [4, 20480, 128], P('section', 'zone')
- duals_out: float32 [4, 20480, 128], P('section', 'zone')
Inputs may be any that keep to these rules, and one draw needn't show every extreme that they name: `tile_col`: flow block ids. For each phase and zone band, at most 4 live slots name flow blocks whose position // 2 is one given band; in each phase one band receives exactly 4 such slots from every zone band. `tile_live`: live flags of the slots, with the counts described for tile_col. `block_place`: A permutation of the flow blocks.
All inputs are finite; a program needn't handle non-finite values.
Results may differ from a plain program's by a relative error of at most 0.019.
Values may be sent and summed in bfloat16 or wider, within the bound.
No kernel may reach another device: no remote copies, remote signals or barrier semaphores. Data moves between devices by JAX's collectives and lax.ppermute only.
A program may use at most 128 MiB of HBM per device.

v0:
```python
import jax
import jax.numpy as jnp
from jax import lax
from jax.sharding import PartitionSpec as P

ITERS = 2


STEP_PRIMAL = 0.25
STEP_DUAL = 0.25


def from_behind(value, axis, by):
    size = lax.axis_size(axis)
    return lax.ppermute(value, axis, [(i, (i + by) % size) for i in range(size)])


def per_device(
    tiles,
    tile_row,
    tile_col,
    tile_live,
    block_place,
    demand,
    flow_cost,
    stock_cost,
    flows,
    stock,
    duals,
):
    phase_count, slot_count, tile_size, unused_size = tiles.shape
    scenarios = flows.shape[2]
    zone_count = lax.axis_size("zone")
    blocks_total = block_place.shape[0]
    block_local = blocks_total // zone_count
    band_tiles = duals.shape[1] // tile_size
    width_flat = tile_size * scenarios
    alive = tile_live == 1
    position = block_place[tile_col]
    demand_rhs = demand.astype(jnp.float32) * 0.25
    phase_ids = jnp.arange(phase_count, dtype=jnp.int32)[:, None]
    block_ids = jnp.where(alive, position, -1)
    row_live = jnp.where(alive, tile_row, band_tiles)
    for iteration in range(ITERS):
        dual_half = duals.astype(jnp.bfloat16).reshape(
            phase_count, band_tiles, tile_size, scenarios
        )
        dual_picked = jnp.take_along_axis(dual_half, tile_row[:, :, None, None], axis=1)
        partial_value = jnp.einsum(
            "snij,snic->snjc", tiles, dual_picked, preferred_element_type=jnp.float32
        )
        partial_value = partial_value.astype(jnp.bfloat16).reshape(
            phase_count, slot_count, width_flat
        )
        shifted = jnp.where(block_ids >= 0, block_ids, -1)
        shifted = jnp.where(shifted < lax.axis_size("zone") * block_local, shifted, -1)

        def one_phase(values, segment_ids):
            return jax.ops.segment_sum(
                values.astype(jnp.float32),
                segment_ids,
                num_segments=lax.axis_size("zone") * block_local,
            )

        summed_blocks = jax.vmap(one_phase)(partial_value, shifted)
        summed = lax.psum_scatter(
            jnp.transpose(summed_blocks, (1, 0, 2)), "zone", scatter_dimension=0, tiled=True
        )
        pulled = jnp.transpose(summed, (1, 0, 2))
        pulled = pulled.reshape(phase_count, block_local * tile_size, scenarios)
        dual_edge = from_behind(duals, "section", -1)
        dual_after = jnp.concatenate([duals[1:], dual_edge], axis=0)
        new_flows = jnp.maximum(flows - STEP_PRIMAL * (flow_cost[:, :, None] - pulled), 0.0)
        new_stock = jnp.maximum(
            stock - STEP_PRIMAL * (stock_cost[:, :, None] - dual_after + duals), 0.0
        )
        flows_bar = (2.0 * new_flows - flows).astype(jnp.bfloat16)
        stock_bar = 2.0 * new_stock - stock
        gathered = lax.all_gather(flows_bar, "zone", axis=1, tiled=True).reshape(
            phase_count, blocks_total, tile_size, scenarios
        )
        flow_picked = jnp.take_along_axis(gathered, position[:, :, None, None], axis=1)
        products = jnp.einsum(
            "snij,snjc->snic", tiles, flow_picked, preferred_element_type=jnp.float32
        )
        pushed = (
            jnp.zeros((phase_count, band_tiles, tile_size, scenarios), jnp.float32)
            .at[phase_ids, row_live]
            .add(products, mode="drop")
        )
        pushed = pushed.reshape(phase_count, band_tiles * tile_size, scenarios)
        stock_edge = from_behind(stock_bar, "section", 1)
        stock_before = jnp.concatenate([stock_edge, stock_bar[:-1]], axis=0)
        duals = duals + STEP_DUAL * (demand_rhs - (pushed + stock_before - stock_bar))
        flows = new_flows
        stock = new_stock
    return (flows, stock, duals)


def solution(mesh):
    in_specs = (
        P("section", "zone", None, None),
        P("section", "zone"),
        P("section", "zone"),
        P("section", "zone"),
        P(),
        P("section", "zone", None),
        P("section", "zone"),
        P("section", "zone"),
        P("section", "zone", None),
        P("section", "zone", None),
        P("section", "zone", None),
    )
    out_specs = (P("section", "zone", None), P("section", "zone", None), P("section", "zone", None))
    return jax.shard_map(
        per_device, mesh=mesh, in_specs=in_specs, out_specs=out_specs, check_vma=False
    )
```

profile of v0, /device:TPU:0, one launch (start us, length us, event | category | flops | bytes accessed | tf_op | source)
XLA Modules:
  0.0 255.2 jit_solution(14325503921861368230)
XLA Ops:
  7.2 3.9 %collective-permute-start = (f32[1,2560,128]{2,1,0:T(8,128)}, f32[1,2560,128]{2,1,0:T(8,128)S(1)}, u32[]{:S(2)}, u32[]{:S(2)}) collective-permute-start(f32[1,2560,128]{2,1,0:T(8,128)} %param.25), channel_id=1, source_target_pairs={{0,24},{8,0},{16,8},{24,16},{1,25},{9,1},{17,9},{25,17},{2,26},{10... | collective-permute-start | bytes 3932168 | tf_op jit(solution)/shard_map/ppermute | solution.py:15
  17.9 21.7 %collective-permute-done = f32[1,2560,128]{2,1,0:T(8,128)S(1)} collective-permute-done((f32[1,2560,128]{2,1,0:T(8,128)}, f32[1,2560,128]{2,1,0:T(8,128)S(1)}, u32[]{:S(2)}, u32[]{:S(2)}) %collective-permute-start) | collective-permute-done | bytes 1310752 | tf_op jit(solution)/shard_map/ppermute | solution.py:15
  39.5 4.0 %multiply_subtract_fusion.1 = (f32[1,2560,128]{2,1,0:T(8,128)}, f32[1,2560,128]{2,1,0:T(8,128)}, bf16[1,2560,128]{2,1,0:T(8,128)(2,1)S(1)}) fusion(f32[1,2560,128]{2,1,0:T(8,128)} %param.24, f32[1,2560,128]{2,1,0:T(8,128)} %param.25, f32[1,2560,128]{2,1,0:T(8,128)S(1)} %collective-permute-done, f32[2560]{0:T(1024)S(1)} %reduce), kind=kLoop, calls=%fused_computation.33 | loop fusion | flops 2621440 | bytes 7219200 | tf_op jit(solution)/shard_map/sub | solution.py:78
  47.0 1.9 copy.25
  48.9 6.2 %scatter_custom_fusion.2 = f32[16,16384]{1,0:T(8,128)} fusion(s32[32]{0:T(128)S(1)} %fusion.33, f32[4,8,128,128]{3,2,1,0:T(8,128)} %bitcast.144, f32[]{:T(128)} %constant.3.clone.1), kind=kCustom, calls=%fused_computation.12 | custom fusion | flops 524288 | bytes 3145732 | tf_op jit(solution)/shard_map/vmap()/scatter-add | solution.py:59
  55.2 2.4 collective-permute-start.1
  57.6 58.6 %all-reduce.6.cloned.1.call-done = f32[16,1,16384]{2,0,1:T(8,128)} async-done(((f32[16,1,16384]{2,0,1:T(8,128)}), f32[16,1,16384]{2,0,1:T(8,128)}) %all-reduce.6.cloned.1.call-update) | async-done | bytes 1048592
  117.5 14.8 %all_gather.6 = bf16[1,2048,128]{2,1,0:T(8,128)(2,1)S(1)} all-gather(bf16[1,256,128]{2,1,0:T(8,128)(2,1)S(1)} %subtract_convert_fusion.1), channel_id=1, replica_groups=mesh['section'=4,'zone'=8] {'zone'}, dimensions={1}, use_global_device_ids=true | all-gather | bytes 589824 | tf_op jit(solution)/shard_map/all_gather | solution.py:79
  134.0 2.2 convolution_bitcast_fusion.1
  136.2 1.9 copy.27
  138.2 4.7 %scatter_fusion = f32[20,128,128]{2,1,0:T(8,128)S(1)} fusion(f32[20,128,128]{2,1,0:T(8,128)S(1)} %broadcast.166.clone, s32[32]{0:T(128)S(1)} %fusion.32, f32[32,128,128]{2,1,0:T(8,128)} %copy.27), kind=kCustom, calls=%fused_computation.5 | custom fusion | flops 524288 | bytes 6291584 | tf_op jit(solution)/shard_map/scatter-add | solution.py:89
  142.9 3.9 %fusion.43 = (bf16[1,2560,128]{2,1,0:T(8,128)(2,1)S(1)}, f32[1,2560,128]{2,1,0:T(8,128)}) fusion(f32[1,2560,128]{2,1,0:T(8,128)} %param.25, f32[1,2560,128]{2,1,0:T(8,128)} %get-tuple-element.11, f32[1,2560,128]{2,1,0:T(8,128)} %collective-permute-done.1, s32[1,2560,128]{2,1,0:T(8,128)} %param.20, f32[1,2560,128]{2,1,0:T(8,128)S(1)} %bitcast.142), kind=kLoop, calls=%fused_computation.92 | loop fusion | flops 2621440 | bytes 8519680 | tf_op jit(solution)/shard_map/convert_element_type | solution.py:45
  146.8 2.4 collective-permute-start.2
  152.6 1.9 copy.29
  154.5 6.3 %scatter_custom_fusion.3 = f32[16,16384]{1,0:T(8,128)} fusion(s32[32]{0:T(128)S(1)} %fusion.33, f32[4,8,128,128]{3,2,1,0:T(8,128)} %bitcast.143, f32[]{:T(128)} %constant.3.clone.1), kind=kCustom, calls=%fused_computation.9 | custom fusion | flops 524288 | bytes 3145732 | tf_op jit(solution)/shard_map/vmap()/scatter-add | solution.py:59
  160.8 17.3 %collective-permute-done.2 = f32[1,2560,128]{2,1,0:T(8,128)} collective-permute-done((f32[1,2560,128]{2,1,0:T(8,128)}, f32[1,2560,128]{2,1,0:T(8,128)}, u32[]{:S(2)}, u32[]{:S(2)}) %collective-permute-start.2) | collective-permute-done | bytes 1310752 | tf_op jit(solution)/shard_map/ppermute | solution.py:15
  178.1 3.6 %multiply_subtract_fusion = (f32[1,2560,128]{2,1,0:T(8,128)}, f32[1,2560,128]{2,1,0:T(8,128)}) fusion(f32[1,2560,128]{2,1,0:T(8,128)S(1)} %copy-done.1, f32[1,2560,128]{2,1,0:T(8,128)} %get-tuple-element.10, f32[1,2560,128]{2,1,0:T(8,128)} %collective-permute-done.2, f32[2560]{0:T(1024)S(1)} %reduce), kind=kLoop, calls=%fused_computation.31 | loop fusion | flops 2293760 | bytes 6563840 | tf_op jit(solution)/shard_map/sub | solution.py:78
  181.8 2.4 collective-permute-start.3
  184.1 33.0 %all-reduce.8.cloned.1.call-done = f32[16,1,16384]{2,0,1:T(8,128)} async-done(((f32[16,1,16384]{2,0,1:T(8,128)}), f32[16,1,16384]{2,0,1:T(8,128)}) %all-reduce.8.cloned.1.call-update) | async-done | bytes 1048592
  219.1 14.8 %all_gather.7 = bf16[1,2048,128]{2,1,0:T(8,128)(2,1)S(1)} all-gather(bf16[1,256,128]{2,1,0:T(8,128)(2,1)S(1)} %get-tuple-element.5), channel_id=1, replica_groups=mesh['section'=4,'zone'=8] {'zone'}, dimensions={1}, use_global_device_ids=true | all-gather | bytes 589824 | tf_op jit(solution)/shard_map/all_gather | solution.py:79
  235.6 2.2 convolution_bitcast_fusion
  237.8 1.9 copy.31
  239.8 4.7 %scatter_fusion.1 = f32[20,128,128]{2,1,0:T(8,128)S(1)} fusion(f32[20,128,128]{2,1,0:T(8,128)S(1)} %broadcast.166, s32[32]{0:T(128)S(1)} %fusion.32, f32[32,128,128]{2,1,0:T(8,128)} %copy.31), kind=kCustom, calls=%fused_computation.6 | custom fusion | flops 524288 | bytes 6291584 | tf_op jit(solution)/shard_map/scatter-add | solution.py:89
  244.5 3.9 %fusion.9 = f32[1,2560,128]{2,1,0:T(8,128)} fusion(f32[1,2560,128]{2,1,0:T(8,128)} %get-tuple-element.10, f32[1,2560,128]{2,1,0:T(8,128)} %get-tuple-element.7, f32[1,2560,128]{2,1,0:T(8,128)} %collective-permute-done.3, s32[1,2560,128]{2,1,0:T(8,128)} %param.20, f32[1,2560,128]{2,1,0:T(8,128)S(1)} %bitcast.141), kind=kLoop, calls=%fused_computation.25 | loop fusion | flops 2293760 | bytes 7864320 | tf_op jit(solution)/shard_map/add | solution.py:94
  (43 shorter events, 20.0 us)
Async XLA Ops:
  7.2 38.0 %copy-start = (bf16[1,32,128,128]{3,2,1,0:T(8,128)(2,1)S(1)}, bf16[1,32,128,128]{3,2,1,0:T(8,128)(2,1)}, u32[]{:S(2)}) copy-start(bf16[1,32,128,128]{3,2,1,0:T(8,128)(2,1)} %param.15) | copy-start | bytes 3145732
  7.2 108.9 %all-reduce.6.cloned.1.call-start = ((), (), s32[]{:S(2)}) async-start(), calls=%async_computation | async-start | bytes 2097152
  7.2 32.3 %collective-permute-start = (f32[1,2560,128]{2,1,0:T(8,128)}, f32[1,2560,128]{2,1,0:T(8,128)S(1)}, u32[]{:S(2)}, u32[]{:S(2)}) collective-permute-start(f32[1,2560,128]{2,1,0:T(8,128)} %param.25), channel_id=1, source_target_pairs={{0,24},{8,0},{16,8},{24,16},{1,25},{9,1},{17,9},{25,17},{2,26},{10... | collective-permute-start | bytes 3932168 | tf_op jit(solution)/shard_map/ppermute | solution.py:15
  55.0 62.3 %copy-start.2 = (f32[1,256,128]{2,1,0:T(8,128)S(1)}, f32[1,256,128]{2,1,0:T(8,128)}, u32[]{:S(2)}) copy-start(f32[1,256,128]{2,1,0:T(8,128)} %param.23) | copy-start | bytes 393220
  55.0 62.3 %copy-start.3 = (f32[1,256]{1,0:T(1,128)S(1)}, f32[1,256]{1,0:T(1,128)}, u32[]{:S(2)}) copy-start(f32[1,256]{1,0:T(1,128)} %param.21) | copy-start | bytes 3076
  55.1 162.0 %all-reduce.8.cloned.1.call-start = ((), (), s32[]{:S(2)}) async-start(), calls=%async_computation.1 | async-start | bytes 2097152
  55.2 87.7 %collective-permute-start.1 = (f32[1,2560,128]{2,1,0:T(8,128)}, f32[1,2560,128]{2,1,0:T(8,128)}, u32[]{:S(2)}, u32[]{:S(2)}) collective-permute-start(f32[1,2560,128]{2,1,0:T(8,128)} %get-tuple-element.11), channel_id=1, source_target_pairs={{0,8},{8,16},{16,24},{24,0},{1,9},{9,17},{17,25},{25,1},{2,10},{10... | collective-permute-start | bytes 3932168 | tf_op jit(solution)/shard_map/ppermute | solution.py:15
  146.8 31.3 %collective-permute-start.2 = (f32[1,2560,128]{2,1,0:T(8,128)}, f32[1,2560,128]{2,1,0:T(8,128)}, u32[]{:S(2)}, u32[]{:S(2)}) collective-permute-start(f32[1,2560,128]{2,1,0:T(8,128)} %get-tuple-element.10), channel_id=1, source_target_pairs={{0,24},{8,0},{16,8},{24,16},{1,25},{9,1},{17,9},{25,17},{2,26},{10... | collective-permute-start | bytes 3932168 | tf_op jit(solution)/shard_map/ppermute | solution.py:15
  154.5 23.6 %copy-start.1 = (f32[1,2560,128]{2,1,0:T(8,128)S(1)}, f32[1,2560,128]{2,1,0:T(8,128)}, u32[]{:S(2)}) copy-start(f32[1,2560,128]{2,1,0:T(8,128)} %get-tuple-element.12) | copy-start | bytes 3932164
  181.8 62.7 %collective-permute-start.3 = (f32[1,2560,128]{2,1,0:T(8,128)}, f32[1,2560,128]{2,1,0:T(8,128)}, u32[]{:S(2)}, u32[]{:S(2)}) collective-permute-start(f32[1,2560,128]{2,1,0:T(8,128)} %get-tuple-element.7), channel_id=1, source_target_pairs={{0,8},{8,16},{16,24},{24,0},{1,9},{9,17},{17,25},{25,1},{2,10},{10... | collective-permute-start | bytes 3932168 | tf_op jit(solution)/shard_map/ppermute | solution.py:15
Sparse Core Ops, SparseCore 0:
  55.2 60.8 all-reduce.5
  160.9 56.1 all-reduce.7
where the time goes:
time: 256 us; the launch traced here: 255 us
  waiting for transfers between devices  131 us (51%)
  other arithmetic  41.4 us (16%)
  blocking collectives  29.7 us (12%)
  local copies, waits for them, and re-layouts  19.5 us (8%)
  between operations  14.9 us (6%)
  starting transfers between devices  11.1 us (4%)
  matrix products  8.05 us (3%)
    unnamed x4, waiting for transfers between devices  91.6 us
    ppermute x4, waiting for transfers between devices, from_behind(): lax.ppermute(value, axis, [(i, (i + by) % size) for i in range(size)])  39 us
    all_gather x2, blocking collectives, per_device(): lax.all_gather(flows_bar, 'zone', axis=1, tiled=True)  29.7 us
    scatter-add x3, other arithmetic, one_phase(): jax.ops.segment_sum(values.astype(jnp.float32), segment_ids, num_segments...  12.4 us
    ppermute x4, starting transfers between devices, from_behind(): lax.ppermute(value, axis, [(i, (i + by) % size) for i in range(size)])  11.1 us
    scatter-add x2, other arithmetic, per_device(): pushed = jnp.zeros((phase_count, band_tiles, tile_size, scenarios), jnp.f...  9.33 us
    sub x2, other arithmetic, per_device(): stock_bar = 2.0 * new_stock - stock  7.61 us
  transfers between devices with their start and end apart: 6, of which 4 were waited for; matrix products, arithmetic and copies ran while one was open for 18% of the time, Pallas kernels for 0%

commit v1 on v0

v1 whole, which is shorter than its diff:
```python
import functools

import jax
import jax.numpy as jnp
from jax import lax
from jax.experimental import pallas as pl
from jax.experimental.pallas import tpu as pltpu
from jax.sharding import PartitionSpec as P

ITERS = 2

STEP_PRIMAL = 0.25
STEP_DUAL = 0.25

BF = jnp.bfloat16
F32 = jnp.float32
VMEM = pl.BlockSpec(memory_space=pltpu.VMEM)
SMEM = pl.BlockSpec(memory_space=pltpu.SMEM)
LIMIT = 48 * 1024 * 1024
CORES = 2


def rotate(value, axis, by):
    size = lax.axis_size(axis)
    return lax.ppermute(value, axis, [(i, (i + by) % size) for i in range(size)])


def rotate_chip(value, by):
    size = lax.axis_size("zone")
    return lax.ppermute(value, "zone", [(i, (i + by * CORES) % size) for i in range(size)])


def swap_core(value):
    size = lax.axis_size("zone")
    return lax.ppermute(value, "zone", [(i, i ^ 1) for i in range(size)])


def call(kernel, outs, scratch, flops, moved, *args, smem=0):
    return pl.pallas_call(
        kernel,
        out_shape=outs,
        in_specs=[SMEM] * smem + [VMEM] * (len(args) - smem),
        out_specs=jax.tree.map(lambda _: VMEM, outs),
        scratch_shapes=scratch,
        compiler_params=pltpu.CompilerParams(vmem_limit_bytes=LIMIT),
        cost_estimate=pl.CostEstimate(flops=flops, bytes_accessed=moved, transcendentals=0),
    )(*args)


def quarter_rows(by, parts, size):
    part = lax.rem(lax.axis_index("section") + by, parts)
    return pl.ds(pl.multiple_of(part * size, size), size)


def pack_kernel(parts, size, tile, duals, stock, cost, *packets):
    pieces = size // tile
    for r in range(parts):
        part = lax.rem(lax.axis_index("section") + r, parts)
        rows = pl.ds(pl.multiple_of(part * size, size), size)
        packets[r][0:size] = duals[rows, :].astype(BF)
        packets[r][size : 2 * size] = stock[rows, :].astype(BF)
        tail = packets[r].shape[0] - 2 * size
        lines = [
            cost[:, pl.ds(pl.multiple_of(part * size + i * tile, tile), tile)]
            for i in range(pieces)
        ]
        lines.append(jnp.zeros((tail - pieces, tile), F32))
        packets[r][2 * size : 2 * size + tail] = jnp.concatenate(lines, axis=0).astype(BF)


def block_slot(place, col, live, k, shape, sign):
    chips, owned = shape
    zone = lax.axis_index("zone")
    chip, core = lax.div(zone, CORES), lax.rem(zone, CORES)
    position = place[col[0, k]]
    owner, inner = lax.div(position, owned), lax.rem(position, owned)
    away = lax.rem(sign * (lax.div(owner, CORES) - chip) + chips, chips)
    half = jnp.where(lax.rem(owner, CORES) == core, 0, chips * owned)
    return half + away * owned + inner


def pull_slots(shape, row, col, live, place, tiles, half, acc):
    slots = tiles.shape[0]
    blocks = acc.shape[0] - 1
    acc[...] = jnp.zeros_like(acc)

    def step(k, carry):
        there = jnp.where(live[0, k] == 1, block_slot(place, col, live, k, shape, 1), blocks)
        acc[there] += lax.dot_general(
            tiles[k], half[row[0, k]], (((0,), (0,)), ((), ())), preferred_element_type=F32
        )
        return carry

    lax.fori_loop(0, slots, step, 0, unroll=8)


def push_slots(shape, row, col, live, place, tiles, blocks, acc):
    slots = tiles.shape[0]
    spare = acc.shape[0] - 1

    def step(k, carry):
        there = jnp.where(live[0, k] == 1, row[0, k], spare)
        acc[there] += jnp.dot(
            tiles[k],
            blocks[block_slot(place, col, live, k, shape, -1)],
            preferred_element_type=F32,
        )
        return carry

    lax.fori_loop(0, slots, step, 0, unroll=8)


def give_partials(acc, keep, send):
    n = keep.shape[0]
    keep[...] = acc[0:n].astype(BF)
    send[...] = acc[n : 2 * n].astype(BF)


def pull_kernel(shape, row, col, live, place, tiles, duals, keep, send, half, acc):
    half[...] = duals[...].astype(BF)
    pull_slots(shape, row, col, live, place, tiles, half, acc)
    give_partials(acc, keep, send)


def step_duals(shape, parts, size, refs, blocks, acc):
    row, col, live, place, tiles, duals, demand, near, far = refs[:9]
    combined = refs[9:]
    n = near.shape[0]
    blocks[0:n] = near[...]
    blocks[n : 2 * n] = far[...]
    pieces = size // tiles.shape[1]
    for r in range(parts):
        part = lax.rem(lax.axis_index("section") + r, parts)
        rows = pl.ds(part * pieces, pieces)
        acc[rows] = (
            duals[rows]
            + (STEP_DUAL * 0.25) * demand[rows].astype(F32)
            - STEP_DUAL * combined[r][...].astype(F32)
        )
    push_slots(shape, row, col, live, place, tiles, blocks, acc)


def push_pull_kernel(shape, parts, size, *refs):
    ins, rest = refs[: 9 + parts], refs[9 + parts :]
    next_duals, keep, send = rest[:3]
    packets = rest[3 : 3 + parts]
    blocks, half, acc, acc_blocks = rest[3 + parts :]
    row, col, live, place, tiles = ins[:5]
    step_duals(shape, parts, size, ins, blocks, acc)
    n = next_duals.shape[0]
    next_duals[...] = acc[0:n]
    half[...] = acc[0:n].astype(BF)
    pieces = size // tiles.shape[1]
    for r in range(parts):
        part = lax.rem(lax.axis_index("section") + r, parts)
        packets[r][...] = half[pl.ds(part * pieces, pieces)]
    pull_slots(shape, row, col, live, place, tiles, half, acc_blocks)
    give_partials(acc_blocks, keep, send)


def push_kernel(shape, parts, size, *refs):
    ins = refs[: 9 + parts]
    next_duals, blocks, acc = refs[9 + parts :]
    step_duals(shape, parts, size, ins, blocks, acc)
    next_duals[...] = acc[0 : next_duals.shape[0]]


def spread_cost(line, eye, ones):
    return jnp.dot(jnp.where(eye, line, jnp.zeros_like(line)), ones, preferred_element_type=F32)


def eye_of(tile):
    return lax.broadcasted_iota(jnp.int32, (tile, tile), 0) == lax.broadcasted_iota(
        jnp.int32, (tile, tile), 1
    )


def stock_step(parts, tile, i, costs, dual, stock, eye, ones):
    new = []
    for r in range(parts):
        cost = spread_cost(costs[r][i : i + 1], eye, ones)
        change = cost - dual[(r - 1) % parts] + dual[r]
        new.append(jnp.maximum(stock[r] - STEP_PRIMAL * change, 0.0))
    return new


def first_stock_kernel(parts, size, tile, *refs):
    packets, stocks, combined = refs[:parts], refs[parts], refs[parts + 1 :]
    eye, ones = eye_of(tile), jnp.ones((tile, tile), BF)
    costs = [packets[r][2 * size :].astype(F32).astype(BF) for r in range(parts)]
    for i in range(size // tile):
        rows = slice(i * tile, (i + 1) * tile)
        behind = slice(size + i * tile, size + (i + 1) * tile)
        dual = [packets[r][rows].astype(F32) for r in range(parts)]
        stock = [packets[r][behind].astype(F32) for r in range(parts)]
        new = stock_step(parts, tile, i, costs, dual, stock, eye, ones)
        bar = [2.0 * new[r] - stock[r] for r in range(parts)]
        for r in range(parts):
            stocks[r, rows] = new[r]
            combined[r][rows] = (bar[(r + 1) % parts] - bar[r]).astype(BF)


def last_stock_kernel(parts, size, tile, *refs):
    packets, stocks, duals = refs[:parts], refs[parts], refs[parts + 1 : 2 * parts + 1]
    combined, moved = refs[2 * parts + 1 : 3 * parts + 1], refs[3 * parts + 1 :]
    eye, ones = eye_of(tile), jnp.ones((tile, tile), BF)
    costs = [packets[r][2 * size :].astype(F32).astype(BF) for r in range(parts)]
    for i in range(size // tile):
        rows = slice(i * tile, (i + 1) * tile)
        dual = [duals[r][rows].astype(F32) for r in range(parts)]
        stock = [stocks[r, rows] for r in range(parts)]
        new = stock_step(parts, tile, i, costs, dual, stock, eye, ones)
        bar = [2.0 * new[r] - stock[r] for r in range(parts)]
        for r in range(parts):
            moved[r][rows] = new[r].astype(BF)
            combined[r][rows] = (bar[(r + 1) % parts] - bar[r]).astype(BF)


def place_kernel(parts, size, *refs):
    out = refs[parts]
    for r in range(parts):
        out[quarter_rows(r, parts, size), :] = refs[r][...].astype(F32)


def per_device(
    tiles,
    tile_row,
    tile_col,
    tile_live,
    block_place,
    demand,
    flow_cost,
    stock_cost,
    flows,
    stock,
    duals,
):
    unused_phases, slots, tile, unused_tile = tiles.shape
    scenarios = flows.shape[2]
    rows = duals.shape[1]
    parts = lax.axis_size("section")
    zones = lax.axis_size("zone")
    chips = zones // CORES
    blocks = block_place.shape[0]
    owned = blocks // zones
    band_tiles = rows // tile
    size = rows // parts
    shape = (chips, owned)
    tail = -(-(size // tile) // 16) * 16

    tiles = tiles.reshape(slots, tile, tile)
    duals2 = duals.reshape(rows, scenarios)
    stock2 = stock.reshape(rows, scenarios)
    flows2 = flows.reshape(owned * tile, scenarios)
    duals3 = duals.reshape(band_tiles, tile, scenarios)
    demand3 = demand.reshape(band_tiles, tile, scenarios)
    where = (tile_row, tile_col, tile_live, block_place)
    flops = 2 * slots * tile * tile * scenarios
    quarter = jax.ShapeDtypeStruct((size, scenarios), BF)
    quarter3 = jax.ShapeDtypeStruct((size // tile, tile, scenarios), BF)
    half_blocks = jax.ShapeDtypeStruct((blocks // 2, tile, scenarios), BF)
    pull_scratch = [
        pltpu.VMEM((band_tiles, tile, scenarios), BF),
        pltpu.VMEM((blocks + 1, tile, scenarios), F32),
    ]
    push_scratch = [
        pltpu.VMEM((blocks, tile, scenarios), BF),
        pltpu.VMEM((band_tiles + 1, tile, scenarios), F32),
    ]

    def collect(keep, send):
        both = (keep.astype(F32) + swap_core(send).astype(F32)).astype(BF)
        parts_of = [both[k * owned : (k + 1) * owned] for k in range(chips)]
        got = [rotate_chip(parts_of[k], k) for k in range(1, chips)]
        total = parts_of[0].astype(F32)
        for value in got:
            total = total + value.astype(F32)
        return total.reshape(owned * tile, scenarios)

    def spread(value):
        own = [value] + [rotate_chip(value, k) for k in range(1, chips)]
        near = jnp.concatenate(own, axis=0).reshape(blocks // 2, tile, scenarios)
        return near, swap_core(near)

    def step_flows(now, pulled):
        new = jnp.maximum(now - STEP_PRIMAL * (flow_cost[0][:, None] - pulled), 0.0)
        return new, ((2.0 * new - now).astype(BF) * BF(-STEP_DUAL))

    packets = call(
        functools.partial(pack_kernel, parts, size, tile),
        [jax.ShapeDtypeStruct((2 * size + tail, scenarios), BF)] * parts,
        [],
        0,
        12 * rows * scenarios,
        duals2,
        stock2,
        stock_cost,
    )
    packets = [packets[0]] + [rotate(packets[r], "section", r) for r in range(1, parts)]

    keep, send = call(
        functools.partial(pull_kernel, shape),
        [half_blocks, half_blocks],
        pull_scratch,
        flops,
        4 * rows * scenarios + 2 * slots * tile * tile,
        *where,
        tiles,
        duals3,
        smem=4,
    )
    pulled = collect(keep, send)
    flows1, bar1 = step_flows(flows2, pulled)
    near, far = spread(bar1)

    stocks, *combined = call(
        functools.partial(first_stock_kernel, parts, size, tile),
        [jax.ShapeDtypeStruct((parts, size, scenarios), F32)] + [quarter] * parts,
        [],
        0,
        10 * rows * scenarios,
        *packets,
    )
    combined = [combined[0]] + [rotate(combined[r], "section", -r) for r in range(1, parts)]
    combined = [c.reshape(size // tile, tile, scenarios) for c in combined]

    duals1, keep, send, *halves = call(
        functools.partial(push_pull_kernel, shape, parts, size),
        [jax.ShapeDtypeStruct((band_tiles, tile, scenarios), F32), half_blocks, half_blocks]
        + [quarter3] * parts,
        [push_scratch[0], pull_scratch[0], push_scratch[1], pull_scratch[1]],
        2 * flops,
        16 * rows * scenarios + 2 * slots * tile * tile,
        *where,
        tiles,
        duals3,
        demand3,
        near,
        far,
        *combined,
        smem=4,
    )
    halves = [h.reshape(size, scenarios) for h in halves]
    halves = [halves[0]] + [rotate(halves[r], "section", r) for r in range(1, parts)]
    pulled = collect(keep, send)
    flows2_out, bar2 = step_flows(flows1, pulled)
    near, far = spread(bar2)

    outs = call(
        functools.partial(last_stock_kernel, parts, size, tile),
        [quarter] * (2 * parts),
        [],
        0,
        10 * rows * scenarios,
        *packets,
        stocks,
        *halves,
    )
    combined, moved = outs[:parts], outs[parts:]
    combined = [combined[0]] + [rotate(combined[r], "section", -r) for r in range(1, parts)]
    combined = [c.reshape(size // tile, tile, scenarios) for c in combined]
    moved = [moved[0]] + [rotate(moved[r], "section", -r) for r in range(1, parts)]

    duals_out = call(
        functools.partial(push_kernel, shape, parts, size),
        jax.ShapeDtypeStruct((band_tiles, tile, scenarios), F32),
        push_scratch,
        flops,
        14 * rows * scenarios + 2 * slots * tile * tile,
        *where,
        tiles,
        duals1,
        demand3,
        near,
        far,
        *combined,
        smem=4,
    )
    stock_out = call(
        functools.partial(place_kernel, parts, size),
        jax.ShapeDtypeStruct((rows, scenarios), F32),
        [],
        0,
        6 * rows * scenarios,
        *moved,
    )
    return (
        flows2_out.reshape(flows.shape),
        stock_out.reshape(stock.shape),
        duals_out.reshape(duals.shape),
    )


def solution(mesh):
    in_specs = (
        P("section", "zone", None, None),
        P("section", "zone"),
        P("section", "zone"),
        P("section", "zone"),
        P(),
        P("section", "zone", None),
        P("section", "zone"),
        P("section", "zone"),
        P("section", "zone", None),
        P("section", "zone", None),
        P("section", "zone", None),
    )
    out_specs = (P("section", "zone", None), P("section", "zone", None), P("section", "zone", None))
    return jax.shard_map(
        per_device, mesh=mesh, in_specs=in_specs, out_specs=out_specs, check_vma=False
    )
```

time: 256 us -> 90.4 us (0.35)
  waiting for transfers between devices: 131 us -> 32.9 us
  other arithmetic: 41.4 us -> 1.25 us
  blocking collectives: 29.7 us -> 0 us
  starting transfers between devices: 11.1 us -> 38.3 us
  local copies, waits for them, and re-layouts: 19.5 us -> 5.25 us
  between operations: 14.9 us -> 0.92 us
  Pallas kernels: 0 us -> 11.5 us
  matrix products: 8.05 us -> 0 us
    unnamed x4 -> x0, waiting for transfers between devices: 91.6 us -> none
    all_gather x2 -> x0, blocking collectives: 29.7 us -> none  [per_device(): lax.all_gather(flows_bar, 'zone', axis=1, tiled=True)]
    ppermute x4 -> x31, starting transfers between devices: 11.1 us -> 38.3 us  [the longest x15 20.2 us: rotate(): lax.ppermute(value, axis, [(i, (i + by) % size) for i in range(size)])]
    scatter-add x5 -> x0, other arithmetic: 21.8 us -> none  [the longest x3 12.4 us: one_phase(): jax.ops.segment_sum(values.astype(jnp.float32), segment_ids, num_segments...]
    pallas_call x0 -> x7, Pallas kernels: none -> 11.5 us  [call(): pl.pallas_call(kernel, out_shape=outs, in_specs=[SMEM] * smem + [VMEM] *...]
    dot_general x4 -> x0, matrix products: 8.05 us -> none  [the longest x2 4.43 us: per_device(): jnp.einsum('snij,snjc->snic', tiles, flow_picked, preferred_element_type=...]
    gather x5 -> x0, local copies, waits for them, and re-layouts: 8.03 us -> none  [the longest x2 3.34 us: per_device(): jnp.take_along_axis(dual_half, tile_row[:, :, None, None], axis=1)]
    sub x2 -> x0, other arithmetic: 7.61 us -> none  [per_device(): stock_bar = 2.0 * new_stock - stock]
  transfers between devices with their start and end apart: 6 -> 31, of which waited for: 4 -> 19; matrix products, arithmetic and copies ran while one was open for 18% -> 1% of each run, Pallas kernels for 0% -> 3%
where the time goes in v1:
time: 90.4 us; the launch traced here: 90.1 us
  starting transfers between devices  38.3 us (42%)
  waiting for transfers between devices  32.9 us (36%)
  Pallas kernels  11.5 us (13%)
  local copies, waits for them, and re-layouts  5.25 us (6%)
  other arithmetic  1.25 us (1%)
  between operations  0.92 us (1%)
    ppermute x15, starting transfers between devices, rotate(): lax.ppermute(value, axis, [(i, (i + by) % size) for i in range(size)])  20.2 us
    ppermute x15, waiting for transfers between devices, rotate(): lax.ppermute(value, axis, [(i, (i + by) % size) for i in range(size)])  17.8 us
    ppermute x12, starting transfers between devices, rotate_chip(): lax.ppermute(value, 'zone', [(i, (i + by * CORES) % size) for i in range(...  17.3 us
    ppermute x12, waiting for transfers between devices, rotate_chip(): lax.ppermute(value, 'zone', [(i, (i + by * CORES) % size) for i in range(...  12.4 us
    pallas_call x7, Pallas kernels, call(): pl.pallas_call(kernel, out_shape=outs, in_specs=[SMEM] * smem + [VMEM] *...  11.5 us
    unnamed x34, local copies, waits for them, and re-layouts  5.22 us
    ppermute x4, waiting for transfers between devices, swap_core(): return lax.ppermute(value, 'zone', [(i, i ^ 1) for i in range(size)])  2.69 us
  transfers between devices with their start and end apart: 31, of which 19 were waited for; matrix products, arithmetic and copies ran while one was open for 1% of the time, Pallas kernels for 3%

profile of v1, /device:TPU:0, one launch (start us, length us, event | category | flops | bytes accessed | tf_op | source)
XLA Modules:
  0.0 90.1 jit_solution(10505554032539293819)
XLA Ops:
  5.8 1.8 %shard_map.133 = (bf16[8,128,128]{2,1,0:T(8,128)(2,1)S(1)}, bf16[8,128,128]{2,1,0:T(8,128)(2,1)S(1)}) custom-call(s32[1,32]{1,0:T(1,128)S(1)} %copy-done.7, s32[1,32]{1,0:T(1,128)S(1)} %copy-done.9, s32[1,32]{1,0:T(1,128)S(1)} %copy-done.11, s32[16]{0:T(128)S(1)} %copy-done.13, bf16[32,128,128]{2,1,0:T(8,128)(2,1)S(1)} %bitcast.84, f32[20,128,128]{2,1,0:T(8,128)S(1)} %bitcast.81), custom_call_target="tpu_custom_call" | custom-call | flops 134217728 | bytes 2359296 | tf_op jit(solution)/shard_map/pallas_call | solution.py:39
  9.5 5.0 %collective-permute-start.3 = (bf16[2,128,128]{2,1,0:T(8,128)(2,1)S(1)}, bf16[2,128,128]{2,1,0:T(8,128)(2,1)S(1)}, u32[]{:S(2)}, u32[]{:S(2)}) collective-permute-start(bf16[2,128,128]{2,1,0:T(8,128)(2,1)S(1)} %get-tuple-element.59), channel_id=1, source_target_pairs={{0,6},{1,7},{2,0},{3,1},{4,2},{5,3},{6,4},{7,5},{8,14},{9,15},{10,... | collective-permute-start | bytes 196616 | tf_op jit(solution)/shard_map/ppermute | solution.py:30
  17.0 4.3 %collective-permute-done.2 = bf16[2,128,128]{2,1,0:T(8,128)(2,1)S(1)} collective-permute-done((bf16[2,128,128]{2,1,0:T(8,128)(2,1)S(1)}, bf16[2,128,128]{2,1,0:T(8,128)(2,1)S(1)}, u32[]{:S(2)}, u32[]{:S(2)}) %collective-permute-start.2) | collective-permute-done | bytes 65568 | tf_op jit(solution)/shard_map/ppermute | solution.py:30
  21.4 1.9 %collective-permute-start.6 = (bf16[256,128]{1,0:T(8,128)(2,1)S(1)}, bf16[256,128]{1,0:T(8,128)(2,1)S(1)}, u32[]{:S(2)}, u32[]{:S(2)}) collective-permute-start(bf16[256,128]{1,0:T(8,128)(2,1)S(1)} %fusion.16), channel_id=1, source_target_pairs={{0,6},{1,7},{2,0},{3,1},{4,2},{5,3},{6,4},{7,5},{8,14},{9,15},{10,... | collective-permute-start | bytes 196616 | tf_op jit(solution)/shard_map/ppermute | solution.py:30
  23.5 1.6 %collective-permute-start.8 = (bf16[1296,128]{1,0:T(8,128)(2,1)S(1)}, bf16[1296,128]{1,0:T(8,128)(2,1)S(1)}, u32[]{:S(2)}, u32[]{:S(2)}) collective-permute-start(bf16[1296,128]{1,0:T(8,128)(2,1)S(1)} %get-tuple-element.32), channel_id=1, source_target_pairs={{0,8},{8,16},{16,24},{24,0},{1,9},{9,17},{17,25},{25,1},{2,10},{10... | collective-permute-start | bytes 995336 | tf_op jit(solution)/shard_map/ppermute | solution.py:25
  25.1 1.5 %collective-permute-start.9 = (bf16[1296,128]{1,0:T(8,128)(2,1)S(1)}, bf16[1296,128]{1,0:T(8,128)(2,1)S(1)}, u32[]{:S(2)}, u32[]{:S(2)}) collective-permute-start(bf16[1296,128]{1,0:T(8,128)(2,1)S(1)} %get-tuple-element.33), channel_id=1, source_target_pairs={{0,16},{8,24},{16,0},{24,8},{1,17},{9,25},{17,1},{25,9},{2,18},{10... | collective-permute-start | bytes 995336 | tf_op jit(solution)/shard_map/ppermute | solution.py:25
  28.0 1.9 %collective-permute-start.4 = (bf16[256,128]{1,0:T(8,128)(2,1)S(1)}, bf16[256,128]{1,0:T(8,128)(2,1)S(1)}, u32[]{:S(2)}, u32[]{:S(2)}) collective-permute-start(bf16[256,128]{1,0:T(8,128)(2,1)S(1)} %fusion.16), channel_id=1, source_target_pairs={{0,2},{1,3},{2,4},{3,5},{4,6},{5,7},{6,0},{7,1},{8,10},{9,11},{10,... | collective-permute-start | bytes 196616 | tf_op jit(solution)/shard_map/ppermute | solution.py:30
  30.0 3.5 %collective-permute-done.5 = bf16[256,128]{1,0:T(8,128)(2,1)S(1)} collective-permute-done((bf16[256,128]{1,0:T(8,128)(2,1)S(1)}, bf16[256,128]{1,0:T(8,128)(2,1)S(1)}, u32[]{:S(2)}, u32[]{:S(2)}) %collective-permute-start.5) | collective-permute-done | bytes 65568 | tf_op jit(solution)/shard_map/ppermute | solution.py:30
  35.2 4.5 %collective-permute-done.9.refs_2_ = bf16[1296,128]{1,0:T(8,128)(2,1)S(1)} collective-permute-done((bf16[1296,128]{1,0:T(8,128)(2,1)S(1)}, bf16[1296,128]{1,0:T(8,128)(2,1)S(1)}, u32[]{:S(2)}, u32[]{:S(2)}) %collective-permute-start.9) | collective-permute-done | bytes 331808 | tf_op jit(solution)/shard_map/ppermute | solution.py:25
  40.5 1.7 %collective-permute-start.11 = (bf16[640,128]{1,0:T(8,128)(2,1)S(1)}, bf16[640,128]{1,0:T(8,128)(2,1)S(1)}, u32[]{:S(2)}, u32[]{:S(2)}) collective-permute-start(bf16[640,128]{1,0:T(8,128)(2,1)S(1)} %get-tuple-element.36), channel_id=1, source_target_pairs={{0,24},{8,0},{16,8},{24,16},{1,25},{9,1},{17,9},{25,17},{2,26},{10... | collective-permute-start | bytes 491528 | tf_op jit(solution)/shard_map/ppermute | solution.py:25
  42.2 1.5 %collective-permute-start.12 = (bf16[640,128]{1,0:T(8,128)(2,1)S(1)}, bf16[640,128]{1,0:T(8,128)(2,1)S(1)}, u32[]{:S(2)}, u32[]{:S(2)}) collective-permute-start(bf16[640,128]{1,0:T(8,128)(2,1)S(1)} %get-tuple-element.37), channel_id=1, source_target_pairs={{0,16},{8,24},{16,0},{24,8},{1,17},{9,25},{17,1},{25,9},{2,18},{10... | collective-permute-start | bytes 491528 | tf_op jit(solution)/shard_map/ppermute | solution.py:25
  44.0 3.6 %collective-permute-done.11 = bf16[640,128]{1,0:T(8,128)(2,1)S(1)} collective-permute-done((bf16[640,128]{1,0:T(8,128)(2,1)S(1)}, bf16[640,128]{1,0:T(8,128)(2,1)S(1)}, u32[]{:S(2)}, u32[]{:S(2)}) %collective-permute-start.11) | collective-permute-done | bytes 163872 | tf_op jit(solution)/shard_map/ppermute | solution.py:25
  47.6 2.3 %collective-permute-done.12 = bf16[640,128]{1,0:T(8,128)(2,1)S(1)} collective-permute-done((bf16[640,128]{1,0:T(8,128)(2,1)S(1)}, bf16[640,128]{1,0:T(8,128)(2,1)S(1)}, u32[]{:S(2)}, u32[]{:S(2)}) %collective-permute-start.12) | collective-permute-done | bytes 163872 | tf_op jit(solution)/shard_map/ppermute | solution.py:25
  51.0 4.0 %shard_map.136 = (f32[20,128,128]{2,1,0:T(8,128)S(1)}, bf16[8,128,128]{2,1,0:T(8,128)(2,1)S(1)}, bf16[8,128,128]{2,1,0:T(8,128)(2,1)S(1)}, bf16[5,128,128]{2,1,0...) custom-call(s32[1,32]{1,0:T(1,128)S(1)} %copy-done.7, ...), custom_call_target="tpu_custom_call" | custom-call | flops 268435456 | bytes 6291456 | tf_op jit(solution)/shard_map/pallas_call | solution.py:39
  55.1 1.5 %collective-permute-done.14 = bf16[8,128,128]{2,1,0:T(8,128)(2,1)S(1)} collective-permute-done((bf16[8,128,128]{2,1,0:T(8,128)(2,1)S(1)}, bf16[8,128,128]{2,1,0:T(8,128)(2,1)S(1)}, u32[]{:S(2)}, u32[]{:S(2)}) %collective-permute-start.14) | collective-permute-done | bytes 262176 | tf_op jit(solution)/shard_map/ppermute | solution.py:35
  56.7 2.3 %collective-permute-start.17 = (bf16[2,128,128]{2,1,0:T(8,128)(2,1)S(1)}, bf16[2,128,128]{2,1,0:T(8,128)(2,1)S(1)}, u32[]{:S(2)}, u32[]{:S(2)}) collective-permute-start(bf16[2,128,128]{2,1,0:T(8,128)(2,1)S(1)} %get-tuple-element.56), channel_id=1, source_target_pairs={{0,6},{1,7},{2,0},{3,1},{4,2},{5,3},{6,4},{7,5},{8,14},{9,15},{10,... | collective-permute-start | bytes 196616 | tf_op jit(solution)/shard_map/ppermute | solution.py:30
  61.5 2.7 %collective-permute-start.20 = (bf16[640,128]{1,0:T(8,128)(2,1)S(1)}, bf16[640,128]{1,0:T(8,128)(2,1)S(1)}, u32[]{:S(2)}, u32[]{:S(2)}) collective-permute-start(bf16[640,128]{1,0:T(8,128)(2,1)S(1)} %bitcast.103), channel_id=1, source_target_pairs={{0,24},{8,0},{16,8},{24,16},{1,25},{9,1},{17,9},{25,17},{2,26},{10... | collective-permute-start | bytes 491528 | tf_op jit(solution)/shard_map/ppermute | solution.py:25
  64.2 1.8 %collective-permute-done.16 = bf16[2,128,128]{2,1,0:T(8,128)(2,1)S(1)} collective-permute-done((bf16[2,128,128]{2,1,0:T(8,128)(2,1)S(1)}, bf16[2,128,128]{2,1,0:T(8,128)(2,1)S(1)}, u32[]{:S(2)}, u32[]{:S(2)}) %collective-permute-start.16) | collective-permute-done | bytes 65568 | tf_op jit(solution)/shard_map/ppermute | solution.py:30
  66.2 1.7 %collective-permute-start.26 = (bf16[256,128]{1,0:T(8,128)(2,1)S(1)}, bf16[256,128]{1,0:T(8,128)(2,1)S(1)}, u32[]{:S(2)}, u32[]{:S(2)}) collective-permute-start(bf16[256,128]{1,0:T(8,128)(2,1)S(1)} %fusion.17), channel_id=1, source_target_pairs={{0,6},{1,7},{2,0},{3,1},{4,2},{5,3},{6,4},{7,5},{8,14},{9,15},{10,... | collective-permute-start | bytes 196616 | tf_op jit(solution)/shard_map/ppermute | solution.py:30
  68.5 2.0 %collective-permute-start.24 = (bf16[256,128]{1,0:T(8,128)(2,1)S(1)}, bf16[256,128]{1,0:T(8,128)(2,1)S(1)}, u32[]{:S(2)}, u32[]{:S(2)}) collective-permute-start(bf16[256,128]{1,0:T(8,128)(2,1)S(1)} %fusion.17), channel_id=1, source_target_pairs={{0,2},{1,3},{2,4},{3,5},{4,6},{5,7},{6,0},{7,1},{8,10},{9,11},{10,... | collective-permute-start | bytes 196616 | tf_op jit(solution)/shard_map/ppermute | solution.py:30
  75.1 1.6 %collective-permute-start.28 = (bf16[640,128]{1,0:T(8,128)(2,1)S(1)}, bf16[640,128]{1,0:T(8,128)(2,1)S(1)}, u32[]{:S(2)}, u32[]{:S(2)}) collective-permute-start(bf16[640,128]{1,0:T(8,128)(2,1)S(1)} %get-tuple-element.52), channel_id=1, source_target_pairs={{0,24},{8,0},{16,8},{24,16},{1,25},{9,1},{17,9},{25,17},{2,26},{10... | collective-permute-start | bytes 491528 | tf_op jit(solution)/shard_map/ppermute | solution.py:25
  78.4 1.7 %collective-permute-start.30 = (bf16[640,128]{1,0:T(8,128)(2,1)S(1)}, bf16[640,128]{1,0:T(8,128)(2,1)S(1)}, u32[]{:S(2)}, u32[]{:S(2)}) collective-permute-start(bf16[640,128]{1,0:T(8,128)(2,1)S(1)} %get-tuple-element.54), channel_id=1, source_target_pairs={{0,8},{8,16},{16,24},{24,0},{1,9},{9,17},{17,25},{25,1},{2,10},{10... | collective-permute-start | bytes 491528 | tf_op jit(solution)/shard_map/ppermute | solution.py:25
  83.6 3.4 %collective-permute-done.29 = bf16[640,128]{1,0:T(8,128)(2,1)S(1)} collective-permute-done((bf16[640,128]{1,0:T(8,128)(2,1)S(1)}, bf16[640,128]{1,0:T(8,128)(2,1)S(1)}, u32[]{:S(2)}, u32[]{:S(2)}) %collective-permute-start.29) | collective-permute-done | bytes 163872 | tf_op jit(solution)/shard_map/ppermute | solution.py:25
  87.1 3.0 %shard_map.139 = f32[20,128,128]{2,1,0:T(8,128)} custom-call(s32[1,32]{1,0:T(1,128)S(1)} %copy-done.8, s32[1,32]{1,0:T(1,128)S(1)} %copy-done.10, s32[1,32]{1,0:T(1,128)S(1)} %copy-done.12, s32[16]{0:T(128)S(1)} %copy-done.14, bf16[32,128,128]{2,1,0:T(8,128)(2,1)S(1)} %bitcast.86, f32[20,128,128]{2,1,0:T(8,128)S(1)} %get-tuple-element.50.refs_5_, ...), custom_call_target="tpu_custom_call" | custom-call | flops 134217728 | bytes 5636096 | tf_op jit(solution)/shard_map/pallas_call | solution.py:39
  (90 shorter events, 28.2 us)
Async XLA Ops:
  9.5 7.5 %collective-permute-start.3 = (bf16[2,128,128]{2,1,0:T(8,128)(2,1)S(1)}, bf16[2,128,128]{2,1,0:T(8,128)(2,1)S(1)}, u32[]{:S(2)}, u32[]{:S(2)}) collective-permute-start(bf16[2,128,128]{2,1,0:T(8,128)(2,1)S(1)} %get-tuple-element.59), channel_id=1, source_target_pairs={{0,6},{1,7},{2,0},{3,1},{4,2},{5,3},{6,4},{7,5},{8,14},{9,15},{10,... | collective-permute-start | bytes 196616 | tf_op jit(solution)/shard_map/ppermute | solution.py:30
  14.5 6.8 %collective-permute-start.2 = (bf16[2,128,128]{2,1,0:T(8,128)(2,1)S(1)}, bf16[2,128,128]{2,1,0:T(8,128)(2,1)S(1)}, u32[]{:S(2)}, u32[]{:S(2)}) collective-permute-start(bf16[2,128,128]{2,1,0:T(8,128)(2,1)S(1)} %get-tuple-element.60), channel_id=1, source_target_pairs={{0,4},{1,5},{2,6},{3,7},{4,0},{5,1},{6,2},{7,3},{8,12},{9,13},{10,... | collective-permute-start | bytes 196616 | tf_op jit(solution)/shard_map/ppermute | solution.py:30
  14.5 6.8 %collective-permute-start.1 = (bf16[2,128,128]{2,1,0:T(8,128)(2,1)S(1)}, bf16[2,128,128]{2,1,0:T(8,128)(2,1)S(1)}, u32[]{:S(2)}, u32[]{:S(2)}) collective-permute-start(bf16[2,128,128]{2,1,0:T(8,128)(2,1)S(1)} %get-tuple-element.58), channel_id=1, source_target_pairs={{0,2},{1,3},{2,4},{3,5},{4,6},{5,7},{6,0},{7,1},{8,10},{9,11},{10,... | collective-permute-start | bytes 196616 | tf_op jit(solution)/shard_map/ppermute | solution.py:30
  21.4 6.6 %collective-permute-start.6 = (bf16[256,128]{1,0:T(8,128)(2,1)S(1)}, bf16[256,128]{1,0:T(8,128)(2,1)S(1)}, u32[]{:S(2)}, u32[]{:S(2)}) collective-permute-start(bf16[256,128]{1,0:T(8,128)(2,1)S(1)} %fusion.16), channel_id=1, source_target_pairs={{0,6},{1,7},{2,0},{3,1},{4,2},{5,3},{6,4},{7,5},{8,14},{9,15},{10,... | collective-permute-start | bytes 196616 | tf_op jit(solution)/shard_map/ppermute | solution.py:30
  23.5 11.7 %collective-permute-start.8 = (bf16[1296,128]{1,0:T(8,128)(2,1)S(1)}, bf16[1296,128]{1,0:T(8,128)(2,1)S(1)}, u32[]{:S(2)}, u32[]{:S(2)}) collective-permute-start(bf16[1296,128]{1,0:T(8,128)(2,1)S(1)} %get-tuple-element.32), channel_id=1, source_target_pairs={{0,8},{8,16},{16,24},{24,0},{1,9},{9,17},{17,25},{25,1},{2,10},{10... | collective-permute-start | bytes 995336 | tf_op jit(solution)/shard_map/ppermute | solution.py:25
  25.1 14.6 %collective-permute-start.9 = (bf16[1296,128]{1,0:T(8,128)(2,1)S(1)}, bf16[1296,128]{1,0:T(8,128)(2,1)S(1)}, u32[]{:S(2)}, u32[]{:S(2)}) collective-permute-start(bf16[1296,128]{1,0:T(8,128)(2,1)S(1)} %get-tuple-element.33), channel_id=1, source_target_pairs={{0,16},{8,24},{16,0},{24,8},{1,17},{9,25},{17,1},{25,9},{2,18},{10... | collective-permute-start | bytes 995336 | tf_op jit(solution)/shard_map/ppermute | solution.py:25
  26.6 13.2 %collective-permute-start.10 = (bf16[1296,128]{1,0:T(8,128)(2,1)S(1)}, bf16[1296,128]{1,0:T(8,128)(2,1)S(1)}, u32[]{:S(2)}, u32[]{:S(2)}) collective-permute-start(bf16[1296,128]{1,0:T(8,128)(2,1)S(1)} %get-tuple-element.34), channel_id=1, source_target_pairs={{0,24},{8,0},{16,8},{24,16},{1,25},{9,1},{17,9},{25,17},{2,26},{10... | collective-permute-start | bytes 995336 | tf_op jit(solution)/shard_map/ppermute | solution.py:25
  34.2 16.8 %collective-permute-start.7 = (bf16[8,128,128]{2,1,0:T(8,128)(2,1)S(1)}, bf16[8,128,128]{2,1,0:T(8,128)(2,1)S(1)}, u32[]{:S(2)}, u32[]{:S(2)}) collective-permute-start(bf16[8,128,128]{2,1,0:T(8,128)(2,1)S(1)} %bitcast.90), channel_id=1, source_target_pairs={{0,1},{1,0},{2,3},{3,2},{4,5},{5,4},{6,7},{7,6},{8,9},{9,8},{10,11... | collective-permute-start | bytes 786440 | tf_op jit(solution)/shard_map/ppermute | solution.py:35
  40.5 7.1 %collective-permute-start.11 = (bf16[640,128]{1,0:T(8,128)(2,1)S(1)}, bf16[640,128]{1,0:T(8,128)(2,1)S(1)}, u32[]{:S(2)}, u32[]{:S(2)}) collective-permute-start(bf16[640,128]{1,0:T(8,128)(2,1)S(1)} %get-tuple-element.36), channel_id=1, source_target_pairs={{0,24},{8,0},{16,8},{24,16},{1,25},{9,1},{17,9},{25,17},{2,26},{10... | collective-permute-start | bytes 491528 | tf_op jit(solution)/shard_map/ppermute | solution.py:25
  42.2 7.7 %collective-permute-start.12 = (bf16[640,128]{1,0:T(8,128)(2,1)S(1)}, bf16[640,128]{1,0:T(8,128)(2,1)S(1)}, u32[]{:S(2)}, u32[]{:S(2)}) collective-permute-start(bf16[640,128]{1,0:T(8,128)(2,1)S(1)} %get-tuple-element.37), channel_id=1, source_target_pairs={{0,16},{8,24},{16,0},{24,8},{1,17},{9,25},{17,1},{25,9},{2,18},{10... | collective-permute-start | bytes 491528 | tf_op jit(solution)/shard_map/ppermute | solution.py:25
  43.7 7.3 %collective-permute-start.13 = (bf16[640,128]{1,0:T(8,128)(2,1)S(1)}, bf16[640,128]{1,0:T(8,128)(2,1)S(1)}, u32[]{:S(2)}, u32[]{:S(2)}) collective-permute-start(bf16[640,128]{1,0:T(8,128)(2,1)S(1)} %get-tuple-element.38), channel_id=1, source_target_pairs={{0,8},{8,16},{16,24},{24,0},{1,9},{9,17},{17,25},{25,1},{2,10},{10... | collective-permute-start | bytes 491528 | tf_op jit(solution)/shard_map/ppermute | solution.py:25
  59.0 7.0 %collective-permute-start.16 = (bf16[2,128,128]{2,1,0:T(8,128)(2,1)S(1)}, bf16[2,128,128]{2,1,0:T(8,128)(2,1)S(1)}, u32[]{:S(2)}, u32[]{:S(2)}) collective-permute-start(bf16[2,128,128]{2,1,0:T(8,128)(2,1)S(1)} %get-tuple-element.57), channel_id=1, source_target_pairs={{0,4},{1,5},{2,6},{3,7},{4,0},{5,1},{6,2},{7,3},{8,12},{9,13},{10,... | collective-permute-start | bytes 196616 | tf_op jit(solution)/shard_map/ppermute | solution.py:30
  59.6 6.5 %collective-permute-start.15 = (bf16[2,128,128]{2,1,0:T(8,128)(2,1)S(1)}, bf16[2,128,128]{2,1,0:T(8,128)(2,1)S(1)}, u32[]{:S(2)}, u32[]{:S(2)}) collective-permute-start(bf16[2,128,128]{2,1,0:T(8,128)(2,1)S(1)} %get-tuple-element.55), channel_id=1, source_target_pairs={{0,2},{1,3},{2,4},{3,5},{4,6},{5,7},{6,0},{7,1},{8,10},{9,11},{10,... | collective-permute-start | bytes 196616 | tf_op jit(solution)/shard_map/ppermute | solution.py:30
  59.9 8.6 %collective-permute-start.18 = (bf16[640,128]{1,0:T(8,128)(2,1)S(1)}, bf16[640,128]{1,0:T(8,128)(2,1)S(1)}, u32[]{:S(2)}, u32[]{:S(2)}) collective-permute-start(bf16[640,128]{1,0:T(8,128)(2,1)S(1)} %bitcast.105), channel_id=1, source_target_pairs={{0,8},{8,16},{16,24},{24,0},{1,9},{9,17},{17,25},{25,1},{2,10},{10... | collective-permute-start | bytes 491528 | tf_op jit(solution)/shard_map/ppermute | solution.py:25
  60.2 10.3 %collective-permute-start.19 = (bf16[640,128]{1,0:T(8,128)(2,1)S(1)}, bf16[640,128]{1,0:T(8,128)(2,1)S(1)}, u32[]{:S(2)}, u32[]{:S(2)}) collective-permute-start(bf16[640,128]{1,0:T(8,128)(2,1)S(1)} %bitcast.104), channel_id=1, source_target_pairs={{0,16},{8,24},{16,0},{24,8},{1,17},{9,25},{17,1},{25,9},{2,18},{10... | collective-permute-start | bytes 491528 | tf_op jit(solution)/shard_map/ppermute | solution.py:25
  61.5 9.1 %collective-permute-start.20 = (bf16[640,128]{1,0:T(8,128)(2,1)S(1)}, bf16[640,128]{1,0:T(8,128)(2,1)S(1)}, u32[]{:S(2)}, u32[]{:S(2)}) collective-permute-start(bf16[640,128]{1,0:T(8,128)(2,1)S(1)} %bitcast.103), channel_id=1, source_target_pairs={{0,24},{8,0},{16,8},{24,16},{1,25},{9,1},{17,9},{25,17},{2,26},{10... | collective-permute-start | bytes 491528 | tf_op jit(solution)/shard_map/ppermute | solution.py:25
  66.2 7.4 %collective-permute-start.26 = (bf16[256,128]{1,0:T(8,128)(2,1)S(1)}, bf16[256,128]{1,0:T(8,128)(2,1)S(1)}, u32[]{:S(2)}, u32[]{:S(2)}) collective-permute-start(bf16[256,128]{1,0:T(8,128)(2,1)S(1)} %fusion.17), channel_id=1, source_target_pairs={{0,6},{1,7},{2,0},{3,1},{4,2},{5,3},{6,4},{7,5},{8,14},{9,15},{10,... | collective-permute-start | bytes 196616 | tf_op jit(solution)/shard_map/ppermute | solution.py:30
  67.9 7.0 %collective-permute-start.25 = (bf16[256,128]{1,0:T(8,128)(2,1)S(1)}, bf16[256,128]{1,0:T(8,128)(2,1)S(1)}, u32[]{:S(2)}, u32[]{:S(2)}) collective-permute-start(bf16[256,128]{1,0:T(8,128)(2,1)S(1)} %fusion.17), channel_id=1, source_target_pairs={{0,4},{1,5},{2,6},{3,7},{4,0},{5,1},{6,2},{7,3},{8,12},{9,13},{10,... | collective-permute-start | bytes 196616 | tf_op jit(solution)/shard_map/ppermute | solution.py:30
  68.5 6.5 %collective-permute-start.24 = (bf16[256,128]{1,0:T(8,128)(2,1)S(1)}, bf16[256,128]{1,0:T(8,128)(2,1)S(1)}, u32[]{:S(2)}, u32[]{:S(2)}) collective-permute-start(bf16[256,128]{1,0:T(8,128)(2,1)S(1)} %fusion.17), channel_id=1, source_target_pairs={{0,2},{1,3},{2,4},{3,5},{4,6},{5,7},{6,0},{7,1},{8,10},{9,11},{10,... | collective-permute-start | bytes 196616 | tf_op jit(solution)/shard_map/ppermute | solution.py:30
  73.5 7.0 %collective-permute-start.23 = (bf16[640,128]{1,0:T(8,128)(2,1)S(1)}, bf16[640,128]{1,0:T(8,128)(2,1)S(1)}, u32[]{:S(2)}, u32[]{:S(2)}) collective-permute-start(bf16[640,128]{1,0:T(8,128)(2,1)S(1)} %get-tuple-element.49), channel_id=1, source_target_pairs={{0,8},{8,16},{16,24},{24,0},{1,9},{9,17},{17,25},{25,1},{2,10},{10... | collective-permute-start | bytes 491528 | tf_op jit(solution)/shard_map/ppermute | solution.py:25
  75.0 12.0 %collective-permute-start.27 = (bf16[8,128,128]{2,1,0:T(8,128)(2,1)S(1)}, bf16[8,128,128]{2,1,0:T(8,128)(2,1)S(1)}, u32[]{:S(2)}, u32[]{:S(2)}) collective-permute-start(bf16[8,128,128]{2,1,0:T(8,128)(2,1)S(1)} %bitcast.92), channel_id=1, source_target_pairs={{0,1},{1,0},{2,3},{3,2},{4,5},{5,4},{6,7},{7,6},{8,9},{9,8},{10,11... | collective-permute-start | bytes 786440 | tf_op jit(solution)/shard_map/ppermute | solution.py:35
  75.1 8.5 %collective-permute-start.28 = (bf16[640,128]{1,0:T(8,128)(2,1)S(1)}, bf16[640,128]{1,0:T(8,128)(2,1)S(1)}, u32[]{:S(2)}, u32[]{:S(2)}) collective-permute-start(bf16[640,128]{1,0:T(8,128)(2,1)S(1)} %get-tuple-element.52), channel_id=1, source_target_pairs={{0,24},{8,0},{16,8},{24,16},{1,25},{9,1},{17,9},{25,17},{2,26},{10... | collective-permute-start | bytes 491528 | tf_op jit(solution)/shard_map/ppermute | solution.py:25
  77.0 10.0 %collective-permute-start.29 = (bf16[640,128]{1,0:T(8,128)(2,1)S(1)}, bf16[640,128]{1,0:T(8,128)(2,1)S(1)}, u32[]{:S(2)}, u32[]{:S(2)}) collective-permute-start(bf16[640,128]{1,0:T(8,128)(2,1)S(1)} %get-tuple-element.53), channel_id=1, source_target_pairs={{0,16},{8,24},{16,0},{24,8},{1,17},{9,25},{17,1},{25,9},{2,18},{10... | collective-permute-start | bytes 491528 | tf_op jit(solution)/shard_map/ppermute | solution.py:25
  78.4 8.6 %collective-permute-start.30 = (bf16[640,128]{1,0:T(8,128)(2,1)S(1)}, bf16[640,128]{1,0:T(8,128)(2,1)S(1)}, u32[]{:S(2)}, u32[]{:S(2)}) collective-permute-start(bf16[640,128]{1,0:T(8,128)(2,1)S(1)} %get-tuple-element.54), channel_id=1, source_target_pairs={{0,8},{8,16},{16,24},{24,0},{1,9},{9,17},{17,25},{25,1},{2,10},{10... | collective-permute-start | bytes 491528 | tf_op jit(solution)/shard_map/ppermute | solution.py:25
  (24 other events, 200.7 us)

commit v2 on v1

--- a/solution.py
+++ b/solution.py
@@ -17,7 +17,9 @@
 VMEM = pl.BlockSpec(memory_space=pltpu.VMEM)
 SMEM = pl.BlockSpec(memory_space=pltpu.SMEM)
 LIMIT = 48 * 1024 * 1024
+FULL = 62 * 1024 * 1024
 CORES = 2
+STEP_COST = 20_000_000_000
 
 
 def rotate(value, axis, by):
@@ -33,6 +35,10 @@
 def swap_core(value):
     size = lax.axis_size("zone")
     return lax.ppermute(value, "zone", [(i, i ^ 1) for i in range(size)])
+
+
+def after(values, others):
+    return lax.optimization_barrier((*values, *others))[: len(values)]
 
 
 def call(kernel, outs, scratch, flops, moved, *args, smem=0):
@@ -52,20 +58,17 @@
     return pl.ds(pl.multiple_of(part * size, size), size)
 
 
-def pack_kernel(parts, size, tile, duals, stock, cost, *packets):
+def give_packet(part, size, tile, duals, stock, cost, packet):
     pieces = size // tile
-    for r in range(parts):
-        part = lax.rem(lax.axis_index("section") + r, parts)
-        rows = pl.ds(pl.multiple_of(part * size, size), size)
-        packets[r][0:size] = duals[rows, :].astype(BF)
-        packets[r][size : 2 * size] = stock[rows, :].astype(BF)
-        tail = packets[r].shape[0] - 2 * size
-        lines = [
-            cost[:, pl.ds(pl.multiple_of(part * size + i * tile, tile), tile)]
-            for i in range(pieces)
-        ]
-        lines.append(jnp.zeros((tail - pieces, tile), F32))
-        packets[r][2 * size : 2 * size + tail] = jnp.concatenate(lines, axis=0).astype(BF)
+    rows = pl.ds(pl.multiple_of(part * size, size), size)
+    packet[0:size] = duals[rows, :].astype(BF)
+    packet[size : 2 * size] = stock[rows, :].astype(BF)
+    tail = packet.shape[0] - 2 * size
+    lines = [
+        cost[:, pl.ds(pl.multiple_of(part * size + i * tile, tile), tile)] for i in range(pieces)
+    ]
+    lines.append(jnp.zeros((tail - pieces, tile), F32))
+    packet[2 * size : 2 * size + tail] = jnp.concatenate(lines, axis=0).astype(BF)
 
 
 def block_slot(place, col, live, k, shape, sign):
@@ -116,10 +119,32 @@
     send[...] = acc[n : 2 * n].astype(BF)
 
 
-def pull_kernel(shape, row, col, live, place, tiles, duals, keep, send, half, acc):
-    half[...] = duals[...].astype(BF)
+def pull_kernel(shape, parts, size, *refs):
+    count = 8
+    ins, outs = refs[:count], refs[count : count + 2 + parts]
+    rest = refs[count + 2 + parts :]
+    held, packets, (half, acc, in_sems, out_sems) = rest[:count], rest[count:-4], rest[-4:]
+    copies = [pltpu.make_async_copy(ins[i], held[i], in_sems.at[i]) for i in range(count)]
+    for i in (5, 6, 7, 0, 1, 2, 3, 4):
+        copies[i].start()
+    row, col, live, place, tiles, duals, stock, cost = held
+    keep, send = outs[:2]
+    tile = tiles.shape[1]
+    for i in (5, 6, 7):
+        copies[i].wait()
+    gives = []
+    for r in range(parts):
+        part = lax.rem(lax.axis_index("section") + r, parts)
+        give_packet(part, size, tile, duals, stock, cost, packets[r])
+        gives.append(pltpu.make_async_copy(packets[r], outs[2 + r], out_sems.at[r]))
+        gives[r].start()
+    half[...] = duals[...].astype(BF).reshape(half.shape)
+    for i in range(5):
+        copies[i].wait()
     pull_slots(shape, row, col, live, place, tiles, half, acc)
     give_partials(acc, keep, send)
+    for give in gives:
+        give.wait()
 
 
 def step_duals(shape, parts, size, refs, blocks, acc):
@@ -158,11 +183,31 @@
     give_partials(acc_blocks, keep, send)
 
 
-def push_kernel(shape, parts, size, *refs):
-    ins = refs[: 9 + parts]
-    next_duals, blocks, acc = refs[9 + parts :]
-    step_duals(shape, parts, size, ins, blocks, acc)
-    next_duals[...] = acc[0 : next_duals.shape[0]]
+def push_kernel(shape, *refs):
+    row, col, live, place, tiles, duals, demand, near, far, base, blocks, acc = refs
+    n = near.shape[0]
+    blocks[0:n] = near[...]
+    blocks[n : 2 * n] = far[...]
+    n = base.shape[0]
+    acc[0:n] = duals[...] + (STEP_DUAL * 0.25) * demand[...].astype(F32)
+    push_slots(shape, row, col, live, place, tiles, blocks, acc)
+    base[...] = acc[0:n]
+
+
+def final_kernel(parts, size, *refs):
+    base, moved, (duals_out, stock_out) = refs[0], refs[1 : 1 + parts], refs[1 + parts : 3 + parts]
+    duals, stock, sems = refs[3 + parts :]
+    copies = []
+    for r in range(parts):
+        part = lax.rem(lax.axis_index("section") + r, parts)
+        rows = pl.ds(pl.multiple_of(part * size, size), size)
+        duals[rows, :] = base[rows, :] - STEP_DUAL * moved[r][0:size].astype(F32)
+        stock[rows, :] = moved[r][size:].astype(F32)
+        for i, (held, out) in enumerate(((duals, duals_out), (stock, stock_out))):
+            copies.append(pltpu.make_async_copy(held.at[rows], out.at[rows], sems.at[2 * r + i]))
+            copies[-1].start()
+    for copy in copies:
+        copy.wait()
 
 
 def spread_cost(line, eye, ones):
@@ -202,7 +247,7 @@
 
 def last_stock_kernel(parts, size, tile, *refs):
     packets, stocks, duals = refs[:parts], refs[parts], refs[parts + 1 : 2 * parts + 1]
-    combined, moved = refs[2 * parts + 1 : 3 * parts + 1], refs[3 * parts + 1 :]
+    outs = refs[2 * parts + 1 :]
     eye, ones = eye_of(tile), jnp.ones((tile, tile), BF)
     costs = [packets[r][2 * size :].astype(F32).astype(BF) for r in range(parts)]
     for i in range(size // tile):
@@ -212,14 +257,8 @@
         new = stock_step(parts, tile, i, costs, dual, stock, eye, ones)
         bar = [2.0 * new[r] - stock[r] for r in range(parts)]
         for r in range(parts):
-            moved[r][rows] = new[r].astype(BF)
-            combined[r][rows] = (bar[(r + 1) % parts] - bar[r]).astype(BF)
-
-
-def place_kernel(parts, size, *refs):
-    out = refs[parts]
-    for r in range(parts):
-        out[quarter_rows(r, parts, size), :] = refs[r][...].astype(F32)
+            outs[r][rows] = (bar[(r + 1) % parts] - bar[r]).astype(BF)
+            outs[r][size + i * tile : size + (i + 1) * tile] = new[r].astype(BF)
 
 
 def per_device(
@@ -268,60 +307,57 @@
         pltpu.VMEM((band_tiles + 1, tile, scenarios), F32),
     ]
 
-    def collect(keep, send):
+    def collect(keep, send, others):
         both = (keep.astype(F32) + swap_core(send).astype(F32)).astype(BF)
         parts_of = [both[k * owned : (k + 1) * owned] for k in range(chips)]
         got = [rotate_chip(parts_of[k], k) for k in range(1, chips)]
+        got = after(got, others)
         total = parts_of[0].astype(F32)
         for value in got:
             total = total + value.astype(F32)
         return total.reshape(owned * tile, scenarios)
 
-    def spread(value):
-        own = [value] + [rotate_chip(value, k) for k in range(1, chips)]
-        near = jnp.concatenate(own, axis=0).reshape(blocks // 2, tile, scenarios)
+    def spread(value, others):
+        own = [rotate_chip(value, k) for k in range(1, chips)]
+        own = after(own, others)
+        near = jnp.concatenate([value, *own], axis=0).reshape(blocks // 2, tile, scenarios)
         return near, swap_core(near)
 
     def step_flows(now, pulled):
         new = jnp.maximum(now - STEP_PRIMAL * (flow_cost[0][:, None] - pulled), 0.0)
         return new, ((2.0 * new - now).astype(BF) * BF(-STEP_DUAL))
 
-    packets = call(
-        functools.partial(pack_kernel, parts, size, tile),
-        [jax.ShapeDtypeStruct((2 * size + tail, scenarios), BF)] * parts,
-        [],
-        0,
-        12 * rows * scenarios,
-        duals2,
-        stock2,
-        stock_cost,
-    )
+    ins = (tile_row, tile_col, tile_live, block_place, tiles, duals2, stock2, stock_cost)
+    keep, send, *packets = pl.pallas_call(
+        functools.partial(pull_kernel, shape, parts, size),
+        out_shape=[half_blocks, half_blocks]
+        + [jax.ShapeDtypeStruct((2 * size + tail, scenarios), BF)] * parts,
+        in_specs=[pl.BlockSpec(memory_space=pltpu.HBM)] * len(ins),
+        out_specs=[VMEM] * 2 + [pl.BlockSpec(memory_space=pltpu.HBM)] * parts,
+        scratch_shapes=[pltpu.SMEM(v.shape, v.dtype) for v in ins[:4]]
+        + [pltpu.VMEM(v.shape, v.dtype) for v in ins[4:]]
+        + [pltpu.VMEM((2 * size + tail, scenarios), BF)] * parts
+        + pull_scratch
+        + [pltpu.SemaphoreType.DMA((len(ins),)), pltpu.SemaphoreType.DMA((parts,))],
+        compiler_params=pltpu.CompilerParams(vmem_limit_bytes=FULL),
+        cost_estimate=pl.CostEstimate(
+            flops=flops, bytes_accessed=12 * rows * scenarios, transcendentals=0
+        ),
+    )(*ins)
     packets = [packets[0]] + [rotate(packets[r], "section", r) for r in range(1, parts)]
-
-    keep, send = call(
-        functools.partial(pull_kernel, shape),
-        [half_blocks, half_blocks],
-        pull_scratch,
-        flops,
-        4 * rows * scenarios + 2 * slots * tile * tile,
-        *where,
-        tiles,
-        duals3,
-        smem=4,
-    )
-    pulled = collect(keep, send)
-    flows1, bar1 = step_flows(flows2, pulled)
-    near, far = spread(bar1)
 
     stocks, *combined = call(
         functools.partial(first_stock_kernel, parts, size, tile),
         [jax.ShapeDtypeStruct((parts, size, scenarios), F32)] + [quarter] * parts,
         [],
-        0,
+        STEP_COST,
         10 * rows * scenarios,
         *packets,
     )
+    pulled = collect(keep, send, combined)
+    flows1, bar1 = step_flows(flows2, pulled)
     combined = [combined[0]] + [rotate(combined[r], "section", -r) for r in range(1, parts)]
+    near, far = spread(bar1, combined)
     combined = [c.reshape(size // tile, tile, scenarios) for c in combined]
 
     duals1, keep, send, *halves = call(
@@ -342,48 +378,47 @@
     )
     halves = [h.reshape(size, scenarios) for h in halves]
     halves = [halves[0]] + [rotate(halves[r], "section", r) for r in range(1, parts)]
-    pulled = collect(keep, send)
-    flows2_out, bar2 = step_flows(flows1, pulled)
-    near, far = spread(bar2)
-
     outs = call(
         functools.partial(last_stock_kernel, parts, size, tile),
-        [quarter] * (2 * parts),
+        [jax.ShapeDtypeStruct((2 * size, scenarios), BF)] * parts,
         [],
-        0,
+        STEP_COST,
         10 * rows * scenarios,
         *packets,
         stocks,
         *halves,
     )
-    combined, moved = outs[:parts], outs[parts:]
-    combined = [combined[0]] + [rotate(combined[r], "section", -r) for r in range(1, parts)]
-    combined = [c.reshape(size // tile, tile, scenarios) for c in combined]
-    moved = [moved[0]] + [rotate(moved[r], "section", -r) for r in range(1, parts)]
-
-    duals_out = call(
-        functools.partial(push_kernel, shape, parts, size),
+    pulled = collect(keep, send, outs)
+    flows2_out, bar2 = step_flows(flows1, pulled)
+    outs = [outs[0]] + [rotate(outs[r], "section", -r) for r in range(1, parts)]
+    near, far = spread(bar2, outs)
+    base = call(
+        functools.partial(push_kernel, shape),
         jax.ShapeDtypeStruct((band_tiles, tile, scenarios), F32),
         push_scratch,
         flops,
-        14 * rows * scenarios + 2 * slots * tile * tile,
+        12 * rows * scenarios + 2 * slots * tile * tile,
         *where,
         tiles,
         duals1,
         demand3,
         near,
         far,
-        *combined,
         smem=4,
     )
-    stock_out = call(
-        functools.partial(place_kernel, parts, size),
-        jax.ShapeDtypeStruct((rows, scenarios), F32),
-        [],
-        0,
-        6 * rows * scenarios,
-        *moved,
-    )
+    whole = jax.ShapeDtypeStruct((rows, scenarios), F32)
+    duals_out, stock_out = pl.pallas_call(
+        functools.partial(final_kernel, parts, size),
+        out_shape=[whole, whole],
+        in_specs=[VMEM] * (parts + 1),
+        out_specs=[pl.BlockSpec(memory_space=pltpu.HBM)] * 2,
+        scratch_shapes=[pltpu.VMEM((rows, scenarios), F32)] * 2
+        + [pltpu.SemaphoreType.DMA((2 * parts,))],
+        compiler_params=pltpu.CompilerParams(vmem_limit_bytes=LIMIT),
+        cost_estimate=pl.CostEstimate(
+            flops=0, bytes_accessed=12 * rows * scenarios, transcendentals=0
+        ),
+    )(base.reshape(rows, scenarios), *outs)
     return (
         flows2_out.reshape(flows.shape),
         stock_out.reshape(stock.shape),

time: 90.4 us -> 80.9 us (0.89)
  waiting for transfers between devices: 32.9 us -> 21 us
  starting transfers between devices: 38.3 us -> 42.7 us
  local copies, waits for them, and re-layouts: 5.25 us -> 1.05 us
  Pallas kernels: 11.5 us -> 12.9 us
  other arithmetic: 1.25 us -> 2.21 us
    ppermute x12, starting transfers between devices: 17.3 us -> 26.7 us  [rotate_chip(): lax.ppermute(value, 'zone', [(i, (i + by * CORES) % size) for i in range(...]
    ppermute x15 -> x12, waiting for transfers between devices: 17.8 us -> 8.85 us  [rotate(): lax.ppermute(value, axis, [(i, (i + by) % size) for i in range(size)])]
    pallas_call x0 -> x2, Pallas kernels: none -> 5.79 us  [the longest x1 4.2 us: per_device(): pl.pallas_call(functools.partial(pull_kernel, shape, parts, size), out_sh...]
    ppermute x15 -> x12, starting transfers between devices: 20.2 us -> 15.1 us  [rotate(): lax.ppermute(value, axis, [(i, (i + by) % size) for i in range(size)])]
    pallas_call x7 -> x4, Pallas kernels: 11.5 us -> 7.14 us  [call(): pl.pallas_call(kernel, out_shape=outs, in_specs=[SMEM] * smem + [VMEM] *...]
    unnamed x34 -> x20, local copies, waits for them, and re-layouts: 5.22 us -> 1.02 us
    ppermute x12, waiting for transfers between devices: 12.4 us -> 9.83 us  [rotate_chip(): lax.ppermute(value, 'zone', [(i, (i + by * CORES) % size) for i in range(...]
    convert_element_type x2, other arithmetic: 0.15 us -> 1.1 us  [collect(): both = (keep.astype(F32) + swap_core(send).astype(F32)).astype(BF)]
  transfers between devices with their start and end apart: 31 -> 28, of which waited for: 19 -> 13; matrix products, arithmetic and copies ran while one was open for 1% -> 3% of each run, Pallas kernels for 3% -> 2%
where the time goes in v2:
time: 80.9 us; the launch traced here: 80.7 us
  starting transfers between devices  42.7 us (53%)
  waiting for transfers between devices  21 us (26%)
  Pallas kernels  12.9 us (16%)
  other arithmetic  2.21 us (3%)
  local copies, waits for them, and re-layouts  1.05 us (1%)
  between operations  0.87 us (1%)
    ppermute x12, starting transfers between devices, rotate_chip(): lax.ppermute(value, 'zone', [(i, (i + by * CORES) % size) for i in range(...  26.7 us
    ppermute x12, starting transfers between devices, rotate(): lax.ppermute(value, axis, [(i, (i + by) % size) for i in range(size)])  15.1 us
    ppermute x12, waiting for transfers between devices, rotate_chip(): lax.ppermute(value, 'zone', [(i, (i + by * CORES) % size) for i in range(...  9.83 us
    ppermute x12, waiting for transfers between devices, rotate(): lax.ppermute(value, axis, [(i, (i + by) % size) for i in range(size)])  8.85 us
    pallas_call x4, Pallas kernels, call(): pl.pallas_call(kernel, out_shape=outs, in_specs=[SMEM] * smem + [VMEM] *...  7.14 us
    pallas_call x1, Pallas kernels, per_device(): pl.pallas_call(functools.partial(pull_kernel, shape, parts, size), out_sh...  4.2 us
    ppermute x4, waiting for transfers between devices, swap_core(): return lax.ppermute(value, 'zone', [(i, i ^ 1) for i in range(size)])  2.28 us
  transfers between devices with their start and end apart: 28, of which 13 were waited for; matrix products, arithmetic and copies ran while one was open for 3% of the time, Pallas kernels for 2%

profile of v2, /device:TPU:0, one launch (start us, length us, event | category | flops | bytes accessed | tf_op | source)
XLA Modules:
  0.0 80.7 jit_solution(17783775296494392043)
XLA Ops:
  0.6 4.2 %shard_map.133 = (bf16[8,128,128]{2,1,0:T(8,128)(2,1)}, bf16[8,128,128]{2,1,0:T(8,128)(2,1)}, bf16[1296,128]{1,0:T(8,128)(2,1)}, bf16[1296,128]{1,0:T(8,128)(2,1...) custom-call(s32[1,32]{1,0:T(1,128)} %refs_0_.5, s32[1,32]{1,0:T(1,128)} %refs_1_.5, s32[1,32]{1,0:T(1,128)} %refs_2_.5, ...), custom_call_target="tpu_custom_call" | custom-call | flops 134217728 | bytes 3932160 | tf_op jit(solution)/shard_map/pallas_call | solution.py:331
  5.3 2.5 %collective-permute-start.4 = (bf16[1296,128]{1,0:T(8,128)(2,1)}, bf16[1296,128]{1,0:T(8,128)(2,1)S(1)}, u32[]{:S(2)}, u32[]{:S(2)}) collective-permute-start(bf16[1296,128]{1,0:T(8,128)(2,1)} %get-tuple-element.42), channel_id=1, source_target_pairs={{0,8},{8,16},{16,24},{24,0},{1,9},{9,17},{17,25},{25,1},{2,10},{10... | collective-permute-start | bytes 995336 | tf_op jit(solution)/shard_map/ppermute | solution.py:27
  11.9 1.6 %collective-permute-start.1 = (bf16[2,128,128]{2,1,0:T(8,128)(2,1)S(1)}, bf16[2,128,128]{2,1,0:T(8,128)(2,1)S(1)}, u32[]{:S(2)}, u32[]{:S(2)}) collective-permute-start(bf16[2,128,128]{2,1,0:T(8,128)(2,1)S(1)} %get-tuple-element.80), channel_id=1, source_target_pairs={{0,2},{1,3},{2,4},{3,5},{4,6},{5,7},{6,0},{7,1},{8,10},{9,11},{10,... | collective-permute-start | bytes 196616 | tf_op jit(solution)/shard_map/ppermute | solution.py:32
  13.5 2.6 %collective-permute-start.2 = (bf16[2,128,128]{2,1,0:T(8,128)(2,1)S(1)}, bf16[2,128,128]{2,1,0:T(8,128)(2,1)S(1)}, u32[]{:S(2)}, u32[]{:S(2)}) collective-permute-start(bf16[2,128,128]{2,1,0:T(8,128)(2,1)S(1)} %get-tuple-element.79), channel_id=1, source_target_pairs={{0,4},{1,5},{2,6},{3,7},{4,0},{5,1},{6,2},{7,3},{8,12},{9,13},{10,... | collective-permute-start | bytes 196616 | tf_op jit(solution)/shard_map/ppermute | solution.py:32
  16.1 1.6 %collective-permute-done.4.refs_1_ = bf16[1296,128]{1,0:T(8,128)(2,1)S(1)} collective-permute-done((bf16[1296,128]{1,0:T(8,128)(2,1)}, bf16[1296,128]{1,0:T(8,128)(2,1)S(1)}, u32[]{:S(2)}, u32[]{:S(2)}) %collective-permute-start.4) | collective-permute-done | bytes 331808 | tf_op jit(solution)/shard_map/ppermute | solution.py:27
  17.8 4.0 %collective-permute-start.3 = (bf16[2,128,128]{2,1,0:T(8,128)(2,1)S(1)}, bf16[2,128,128]{2,1,0:T(8,128)(2,1)S(1)}, u32[]{:S(2)}, u32[]{:S(2)}) collective-permute-start(bf16[2,128,128]{2,1,0:T(8,128)(2,1)S(1)} %get-tuple-element.78), channel_id=1, source_target_pairs={{0,6},{1,7},{2,0},{3,1},{4,2},{5,3},{6,4},{7,5},{8,14},{9,15},{10,... | collective-permute-start | bytes 196616 | tf_op jit(solution)/shard_map/ppermute | solution.py:32
  21.8 2.8 %collective-permute-done.5.refs_2_ = bf16[1296,128]{1,0:T(8,128)(2,1)S(1)} collective-permute-done((bf16[1296,128]{1,0:T(8,128)(2,1)}, bf16[1296,128]{1,0:T(8,128)(2,1)S(1)}, u32[]{:S(2)}, u32[]{:S(2)}) %collective-permute-start.5) | collective-permute-done | bytes 331808 | tf_op jit(solution)/shard_map/ppermute | solution.py:27
  28.1 1.7 %collective-permute-start.11 = (bf16[640,128]{1,0:T(8,128)(2,1)S(1)}, bf16[640,128]{1,0:T(8,128)(2,1)S(1)}, u32[]{:S(2)}, u32[]{:S(2)}) collective-permute-start(bf16[640,128]{1,0:T(8,128)(2,1)S(1)} %get-tuple-element.47), channel_id=1, source_target_pairs={{0,16},{8,24},{16,0},{24,8},{1,17},{9,25},{17,1},{25,9},{2,18},{10... | collective-permute-start | bytes 491528 | tf_op jit(solution)/shard_map/ppermute | solution.py:27
  30.3 1.6 %collective-permute-start.7 = (bf16[256,128]{1,0:T(8,128)(2,1)S(1)}, bf16[256,128]{1,0:T(8,128)(2,1)S(1)}, u32[]{:S(2)}, u32[]{:S(2)}) collective-permute-start(bf16[256,128]{1,0:T(8,128)(2,1)S(1)} %fusion.16), channel_id=1, source_target_pairs={{0,2},{1,3},{2,4},{3,5},{4,6},{5,7},{6,0},{7,1},{8,10},{9,11},{10,... | collective-permute-start | bytes 196616 | tf_op jit(solution)/shard_map/ppermute | solution.py:32
  31.9 2.6 %collective-permute-start.8 = (bf16[256,128]{1,0:T(8,128)(2,1)S(1)}, bf16[256,128]{1,0:T(8,128)(2,1)S(1)}, u32[]{:S(2)}, u32[]{:S(2)}) collective-permute-start(bf16[256,128]{1,0:T(8,128)(2,1)S(1)} %fusion.16), channel_id=1, source_target_pairs={{0,4},{1,5},{2,6},{3,7},{4,0},{5,1},{6,2},{7,3},{8,12},{9,13},{10,... | collective-permute-start | bytes 196616 | tf_op jit(solution)/shard_map/ppermute | solution.py:32
  34.5 2.3 %collective-permute-done.7 = bf16[256,128]{1,0:T(8,128)(2,1)S(1)} collective-permute-done((bf16[256,128]{1,0:T(8,128)(2,1)S(1)}, bf16[256,128]{1,0:T(8,128)(2,1)S(1)}, u32[]{:S(2)}, u32[]{:S(2)}) %collective-permute-start.7) | collective-permute-done | bytes 65568 | tf_op jit(solution)/shard_map/ppermute | solution.py:32
  38.9 2.2 %collective-permute-done.9 = bf16[256,128]{1,0:T(8,128)(2,1)S(1)} collective-permute-done((bf16[256,128]{1,0:T(8,128)(2,1)S(1)}, bf16[256,128]{1,0:T(8,128)(2,1)S(1)}, u32[]{:S(2)}, u32[]{:S(2)}) %collective-permute-start.9) | collective-permute-done | bytes 65568 | tf_op jit(solution)/shard_map/ppermute | solution.py:32
  42.8 4.0 %shard_map.135 = (f32[20,128,128]{2,1,0:T(8,128)S(1)}, bf16[8,128,128]{2,1,0:T(8,128)(2,1)S(1)}, bf16[8,128,128]{2,1,0:T(8,128)(2,1)S(1)}, bf16[5,128,128]{2,1,0...) custom-call(s32[1,32]{1,0:T(1,128)S(1)} %copy-done.3, ...), custom_call_target="tpu_custom_call" | custom-call | flops 268435456 | bytes 6291456 | tf_op jit(solution)/shard_map/pallas_call | solution.py:45
  48.1 1.7 %collective-permute-start.19 = (bf16[640,128]{1,0:T(8,128)(2,1)S(1)}, bf16[640,128]{1,0:T(8,128)(2,1)S(1)}, u32[]{:S(2)}, u32[]{:S(2)}) collective-permute-start(bf16[640,128]{1,0:T(8,128)(2,1)S(1)} %bitcast.96), channel_id=1, source_target_pairs={{0,16},{8,24},{16,0},{24,8},{1,17},{9,25},{17,1},{25,9},{2,18},{10... | collective-permute-start | bytes 491528 | tf_op jit(solution)/shard_map/ppermute | solution.py:27
  50.6 3.8 %collective-permute-start.16 = (bf16[2,128,128]{2,1,0:T(8,128)(2,1)S(1)}, bf16[2,128,128]{2,1,0:T(8,128)(2,1)S(1)}, u32[]{:S(2)}, u32[]{:S(2)}) collective-permute-start(bf16[2,128,128]{2,1,0:T(8,128)(2,1)S(1)} %get-tuple-element.76), channel_id=1, source_target_pairs={{0,4},{1,5},{2,6},{3,7},{4,0},{5,1},{6,2},{7,3},{8,12},{9,13},{10,... | collective-permute-start | bytes 196616 | tf_op jit(solution)/shard_map/ppermute | solution.py:32
  55.0 3.1 %collective-permute-start.17 = (bf16[2,128,128]{2,1,0:T(8,128)(2,1)S(1)}, bf16[2,128,128]{2,1,0:T(8,128)(2,1)S(1)}, u32[]{:S(2)}, u32[]{:S(2)}) collective-permute-start(bf16[2,128,128]{2,1,0:T(8,128)(2,1)S(1)} %get-tuple-element.75), channel_id=1, source_target_pairs={{0,6},{1,7},{2,0},{3,1},{4,2},{5,3},{6,4},{7,5},{8,14},{9,15},{10,... | collective-permute-start | bytes 196616 | tf_op jit(solution)/shard_map/ppermute | solution.py:32
  58.8 1.8 %collective-permute-start.24 = (bf16[1280,128]{1,0:T(8,128)(2,1)S(1)}, bf16[1280,128]{1,0:T(8,128)(2,1)S(1)}, u32[]{:S(2)}, u32[]{:S(2)}) collective-permute-start(bf16[1280,128]{1,0:T(8,128)(2,1)S(1)} %get-tuple-element.63), channel_id=1, source_target_pairs={{0,24},{8,0},{16,8},{24,16},{1,25},{9,1},{17,9},{25,17},{2,26},{10... | collective-permute-start | bytes 983048 | tf_op jit(solution)/shard_map/ppermute | solution.py:27
  62.0 3.7 %collective-permute-start.22 = (bf16[256,128]{1,0:T(8,128)(2,1)S(1)}, bf16[256,128]{1,0:T(8,128)(2,1)S(1)}, u32[]{:S(2)}, u32[]{:S(2)}) collective-permute-start(bf16[256,128]{1,0:T(8,128)(2,1)S(1)} %fusion.17), channel_id=1, source_target_pairs={{0,4},{1,5},{2,6},{3,7},{4,0},{5,1},{6,2},{7,3},{8,12},{9,13},{10,... | collective-permute-start | bytes 196616 | tf_op jit(solution)/shard_map/ppermute | solution.py:32
  65.8 2.1 %collective-permute-done.21 = bf16[256,128]{1,0:T(8,128)(2,1)S(1)} collective-permute-done((bf16[256,128]{1,0:T(8,128)(2,1)S(1)}, bf16[256,128]{1,0:T(8,128)(2,1)S(1)}, u32[]{:S(2)}, u32[]{:S(2)}) %collective-permute-start.21) | collective-permute-done | bytes 65568 | tf_op jit(solution)/shard_map/ppermute | solution.py:32
  67.8 1.8 %collective-permute-start.23 = (bf16[256,128]{1,0:T(8,128)(2,1)S(1)}, bf16[256,128]{1,0:T(8,128)(2,1)S(1)}, u32[]{:S(2)}, u32[]{:S(2)}) collective-permute-start(bf16[256,128]{1,0:T(8,128)(2,1)S(1)} %fusion.17), channel_id=1, source_target_pairs={{0,6},{1,7},{2,0},{3,1},{4,2},{5,3},{6,4},{7,5},{8,14},{9,15},{10,... | collective-permute-start | bytes 196616 | tf_op jit(solution)/shard_map/ppermute | solution.py:32
  70.0 2.1 %collective-permute-done.23 = bf16[256,128]{1,0:T(8,128)(2,1)S(1)} collective-permute-done((bf16[256,128]{1,0:T(8,128)(2,1)S(1)}, bf16[256,128]{1,0:T(8,128)(2,1)S(1)}, u32[]{:S(2)}, u32[]{:S(2)}) %collective-permute-start.23) | collective-permute-done | bytes 65568 | tf_op jit(solution)/shard_map/ppermute | solution.py:32
  72.1 3.5 %collective-permute-done.25.refs_3_ = bf16[1280,128]{1,0:T(8,128)(2,1)S(1)} collective-permute-done((bf16[1280,128]{1,0:T(8,128)(2,1)S(1)}, bf16[1280,128]{1,0:T(8,128)(2,1)S(1)}, u32[]{:S(2)}, u32[]{:S(2)}) %collective-permute-start.25) | collective-permute-done | bytes 327712 | tf_op jit(solution)/shard_map/ppermute | solution.py:27
  77.3 1.8 %shard_map.137 = f32[20,128,128]{2,1,0:T(8,128)S(1)} custom-call(s32[1,32]{1,0:T(1,128)S(1)} %copy-done.3, s32[1,32]{1,0:T(1,128)S(1)} %copy-done.4, s32[1,32]{1,0:T(1,128)S(1)} %copy-done.5, s32[16]{0:T(128)S(1)} %copy-done.6, bf16[32,128,128]{2,1,0:T(8,128)(2,1)S(1)} %bitcast.80, f32[20,128,128]{2,1,0:T(8,128)S(1)} %get-tuple-element.69.refs_5_, ...), custom_call_target="tpu_custom_call" | custom-call | flops 134217728 | bytes 4980736 | tf_op jit(solution)/shard_map/pallas_call | solution.py:45
  79.1 1.6 %shard_map.138 = (f32[2560,128]{1,0:T(8,128)}, f32[2560,128]{1,0:T(8,128)}) custom-call(f32[2560,128]{1,0:T(8,128)S(1)} %bitcast.81, bf16[1280,128]{1,0:T(8,128)(2,1)S(1)} %get-tuple-element.62.refs_1_, bf16[1280,128]{1,0:T(8,128)(2,1)S(1)} %collective-permute-done.24.refs_2_, bf16[1280,128]{1,0:T(8,128)(2,1)S(1)} %collective-permute-done.25.refs_3_, ...), custom_call_target="tpu_custom_call" | custom-call | bytes 3932160 | tf_op jit(solution)/shard_map/pallas_call | solution.py:410
  (69 shorter events, 18.8 us)
Async XLA Ops:
  4.8 6.0 %collective-permute-start = (bf16[8,128,128]{2,1,0:T(8,128)(2,1)}, bf16[8,128,128]{2,1,0:T(8,128)(2,1)S(1)}, u32[]{:S(2)}, u32[]{:S(2)}) collective-permute-start(bf16[8,128,128]{2,1,0:T(8,128)(2,1)} %get-tuple-element.40), channel_id=1, source_target_pairs={{0,1},{1,0},{2,3},{3,2},{4,5},{5,4},{6,7},{7,6},{8,9},{9,8},{10,11... | collective-permute-start | bytes 786440 | tf_op jit(solution)/shard_map/ppermute | solution.py:37
  5.3 12.4 %collective-permute-start.4 = (bf16[1296,128]{1,0:T(8,128)(2,1)}, bf16[1296,128]{1,0:T(8,128)(2,1)S(1)}, u32[]{:S(2)}, u32[]{:S(2)}) collective-permute-start(bf16[1296,128]{1,0:T(8,128)(2,1)} %get-tuple-element.42), channel_id=1, source_target_pairs={{0,8},{8,16},{16,24},{24,0},{1,9},{9,17},{17,25},{25,1},{2,10},{10... | collective-permute-start | bytes 995336 | tf_op jit(solution)/shard_map/ppermute | solution.py:27
  7.9 16.7 %collective-permute-start.5 = (bf16[1296,128]{1,0:T(8,128)(2,1)}, bf16[1296,128]{1,0:T(8,128)(2,1)S(1)}, u32[]{:S(2)}, u32[]{:S(2)}) collective-permute-start(bf16[1296,128]{1,0:T(8,128)(2,1)} %get-tuple-element.43), channel_id=1, source_target_pairs={{0,16},{8,24},{16,0},{24,8},{1,17},{9,25},{17,1},{25,9},{2,18},{10... | collective-permute-start | bytes 995336 | tf_op jit(solution)/shard_map/ppermute | solution.py:27
  9.4 15.5 %collective-permute-start.6 = (bf16[1296,128]{1,0:T(8,128)(2,1)}, bf16[1296,128]{1,0:T(8,128)(2,1)S(1)}, u32[]{:S(2)}, u32[]{:S(2)}) collective-permute-start(bf16[1296,128]{1,0:T(8,128)(2,1)} %get-tuple-element.44), channel_id=1, source_target_pairs={{0,24},{8,0},{16,8},{24,16},{1,25},{9,1},{17,9},{25,17},{2,26},{10... | collective-permute-start | bytes 995336 | tf_op jit(solution)/shard_map/ppermute | solution.py:27
  11.9 17.9 %collective-permute-start.1 = (bf16[2,128,128]{2,1,0:T(8,128)(2,1)S(1)}, bf16[2,128,128]{2,1,0:T(8,128)(2,1)S(1)}, u32[]{:S(2)}, u32[]{:S(2)}) collective-permute-start(bf16[2,128,128]{2,1,0:T(8,128)(2,1)S(1)} %get-tuple-element.80), channel_id=1, source_target_pairs={{0,2},{1,3},{2,4},{3,5},{4,6},{5,7},{6,0},{7,1},{8,10},{9,11},{10,... | collective-permute-start | bytes 196616 | tf_op jit(solution)/shard_map/ppermute | solution.py:32
  13.5 16.6 %collective-permute-start.2 = (bf16[2,128,128]{2,1,0:T(8,128)(2,1)S(1)}, bf16[2,128,128]{2,1,0:T(8,128)(2,1)S(1)}, u32[]{:S(2)}, u32[]{:S(2)}) collective-permute-start(bf16[2,128,128]{2,1,0:T(8,128)(2,1)S(1)} %get-tuple-element.79), channel_id=1, source_target_pairs={{0,4},{1,5},{2,6},{3,7},{4,0},{5,1},{6,2},{7,3},{8,12},{9,13},{10,... | collective-permute-start | bytes 196616 | tf_op jit(solution)/shard_map/ppermute | solution.py:32
  17.8 12.3 %collective-permute-start.3 = (bf16[2,128,128]{2,1,0:T(8,128)(2,1)S(1)}, bf16[2,128,128]{2,1,0:T(8,128)(2,1)S(1)}, u32[]{:S(2)}, u32[]{:S(2)}) collective-permute-start(bf16[2,128,128]{2,1,0:T(8,128)(2,1)S(1)} %get-tuple-element.78), channel_id=1, source_target_pairs={{0,6},{1,7},{2,0},{3,1},{4,2},{5,3},{6,4},{7,5},{8,14},{9,15},{10,... | collective-permute-start | bytes 196616 | tf_op jit(solution)/shard_map/ppermute | solution.py:32
  26.6 14.5 %collective-permute-start.10 = (bf16[640,128]{1,0:T(8,128)(2,1)S(1)}, bf16[640,128]{1,0:T(8,128)(2,1)S(1)}, u32[]{:S(2)}, u32[]{:S(2)}) collective-permute-start(bf16[640,128]{1,0:T(8,128)(2,1)S(1)} %get-tuple-element.46), channel_id=1, source_target_pairs={{0,24},{8,0},{16,8},{24,16},{1,25},{9,1},{17,9},{25,17},{2,26},{10... | collective-permute-start | bytes 491528 | tf_op jit(solution)/shard_map/ppermute | solution.py:27
  28.1 13.0 %collective-permute-start.11 = (bf16[640,128]{1,0:T(8,128)(2,1)S(1)}, bf16[640,128]{1,0:T(8,128)(2,1)S(1)}, u32[]{:S(2)}, u32[]{:S(2)}) collective-permute-start(bf16[640,128]{1,0:T(8,128)(2,1)S(1)} %get-tuple-element.47), channel_id=1, source_target_pairs={{0,16},{8,24},{16,0},{24,8},{1,17},{9,25},{17,1},{25,9},{2,18},{10... | collective-permute-start | bytes 491528 | tf_op jit(solution)/shard_map/ppermute | solution.py:27
  29.8 11.3 %collective-permute-start.12 = (bf16[640,128]{1,0:T(8,128)(2,1)S(1)}, bf16[640,128]{1,0:T(8,128)(2,1)S(1)}, u32[]{:S(2)}, u32[]{:S(2)}) collective-permute-start(bf16[640,128]{1,0:T(8,128)(2,1)S(1)} %get-tuple-element.48), channel_id=1, source_target_pairs={{0,8},{8,16},{16,24},{24,0},{1,9},{9,17},{17,25},{25,1},{2,10},{10... | collective-permute-start | bytes 491528 | tf_op jit(solution)/shard_map/ppermute | solution.py:27
  30.3 6.6 %collective-permute-start.7 = (bf16[256,128]{1,0:T(8,128)(2,1)S(1)}, bf16[256,128]{1,0:T(8,128)(2,1)S(1)}, u32[]{:S(2)}, u32[]{:S(2)}) collective-permute-start(bf16[256,128]{1,0:T(8,128)(2,1)S(1)} %fusion.16), channel_id=1, source_target_pairs={{0,2},{1,3},{2,4},{3,5},{4,6},{5,7},{6,0},{7,1},{8,10},{9,11},{10,... | collective-permute-start | bytes 196616 | tf_op jit(solution)/shard_map/ppermute | solution.py:32
  31.9 7.0 %collective-permute-start.8 = (bf16[256,128]{1,0:T(8,128)(2,1)S(1)}, bf16[256,128]{1,0:T(8,128)(2,1)S(1)}, u32[]{:S(2)}, u32[]{:S(2)}) collective-permute-start(bf16[256,128]{1,0:T(8,128)(2,1)S(1)} %fusion.16), channel_id=1, source_target_pairs={{0,4},{1,5},{2,6},{3,7},{4,0},{5,1},{6,2},{7,3},{8,12},{9,13},{10,... | collective-permute-start | bytes 196616 | tf_op jit(solution)/shard_map/ppermute | solution.py:32
  36.8 4.3 %collective-permute-start.9 = (bf16[256,128]{1,0:T(8,128)(2,1)S(1)}, bf16[256,128]{1,0:T(8,128)(2,1)S(1)}, u32[]{:S(2)}, u32[]{:S(2)}) collective-permute-start(bf16[256,128]{1,0:T(8,128)(2,1)S(1)} %fusion.16), channel_id=1, source_target_pairs={{0,6},{1,7},{2,0},{3,1},{4,2},{5,3},{6,4},{7,5},{8,14},{9,15},{10,... | collective-permute-start | bytes 196616 | tf_op jit(solution)/shard_map/ppermute | solution.py:32
  47.0 8.0 %collective-permute-start.18 = (bf16[640,128]{1,0:T(8,128)(2,1)S(1)}, bf16[640,128]{1,0:T(8,128)(2,1)S(1)}, u32[]{:S(2)}, u32[]{:S(2)}) collective-permute-start(bf16[640,128]{1,0:T(8,128)(2,1)S(1)} %bitcast.97), channel_id=1, source_target_pairs={{0,8},{8,16},{16,24},{24,0},{1,9},{9,17},{17,25},{25,1},{2,10},{10... | collective-permute-start | bytes 491528 | tf_op jit(solution)/shard_map/ppermute | solution.py:27
  48.1 10.0 %collective-permute-start.19 = (bf16[640,128]{1,0:T(8,128)(2,1)S(1)}, bf16[640,128]{1,0:T(8,128)(2,1)S(1)}, u32[]{:S(2)}, u32[]{:S(2)}) collective-permute-start(bf16[640,128]{1,0:T(8,128)(2,1)S(1)} %bitcast.96), channel_id=1, source_target_pairs={{0,16},{8,24},{16,0},{24,8},{1,17},{9,25},{17,1},{25,9},{2,18},{10... | collective-permute-start | bytes 491528 | tf_op jit(solution)/shard_map/ppermute | solution.py:27
  49.8 8.3 %collective-permute-start.20 = (bf16[640,128]{1,0:T(8,128)(2,1)S(1)}, bf16[640,128]{1,0:T(8,128)(2,1)S(1)}, u32[]{:S(2)}, u32[]{:S(2)}) collective-permute-start(bf16[640,128]{1,0:T(8,128)(2,1)S(1)} %bitcast.95), channel_id=1, source_target_pairs={{0,24},{8,0},{16,8},{24,16},{1,25},{9,1},{17,9},{25,17},{2,26},{10... | collective-permute-start | bytes 491528 | tf_op jit(solution)/shard_map/ppermute | solution.py:27
  50.5 10.9 %collective-permute-start.15 = (bf16[2,128,128]{2,1,0:T(8,128)(2,1)S(1)}, bf16[2,128,128]{2,1,0:T(8,128)(2,1)S(1)}, u32[]{:S(2)}, u32[]{:S(2)}) collective-permute-start(bf16[2,128,128]{2,1,0:T(8,128)(2,1)S(1)} %get-tuple-element.77), channel_id=1, source_target_pairs={{0,2},{1,3},{2,4},{3,5},{4,6},{5,7},{6,0},{7,1},{8,10},{9,11},{10,... | collective-permute-start | bytes 196616 | tf_op jit(solution)/shard_map/ppermute | solution.py:32
  50.6 10.8 %collective-permute-start.16 = (bf16[2,128,128]{2,1,0:T(8,128)(2,1)S(1)}, bf16[2,128,128]{2,1,0:T(8,128)(2,1)S(1)}, u32[]{:S(2)}, u32[]{:S(2)}) collective-permute-start(bf16[2,128,128]{2,1,0:T(8,128)(2,1)S(1)} %get-tuple-element.76), channel_id=1, source_target_pairs={{0,4},{1,5},{2,6},{3,7},{4,0},{5,1},{6,2},{7,3},{8,12},{9,13},{10,... | collective-permute-start | bytes 196616 | tf_op jit(solution)/shard_map/ppermute | solution.py:32
  55.0 6.5 %collective-permute-start.17 = (bf16[2,128,128]{2,1,0:T(8,128)(2,1)S(1)}, bf16[2,128,128]{2,1,0:T(8,128)(2,1)S(1)}, u32[]{:S(2)}, u32[]{:S(2)}) collective-permute-start(bf16[2,128,128]{2,1,0:T(8,128)(2,1)S(1)} %get-tuple-element.75), channel_id=1, source_target_pairs={{0,6},{1,7},{2,0},{3,1},{4,2},{5,3},{6,4},{7,5},{8,14},{9,15},{10,... | collective-permute-start | bytes 196616 | tf_op jit(solution)/shard_map/ppermute | solution.py:32
  58.8 13.3 %collective-permute-start.24 = (bf16[1280,128]{1,0:T(8,128)(2,1)S(1)}, bf16[1280,128]{1,0:T(8,128)(2,1)S(1)}, u32[]{:S(2)}, u32[]{:S(2)}) collective-permute-start(bf16[1280,128]{1,0:T(8,128)(2,1)S(1)} %get-tuple-element.63), channel_id=1, source_target_pairs={{0,24},{8,0},{16,8},{24,16},{1,25},{9,1},{17,9},{25,17},{2,26},{10... | collective-permute-start | bytes 983048 | tf_op jit(solution)/shard_map/ppermute | solution.py:27
  60.5 15.1 %collective-permute-start.25 = (bf16[1280,128]{1,0:T(8,128)(2,1)S(1)}, bf16[1280,128]{1,0:T(8,128)(2,1)S(1)}, u32[]{:S(2)}, u32[]{:S(2)}) collective-permute-start(bf16[1280,128]{1,0:T(8,128)(2,1)S(1)} %get-tuple-element.64), channel_id=1, source_target_pairs={{0,16},{8,24},{16,0},{24,8},{1,17},{9,25},{17,1},{25,9},{2,18},{10... | collective-permute-start | bytes 983048 | tf_op jit(solution)/shard_map/ppermute | solution.py:27
  61.4 14.2 %collective-permute-start.26 = (bf16[1280,128]{1,0:T(8,128)(2,1)S(1)}, bf16[1280,128]{1,0:T(8,128)(2,1)S(1)}, u32[]{:S(2)}, u32[]{:S(2)}) collective-permute-start(bf16[1280,128]{1,0:T(8,128)(2,1)S(1)} %get-tuple-element.65), channel_id=1, source_target_pairs={{0,8},{8,16},{16,24},{24,0},{1,9},{9,17},{17,25},{25,1},{2,10},{10... | collective-permute-start | bytes 983048 | tf_op jit(solution)/shard_map/ppermute | solution.py:27
  61.6 6.2 %collective-permute-start.21 = (bf16[256,128]{1,0:T(8,128)(2,1)S(1)}, bf16[256,128]{1,0:T(8,128)(2,1)S(1)}, u32[]{:S(2)}, u32[]{:S(2)}) collective-permute-start(bf16[256,128]{1,0:T(8,128)(2,1)S(1)} %fusion.17), channel_id=1, source_target_pairs={{0,2},{1,3},{2,4},{3,5},{4,6},{5,7},{6,0},{7,1},{8,10},{9,11},{10,... | collective-permute-start | bytes 196616 | tf_op jit(solution)/shard_map/ppermute | solution.py:32
  62.0 7.9 %collective-permute-start.22 = (bf16[256,128]{1,0:T(8,128)(2,1)S(1)}, bf16[256,128]{1,0:T(8,128)(2,1)S(1)}, u32[]{:S(2)}, u32[]{:S(2)}) collective-permute-start(bf16[256,128]{1,0:T(8,128)(2,1)S(1)} %fusion.17), channel_id=1, source_target_pairs={{0,4},{1,5},{2,6},{3,7},{4,0},{5,1},{6,2},{7,3},{8,12},{9,13},{10,... | collective-permute-start | bytes 196616 | tf_op jit(solution)/shard_map/ppermute | solution.py:32
  (14 other events, 139.8 us)

commit v3 on v1

v3 whole, which is shorter than its diff:
```python
import functools

import jax
import jax.numpy as jnp
from jax import lax
from jax.experimental import pallas as pl
from jax.experimental.pallas import tpu as pltpu
from jax.sharding import PartitionSpec as P

ITERS = 2

STEP_PRIMAL = 0.25
STEP_DUAL = 0.25

BF = jnp.bfloat16
F32 = jnp.float32
VMEM = pl.BlockSpec(memory_space=pltpu.VMEM)
SMEM = pl.BlockSpec(memory_space=pltpu.SMEM)
LIMIT = 48 * 1024 * 1024
FULL = 62 * 1024 * 1024
CORES = 2
STEP_COST = 0


def rotate(value, axis, by):
    size = lax.axis_size(axis)
    return lax.ppermute(value, axis, [(i, (i + by) % size) for i in range(size)])


def rotate_chip(value, by):
    size = lax.axis_size("zone")
    return lax.ppermute(value, "zone", [(i, (i + by * CORES) % size) for i in range(size)])


def flip_chip(value, by):
    size = lax.axis_size("zone")
    return lax.ppermute(value, "zone", [(i, i ^ (by * CORES)) for i in range(size)])


def swap_core(value):
    size = lax.axis_size("zone")
    return lax.ppermute(value, "zone", [(i, i ^ 1) for i in range(size)])


def after(values, others):
    return lax.optimization_barrier((*values, *others))[: len(values)]


def call(kernel, outs, scratch, flops, moved, *args, smem=0):
    return pl.pallas_call(
        kernel,
        out_shape=outs,
        in_specs=[SMEM] * smem + [VMEM] * (len(args) - smem),
        out_specs=jax.tree.map(lambda _: VMEM, outs),
        scratch_shapes=scratch,
        compiler_params=pltpu.CompilerParams(vmem_limit_bytes=LIMIT),
        cost_estimate=pl.CostEstimate(flops=flops, bytes_accessed=moved, transcendentals=0),
    )(*args)


def quarter_rows(by, parts, size):
    part = lax.rem(lax.axis_index("section") + by, parts)
    return pl.ds(pl.multiple_of(part * size, size), size)


def pack_kernel(parts, size, *refs):
    duals_in, stock_in, cost_in = refs[:3]
    outs = refs[3 : 2 + parts]
    duals, stock, cost = refs[2 + parts : 5 + parts]
    packets = refs[5 + parts : 4 + 2 * parts]
    sems, cost_sem, out_sems = refs[4 + 2 * parts :]
    tile = packets[0].shape[1]
    pieces = size // tile
    cost_copy = pltpu.make_async_copy(cost_in, cost, cost_sem)
    cost_copy.start()
    gets, gives = [], []
    for r in range(1, parts):
        rows = quarter_rows(r, parts, size)
        here = pl.ds((r - 1) * size, size)
        for i, (there, held) in enumerate(((duals_in, duals), (stock_in, stock))):
            gets.append(
                pltpu.make_async_copy(there.at[rows], held.at[here], sems.at[2 * (r - 1) + i])
            )
            gets[-1].start()
        gives.append(pltpu.make_async_copy(packets[r - 1], outs[r - 1], out_sems.at[r - 1]))
    cost_copy.wait()
    for r in range(1, parts):
        part = lax.rem(lax.axis_index("section") + r, parts)
        packet = packets[r - 1]
        here = slice((r - 1) * size, r * size)
        tail = packet.shape[0] - 2 * size
        lines = [
            cost[:, pl.ds(pl.multiple_of(part * size + i * tile, tile), tile)]
            for i in range(pieces)
        ]
        lines.append(jnp.zeros((tail - pieces, tile), F32))
        packet[2 * size :] = jnp.concatenate(lines, axis=0).astype(BF)
        gets[2 * r - 2].wait()
        packet[0:size] = duals[here].astype(BF)
        gets[2 * r - 1].wait()
        packet[size : 2 * size] = stock[here].astype(BF)
        gives[r - 1].start()
    for give in gives:
        give.wait()


def block_slot(place, col, k, shape):
    chips, owned = shape
    zone = lax.axis_index("zone")
    chip, core = lax.div(zone, CORES), lax.rem(zone, CORES)
    position = place[col[0, k]]
    owner, inner = lax.div(position, owned), lax.rem(position, owned)
    differ = lax.div(owner, CORES) ^ chip
    away, step, bit = 0, chips // 2, 1
    while step:
        away = away + bit * lax.rem(lax.div(differ, step), 2)
        step, bit = step // 2, bit * 2
    half = jnp.where(lax.rem(owner, CORES) == core, 0, chips * owned)
    return half + away * owned + inner


def pull_slots(shape, row, col, live, place, tiles, half, acc):
    slots = tiles.shape[0]
    blocks = acc.shape[0] - 1
    acc[...] = jnp.zeros_like(acc)

    def step(k, carry):
        there = jnp.where(live[0, k] == 1, block_slot(place, col, k, shape), blocks)
        acc[there] += lax.dot_general(
            tiles[k], half[row[0, k]], (((0,), (0,)), ((), ())), preferred_element_type=F32
        )
        return carry

    lax.fori_loop(0, slots, step, 0, unroll=8)


def push_slots(shape, row, col, live, place, tiles, blocks, acc):
    slots = tiles.shape[0]
    spare = acc.shape[0] - 1

    def step(k, carry):
        there = jnp.where(live[0, k] == 1, row[0, k], spare)
        acc[there] += jnp.dot(
            tiles[k],
            blocks[block_slot(place, col, k, shape)],
            preferred_element_type=F32,
        )
        return carry

    lax.fori_loop(0, slots, step, 0, unroll=8)


def give_partials(acc, keep, send):
    n = keep.shape[0]
    keep[...] = acc[0:n].astype(BF)
    send[...] = acc[n : 2 * n].astype(BF)


def pull_kernel(shape, row, col, live, place, tiles, duals, keep, send, *scratch):
    half, acc = scratch if len(scratch) == 2 else (duals, scratch[0])
    if len(scratch) == 2:
        half[...] = duals[...].astype(BF)
    pull_slots(shape, row, col, live, place, tiles, half, acc)
    give_partials(acc, keep, send)


def step_duals(shape, parts, size, refs, blocks, acc):
    row, col, live, place, tiles, duals, demand, near, far = refs[:9]
    combined = refs[9:]
    n = near.shape[0]
    blocks[0:n] = near[...]
    blocks[n : 2 * n] = far[...]
    pieces = size // tiles.shape[1]
    for r in range(parts):
        part = lax.rem(lax.axis_index("section") + r, parts)
        rows = pl.ds(part * pieces, pieces)
        acc[rows] = (
            duals[rows]
            + (STEP_DUAL * 0.25) * demand[rows].astype(F32)
            - STEP_DUAL * combined[r][0:size].astype(F32).reshape(pieces, *duals.shape[1:])
        )
    push_slots(shape, row, col, live, place, tiles, blocks, acc)


def push_step_kernel(shape, parts, size, *refs):
    ins, (next_duals, half), packets = refs[: 9 + parts], refs[9 + parts : 11 + parts], refs[11 + parts : -2]
    blocks, acc = refs[-2:]
    tile = ins[4].shape[1]
    step_duals(shape, parts, size, ins, blocks, acc)
    n = next_duals.shape[0]
    next_duals[...] = acc[0:n]
    half[...] = acc[0:n].astype(BF)
    pieces = size // tile
    for r in range(1, parts):
        part = lax.rem(lax.axis_index("section") + r, parts)
        packets[r - 1][...] = half[pl.ds(part * pieces, pieces)]


def place_kernel(parts, size, *refs):
    out = refs[parts]
    for r in range(parts):
        out[quarter_rows(r, parts, size), :] = refs[r][size:].astype(F32)


def last_push_kernel(shape, parts, size, *refs):
    ins = refs[: 9 + parts]
    next_duals, blocks, acc = refs[9 + parts :]
    step_duals(shape, parts, size, ins, blocks, acc)
    next_duals[...] = acc[0 : next_duals.shape[0]]


def own_rows(size, tile, i):
    return pl.ds(pl.multiple_of(lax.axis_index("section") * size + i * tile, tile), tile)


def eye_of(tile):
    return lax.broadcasted_iota(jnp.int32, (tile, tile), 0) == lax.broadcasted_iota(
        jnp.int32, (tile, tile), 1
    )


def stock_step(parts, lines, dual, stock, eye, ones):
    new = []
    for r in range(parts):
        line = jnp.where(eye, lines[r], 0.0).astype(BF)
        cost = jnp.dot(line, ones, preferred_element_type=F32)
        change = cost - dual[(r - 1) % parts] + dual[r]
        new.append(jnp.maximum(stock[r] - STEP_PRIMAL * change, 0.0))
    return new


def first_stock_kernel(parts, size, tile, *refs):
    own_duals, own_stock, own_cost, packets = *refs[:3], refs[3 : 2 + parts]
    stocks, combined = refs[2 + parts], refs[3 + parts :]
    eye, ones = eye_of(tile), jnp.ones((tile, tile), BF)
    costs = [None] + [packet[2 * size :].astype(F32) for packet in packets]
    for i in range(size // tile):
        rows = slice(i * tile, (i + 1) * tile)
        behind = slice(size + i * tile, size + (i + 1) * tile)
        own = own_rows(size, tile, i)
        dual = [own_duals[own, :]] + [packet[rows].astype(F32) for packet in packets]
        stock = [own_stock[own, :]] + [packet[behind].astype(F32) for packet in packets]
        lines = [own_cost[:, own]] + [c[i : i + 1] for c in costs[1:]]
        new = stock_step(parts, lines, dual, stock, eye, ones)
        bar = [2.0 * new[r] - stock[r] for r in range(parts)]
        for r in range(parts):
            stocks[r, rows] = new[r]
            combined[r][rows] = (bar[(r + 1) % parts] - bar[r]).astype(BF)


def last_stock_kernel(parts, size, tile, *refs):
    own_duals, own_cost, packets = *refs[:2], refs[2 : 1 + parts]
    stocks, duals, outs = refs[1 + parts], refs[2 + parts : 1 + 2 * parts], refs[1 + 2 * parts :]
    eye, ones = eye_of(tile), jnp.ones((tile, tile), BF)
    costs = [None] + [packet[2 * size :].astype(F32) for packet in packets]
    for i in range(size // tile):
        rows = slice(i * tile, (i + 1) * tile)
        behind = slice(size + i * tile, size + (i + 1) * tile)
        own = own_rows(size, tile, i)
        dual = [own_duals[own, :]] + [d[rows].astype(F32) for d in duals]
        stock = [stocks[r, rows] for r in range(parts)]
        lines = [own_cost[:, own]] + [c[i : i + 1] for c in costs[1:]]
        new = stock_step(parts, lines, dual, stock, eye, ones)
        bar = [2.0 * new[r] - stock[r] for r in range(parts)]
        for r in range(parts):
            outs[r][rows] = (bar[(r + 1) % parts] - bar[r]).astype(BF)
            outs[r][behind] = new[r].astype(BF)


def per_device(
    tiles,
    tile_row,
    tile_col,
    tile_live,
    block_place,
    demand,
    flow_cost,
    stock_cost,
    flows,
    stock,
    duals,
):
    unused_phases, slots, tile, unused_tile = tiles.shape
    scenarios = flows.shape[2]
    rows = duals.shape[1]
    parts = lax.axis_size("section")
    zones = lax.axis_size("zone")
    chips = zones // CORES
    blocks = block_place.shape[0]
    owned = blocks // zones
    band_tiles = rows // tile
    size = rows // parts
    shape = (chips, owned)
    tail = -(-(size // tile) // 16) * 16

    tiles = tiles.reshape(slots, tile, tile)
    duals2 = duals.reshape(rows, scenarios)
    stock2 = stock.reshape(rows, scenarios)
    flows2 = flows.reshape(owned * tile, scenarios)
    duals3 = duals.reshape(band_tiles, tile, scenarios)
    demand3 = demand.reshape(band_tiles, tile, scenarios)
    where = (tile_row, tile_col, tile_live, block_place)
    flops = 2 * slots * tile * tile * scenarios
    quarter = jax.ShapeDtypeStruct((size, scenarios), BF)
    quarter3 = jax.ShapeDtypeStruct((size // tile, tile, scenarios), BF)
    whole_half = jax.ShapeDtypeStruct((band_tiles, tile, scenarios), BF)
    half_blocks = jax.ShapeDtypeStruct((blocks // 2, tile, scenarios), BF)
    pull_scratch = [
        pltpu.VMEM((band_tiles, tile, scenarios), BF),
        pltpu.VMEM((blocks + 1, tile, scenarios), F32),
    ]
    push_scratch = [
        pltpu.VMEM((blocks, tile, scenarios), BF),
        pltpu.VMEM((band_tiles + 1, tile, scenarios), F32),
    ]

    known = block_place[0] >= 0

    def apart(f, *args):
        shapes = jax.eval_shape(f, *args)

        def none(*unused):
            return jax.tree.map(lambda v: jnp.zeros(v.shape, v.dtype), shapes)

        return lax.cond(known, f, none, *args)

    def add(value, other):
        return value.astype(F32) + other.astype(F32)

    def collect(keep, send, others):
        both = add(keep, send).astype(BF)
        parts_of = [both[k * owned : (k + 1) * owned] for k in range(chips)]
        got = []
        for k in range(1, chips):
            away = sum((chips // 2 >> i) * ((k >> i) & 1) for i in range(chips.bit_length()))
            got.append(flip_chip(parts_of[k], away))
        got = after(got, others)
        total = parts_of[0].astype(F32)
        for value in got:
            total = total + value.astype(F32)
        return total.reshape(owned * tile, scenarios)

    def spread(value, others):
        own = [value]
        step = chips // 2
        while step:
            own = own + [flip_chip(v, step) for v in own]
            step //= 2
        own = own[1:]
        own = after(own, others)
        near = jnp.concatenate([value, *own], axis=0).reshape(blocks // 2, tile, scenarios)
        return near, swap_core(near)

    def step_flows(now, pulled):
        new = jnp.maximum(now - STEP_PRIMAL * (flow_cost[0][:, None] - pulled), 0.0)
        return new, ((2.0 * new - now).astype(BF) * BF(-STEP_DUAL))

    ins = (duals2, stock2, stock_cost)
    packed = [jax.ShapeDtypeStruct((2 * size + tail, scenarios), BF)] * (parts - 1)
    packets = pl.pallas_call(
        functools.partial(pack_kernel, parts, size),
        out_shape=packed,
        in_specs=[pl.BlockSpec(memory_space=pltpu.HBM)] * len(ins),
        out_specs=[pl.BlockSpec(memory_space=pltpu.HBM)] * len(packed),
        scratch_shapes=[
            pltpu.VMEM(((parts - 1) * size, scenarios), F32),
            pltpu.VMEM(((parts - 1) * size, scenarios), F32),
            pltpu.VMEM(stock_cost.shape, F32),
        ]
        + [pltpu.VMEM(v.shape, v.dtype) for v in packed]
        + [
            pltpu.SemaphoreType.DMA((2 * (parts - 1),)),
            pltpu.SemaphoreType.DMA(()),
            pltpu.SemaphoreType.DMA((parts - 1,)),
        ],
        compiler_params=pltpu.CompilerParams(vmem_limit_bytes=FULL),
        cost_estimate=pl.CostEstimate(
            flops=0, bytes_accessed=12 * rows * scenarios, transcendentals=0
        ),
    )(*ins)
    packets = [rotate(packets[r - 1], "section", r) for r in range(1, parts)]

    stocks, *combined = call(
        functools.partial(first_stock_kernel, parts, size, tile),
        [jax.ShapeDtypeStruct((parts, size, scenarios), F32)] + [quarter] * parts,
        [],
        0,
        10 * rows * scenarios,
        duals2,
        stock2,
        stock_cost,
        *packets,
    )

    def pull(value, scratch):
        keep, send = call(
            functools.partial(pull_kernel, shape),
            [half_blocks, half_blocks],
            scratch,
            flops,
            2 * rows * scenarios + 2 * slots * tile * tile,
            *where,
            tiles,
            value,
            smem=4,
        )
        return keep, swap_core(send)

    keep, send = apart(lambda value: pull(value, pull_scratch), duals3)
    pulled = collect(keep, send, combined)
    flows1, bar1 = step_flows(flows2, pulled)
    combined = [combined[0]] + [rotate(combined[r], "section", -r) for r in range(1, parts)]
    near, far = spread(bar1, combined)

    duals1, half, *halves = call(
        functools.partial(push_step_kernel, shape, parts, size),
        [jax.ShapeDtypeStruct((band_tiles, tile, scenarios), F32), whole_half]
        + [quarter3] * (parts - 1),
        push_scratch,
        flops,
        16 * rows * scenarios + 2 * slots * tile * tile,
        *where,
        tiles,
        duals3,
        demand3,
        near,
        far,
        *combined,
        smem=4,
    )
    halves = [rotate(halves[r - 1].reshape(size, scenarios), "section", r) for r in range(1, parts)]
    outs = call(
        functools.partial(last_stock_kernel, parts, size, tile),
        [jax.ShapeDtypeStruct((2 * size, scenarios), BF)] * parts,
        [],
        0,
        10 * rows * scenarios,
        duals1.reshape(rows, scenarios),
        stock_cost,
        *packets,
        stocks,
        *halves,
    )
    keep, send = pull(half, pull_scratch[1:])
    pulled = collect(keep, send, outs)
    outs = [outs[0]] + [rotate(outs[r], "section", -r) for r in range(1, parts)]
    flows2_out, bar2 = step_flows(flows1, pulled)
    near, far = spread(bar2, outs)
    duals_out = call(
        functools.partial(last_push_kernel, shape, parts, size),
        jax.ShapeDtypeStruct((band_tiles, tile, scenarios), F32),
        push_scratch,
        flops,
        14 * rows * scenarios + 2 * slots * tile * tile,
        *where,
        tiles,
        duals1,
        demand3,
        near,
        far,
        *outs,
        smem=4,
    )
    stock_out = call(
        functools.partial(place_kernel, parts, size),
        jax.ShapeDtypeStruct((rows, scenarios), F32),
        [],
        0,
        6 * rows * scenarios,
        *outs,
    )
    return (
        flows2_out.reshape(flows.shape),
        stock_out.reshape(stock.shape),
        duals_out.reshape(duals.shape),
    )


def solution(mesh):
    in_specs = (
        P("section", "zone", None, None),
        P("section", "zone"),
        P("section", "zone"),
        P("section", "zone"),
        P(),
        P("section", "zone", None),
        P("section", "zone"),
        P("section", "zone"),
        P("section", "zone", None),
        P("section", "zone", None),
        P("section", "zone", None),
    )
    out_specs = (P("section", "zone", None), P("section", "zone", None), P("section", "zone", None))
    return jax.shard_map(
        per_device, mesh=mesh, in_specs=in_specs, out_specs=out_specs, check_vma=False
    )
```

time: 90.4 us -> 76.5 us (0.85)
  waiting for transfers between devices: 32.9 us -> 18.3 us
  local copies, waits for them, and re-layouts: 5.25 us -> 0.08 us
  starting transfers between devices: 38.3 us -> 41.2 us
  Pallas kernels: 11.5 us -> 14.3 us
    ppermute x15 -> x12, waiting for transfers between devices: 17.8 us -> 7.94 us  [rotate(): lax.ppermute(value, axis, [(i, (i + by) % size) for i in range(size)])]
    ppermute x12, starting transfers between devices: 17.3 us -> 24.7 us  [flip_chip(): lax.ppermute(value, 'zone', [(i, i ^ by * CORES) for i in range(size)])]
    unnamed x34 -> x22, local copies, waits for them, and re-layouts: 5.22 us -> 0.05 us
    ppermute x12, waiting for transfers between devices: 12.4 us -> 7.39 us  [flip_chip(): lax.ppermute(value, 'zone', [(i, i ^ by * CORES) for i in range(size)])]
    ppermute x15 -> x12, starting transfers between devices: 20.2 us -> 16.2 us  [rotate(): lax.ppermute(value, axis, [(i, (i + by) % size) for i in range(size)])]
    pallas_call x0 -> x1, Pallas kernels: none -> 2.42 us  [per_device(): pl.pallas_call(functools.partial(pack_kernel, parts, size), out_shape=pac...]
  transfers between devices with their start and end apart: 31 -> 28, of which waited for: 19 -> 13; matrix products, arithmetic and copies ran while one was open for 1% -> 2% of each run, Pallas kernels for 3% -> 7%
where the time goes in v3:
time: 76.5 us; the launch traced here: 76.3 us
  starting transfers between devices  41.2 us (54%)
  waiting for transfers between devices  18.3 us (24%)
  Pallas kernels  14.3 us (19%)
  other arithmetic  1.32 us (2%)
  between operations  0.96 us (1%)
    ppermute x12, starting transfers between devices, flip_chip(): lax.ppermute(value, 'zone', [(i, i ^ by * CORES) for i in range(size)])  24.7 us
    ppermute x12, starting transfers between devices, rotate(): lax.ppermute(value, axis, [(i, (i + by) % size) for i in range(size)])  16.2 us
    pallas_call x7, Pallas kernels, call(): pl.pallas_call(kernel, out_shape=outs, in_specs=[SMEM] * smem + [VMEM] *...  11.9 us
    ppermute x12, waiting for transfers between devices, rotate(): lax.ppermute(value, axis, [(i, (i + by) % size) for i in range(size)])  7.94 us
    ppermute x12, waiting for transfers between devices, flip_chip(): lax.ppermute(value, 'zone', [(i, i ^ by * CORES) for i in range(size)])  7.39 us
    ppermute x4, waiting for transfers between devices, swap_core(): return lax.ppermute(value, 'zone', [(i, i ^ 1) for i in range(size)])  3 us
    pallas_call x1, Pallas kernels, per_device(): pl.pallas_call(functools.partial(pack_kernel, parts, size), out_shape=pac...  2.42 us
  transfers between devices with their start and end apart: 28, of which 13 were waited for; matrix products, arithmetic and copies ran while one was open for 2% of the time, Pallas kernels for 7%

profile of v3, /device:TPU:0, one launch (start us, length us, event | category | flops | bytes accessed | tf_op | source)
XLA Modules:
  0.0 76.3 jit_solution(17401509948472742153)
XLA Ops:
  0.7 2.4 %shard_map.133 = (bf16[1296,128]{1,0:T(8,128)(2,1)}, bf16[1296,128]{1,0:T(8,128)(2,1)}, bf16[1296,128]{1,0:T(8,128)(2,1)}) custom-call(f32[2560,128]{1,0:T(8,128)} %bitcast.87, f32[2560,128]{1,0:T(8,128)} %bitcast.75, f32[1,2560]{1,0:T(1,128)} %refs_1_.4), custom_call_target="tpu_custom_call" | custom-call | bytes 3932160 | tf_op jit(solution)/shard_map/pallas_call | solution.py:360
  3.1 3.0 %collective-permute-start.4 = (bf16[1296,128]{1,0:T(8,128)(2,1)}, bf16[1296,128]{1,0:T(8,128)(2,1)S(1)}, u32[]{:S(2)}, u32[]{:S(2)}) collective-permute-start(bf16[1296,128]{1,0:T(8,128)(2,1)} %get-tuple-element.60), channel_id=1, source_target_pairs={{0,8},{8,16},{16,24},{24,0},{1,9},{9,17},{17,25},{25,1},{2,10},{10... | collective-permute-start | bytes 995336 | tf_op jit(solution)/shard_map/ppermute | solution.py:27
  9.1 4.2 %conditional.1 = (f32[8,128,128]{2,1,0:T(8,128)S(1)}, f32[8,128,128]{2,1,0:T(8,128)S(1)}) conditional(s32[]{:T(128)} %bitcast.1, () %tuple.24, (s32[1,32]{1,0:T(1,128)S(1)}, s32[1,32]{1,0:T(1,128)S(1)}, s32[1,32]{1,0:T(1,128)S(1)}, s32[16]{0:T(128)S(1)}, bf16[32,128,128]{2,1,0:T(8,128)(2,1)}, /*index=5*/f32[20,128,128]{2,1,0:T(8,128)S(1)}) %tuple.42), branch_computations={%region_0.0_spmd, %region_1.0_spmd} | conditional | flops 134479872 | bytes 4325432 | solution.py:325
  9.2 2.5 %branch_1_fun.1 = (bf16[8,128,128]{2,1,0:T(8,128)(2,1)S(1)}, bf16[8,128,128]{2,1,0:T(8,128)(2,1)S(1)}) custom-call(s32[1,32]{1,0:T(1,128)S(1)} %get-tuple-element.14.row, s32[1,32]{1,0:T(1,128)S(1)} %get-tuple-element.15.col, s32[1,32]{1,0:T(1,128)S(1)} %get-tuple-element.16.live, s32[16]{0:T(128)S(1)} %get-tuple-element.17.place, ...), custom_call_target="tpu_custom_call" | custom-call | flops 134217728 | bytes 1703936 | tf_op jit(solution)/shard_map/cond/branch_1_fun/pallas_call | solution.py:50
  13.4 3.7 %collective-permute-start.3 = (bf16[2,128,128]{2,1,0:T(8,128)(2,1)S(1)}, bf16[2,128,128]{2,1,0:T(8,128)(2,1)S(1)}, u32[]{:S(2)}, u32[]{:S(2)}) collective-permute-start(bf16[2,128,128]{2,1,0:T(8,128)(2,1)S(1)} %get-tuple-element.94), channel_id=1, source_target_pairs={{0,6},{1,7},{2,4},{3,5},{4,2},{5,3},{6,0},{7,1},{8,14},{9,15},{10,... | collective-permute-start | bytes 196616 | tf_op jit(solution)/shard_map/ppermute | solution.py:37
  17.1 1.9 %collective-permute-start.1 = (bf16[2,128,128]{2,1,0:T(8,128)(2,1)S(1)}, bf16[2,128,128]{2,1,0:T(8,128)(2,1)S(1)}, u32[]{:S(2)}, u32[]{:S(2)}) collective-permute-start(bf16[2,128,128]{2,1,0:T(8,128)(2,1)S(1)} %get-tuple-element.96), channel_id=1, source_target_pairs={{0,4},{1,5},{2,6},{3,7},{4,0},{5,1},{6,2},{7,3},{8,12},{9,13},{10,... | collective-permute-start | bytes 196616 | tf_op jit(solution)/shard_map/ppermute | solution.py:37
  19.0 3.1 %collective-permute-done.5.refs_4_.refs_3_ = bf16[1296,128]{1,0:T(8,128)(2,1)S(1)} collective-permute-done((bf16[1296,128]{1,0:T(8,128)(2,1)}, bf16[1296,128]{1,0:T(8,128)(2,1)S(1)}, u32[]{:S(2)}, u32[]{:S(2)}) %collective-permute-start.5) | collective-permute-done | bytes 331808 | tf_op jit(solution)/shard_map/ppermute | solution.py:27
  23.2 1.6 %collective-permute-start.10 = (bf16[640,128]{1,0:T(8,128)(2,1)S(1)}, bf16[640,128]{1,0:T(8,128)(2,1)S(1)}, u32[]{:S(2)}, u32[]{:S(2)}) collective-permute-start(bf16[640,128]{1,0:T(8,128)(2,1)S(1)} %get-tuple-element.64), channel_id=1, source_target_pairs={{0,24},{8,0},{16,8},{24,16},{1,25},{9,1},{17,9},{25,17},{2,26},{10... | collective-permute-start | bytes 491528 | tf_op jit(solution)/shard_map/ppermute | solution.py:27
  24.8 1.6 %collective-permute-start.11 = (bf16[640,128]{1,0:T(8,128)(2,1)S(1)}, bf16[640,128]{1,0:T(8,128)(2,1)S(1)}, u32[]{:S(2)}, u32[]{:S(2)}) collective-permute-start(bf16[640,128]{1,0:T(8,128)(2,1)S(1)} %get-tuple-element.65), channel_id=1, source_target_pairs={{0,16},{8,24},{16,0},{24,8},{1,17},{9,25},{17,1},{25,9},{2,18},{10... | collective-permute-start | bytes 491528 | tf_op jit(solution)/shard_map/ppermute | solution.py:27
  26.9 2.7 %collective-permute-start.7 = (bf16[256,128]{1,0:T(8,128)(2,1)S(1)}, bf16[256,128]{1,0:T(8,128)(2,1)S(1)}, u32[]{:S(2)}, u32[]{:S(2)}) collective-permute-start(bf16[256,128]{1,0:T(8,128)(2,1)S(1)} %fusion.16), channel_id=1, source_target_pairs={{0,4},{1,5},{2,6},{3,7},{4,0},{5,1},{6,2},{7,3},{8,12},{9,13},{10,... | collective-permute-start | bytes 196616 | tf_op jit(solution)/shard_map/ppermute | solution.py:37
  29.5 1.6 %collective-permute-start.8 = (bf16[256,128]{1,0:T(8,128)(2,1)S(1)}, bf16[256,128]{1,0:T(8,128)(2,1)S(1)}, u32[]{:S(2)}, u32[]{:S(2)}) collective-permute-start(bf16[256,128]{1,0:T(8,128)(2,1)S(1)} %fusion.16), channel_id=1, source_target_pairs={{0,2},{1,3},{2,0},{3,1},{4,6},{5,7},{6,4},{7,5},{8,10},{9,11},{10,... | collective-permute-start | bytes 196616 | tf_op jit(solution)/shard_map/ppermute | solution.py:37
  34.1 2.3 %collective-permute-done.9 = bf16[256,128]{1,0:T(8,128)(2,1)S(1)} collective-permute-done((bf16[256,128]{1,0:T(8,128)(2,1)S(1)}, bf16[256,128]{1,0:T(8,128)(2,1)S(1)}, u32[]{:S(2)}, u32[]{:S(2)}) %collective-permute-start.9) | collective-permute-done | bytes 65568 | tf_op jit(solution)/shard_map/ppermute | solution.py:37
  38.1 2.1 %shard_map.135 = (f32[20,128,128]{2,1,0:T(8,128)S(1)}, bf16[20,128,128]{2,1,0:T(8,128)(2,1)S(1)}, bf16[5,128,128]{2,1,0:T(8,128)(2,1)S(1)}, bf16[5,128,128]{2,1,0:T(8,128)(2,1)S(1)}, bf16[5,128,128]{2,1,0:T(8,128)(2,1)S(1)}) custom-call(s32[1,32]{1,0:T(1,128)S(1)} %copy-done.7, s32[1,32]{1,0:T(1,128)S(1)} %copy-done.8, s32[1,32]{1,0:T(1,128)S(1)} %copy-done.9, ...), custom_call_target="tpu_custom_call" | custom-call | flops 134217728 | bytes 6291456 | tf_op jit(solution)/shard_map/pallas_call | solution.py:50
  40.2 1.8 %shard_map.136 = (bf16[8,128,128]{2,1,0:T(8,128)(2,1)S(1)}, bf16[8,128,128]{2,1,0:T(8,128)(2,1)S(1)}) custom-call(s32[1,32]{1,0:T(1,128)S(1)} %copy-done.7, s32[1,32]{1,0:T(1,128)S(1)} %copy-done.8, s32[1,32]{1,0:T(1,128)S(1)} %copy-done.9, s32[16]{0:T(128)S(1)} %copy-done.10, bf16[32,128,128]{2,1,0:T(8,128)(2,1)S(1)} %bitcast.93, ...), custom_call_target="tpu_custom_call" | custom-call | flops 134217728 | bytes 1703936 | tf_op jit(solution)/shard_map/pallas_call | solution.py:50
  43.7 1.6 %collective-permute-start.19 = (bf16[640,128]{1,0:T(8,128)(2,1)S(1)}, bf16[640,128]{1,0:T(8,128)(2,1)S(1)}, u32[]{:S(2)}, u32[]{:S(2)}) collective-permute-start(bf16[640,128]{1,0:T(8,128)(2,1)S(1)} %bitcast.85), channel_id=1, source_target_pairs={{0,16},{8,24},{16,0},{24,8},{1,17},{9,25},{17,1},{25,9},{2,18},{10... | collective-permute-start | bytes 491528 | tf_op jit(solution)/shard_map/ppermute | solution.py:27
  45.8 4.2 %collective-permute-start.17 = (bf16[2,128,128]{2,1,0:T(8,128)(2,1)S(1)}, bf16[2,128,128]{2,1,0:T(8,128)(2,1)S(1)}, u32[]{:S(2)}, u32[]{:S(2)}) collective-permute-start(bf16[2,128,128]{2,1,0:T(8,128)(2,1)S(1)} %get-tuple-element.91), channel_id=1, source_target_pairs={{0,6},{1,7},{2,4},{3,5},{4,2},{5,3},{6,0},{7,1},{8,14},{9,15},{10,... | collective-permute-start | bytes 196616 | tf_op jit(solution)/shard_map/ppermute | solution.py:37
  50.2 2.8 %collective-permute-start.15 = (bf16[2,128,128]{2,1,0:T(8,128)(2,1)S(1)}, bf16[2,128,128]{2,1,0:T(8,128)(2,1)S(1)}, u32[]{:S(2)}, u32[]{:S(2)}) collective-permute-start(bf16[2,128,128]{2,1,0:T(8,128)(2,1)S(1)} %get-tuple-element.93), channel_id=1, source_target_pairs={{0,4},{1,5},{2,6},{3,7},{4,0},{5,1},{6,2},{7,3},{8,12},{9,13},{10,... | collective-permute-start | bytes 196616 | tf_op jit(solution)/shard_map/ppermute | solution.py:37
  53.8 1.8 %collective-permute-start.21 = (bf16[1280,128]{1,0:T(8,128)(2,1)S(1)}, bf16[1280,128]{1,0:T(8,128)(2,1)S(1)}, u32[]{:S(2)}, u32[]{:S(2)}) collective-permute-start(bf16[1280,128]{1,0:T(8,128)(2,1)S(1)} %get-tuple-element.82), channel_id=1, source_target_pairs={{0,24},{8,0},{16,8},{24,16},{1,25},{9,1},{17,9},{25,17},{2,26},{10... | collective-permute-start | bytes 983048 | tf_op jit(solution)/shard_map/ppermute | solution.py:27
  57.1 3.1 %collective-permute-start.24 = (bf16[256,128]{1,0:T(8,128)(2,1)S(1)}, bf16[256,128]{1,0:T(8,128)(2,1)S(1)}, u32[]{:S(2)}, u32[]{:S(2)}) collective-permute-start(bf16[256,128]{1,0:T(8,128)(2,1)S(1)} %fusion.17), channel_id=1, source_target_pairs={{0,4},{1,5},{2,6},{3,7},{4,0},{5,1},{6,2},{7,3},{8,12},{9,13},{10,... | collective-permute-start | bytes 196616 | tf_op jit(solution)/shard_map/ppermute | solution.py:37
  60.2 1.8 %collective-permute-start.25 = (bf16[256,128]{1,0:T(8,128)(2,1)S(1)}, bf16[256,128]{1,0:T(8,128)(2,1)S(1)}, u32[]{:S(2)}, u32[]{:S(2)}) collective-permute-start(bf16[256,128]{1,0:T(8,128)(2,1)S(1)} %fusion.17), channel_id=1, source_target_pairs={{0,2},{1,3},{2,0},{3,1},{4,6},{5,7},{6,4},{7,5},{8,10},{9,11},{10,... | collective-permute-start | bytes 196616 | tf_op jit(solution)/shard_map/ppermute | solution.py:37
  62.8 1.5 %collective-permute-start.26 = (bf16[256,128]{1,0:T(8,128)(2,1)S(1)}, bf16[256,128]{1,0:T(8,128)(2,1)S(1)}, u32[]{:S(2)}, u32[]{:S(2)}) collective-permute-start(bf16[256,128]{1,0:T(8,128)(2,1)S(1)} %collective-permute-done.24), channel_id=1, source_target_pairs={{0,2},{1,3},{2,0},{3,1},{4,6},{5,7},{6,4},{7,5},{8,10},{9,11},{10,... | collective-permute-start | bytes 196616 | tf_op jit(solution)/shard_map/ppermute | solution.py:37
  64.7 2.4 %collective-permute-done.26 = bf16[256,128]{1,0:T(8,128)(2,1)S(1)} collective-permute-done((bf16[256,128]{1,0:T(8,128)(2,1)S(1)}, bf16[256,128]{1,0:T(8,128)(2,1)S(1)}, u32[]{:S(2)}, u32[]{:S(2)}) %collective-permute-start.26) | collective-permute-done | bytes 65568 | tf_op jit(solution)/shard_map/ppermute | solution.py:37
  67.1 4.2 %collective-permute-done.22.refs_2_.refs_11_ = bf16[1280,128]{1,0:T(8,128)(2,1)S(1)} collective-permute-done((bf16[1280,128]{1,0:T(8,128)(2,1)S(1)}, bf16[1280,128]{1,0:T(8,128)(2,1)S(1)}, u32[]{:S(2)}, u32[]{:S(2)}) %collective-permute-start.22) | collective-permute-done | bytes 327712 | tf_op jit(solution)/shard_map/ppermute | solution.py:27
  73.3 3.1 %shard_map.139 = f32[20,128,128]{2,1,0:T(8,128)} custom-call(s32[1,32]{1,0:T(1,128)S(1)} %copy-done.7, s32[1,32]{1,0:T(1,128)S(1)} %copy-done.8, s32[1,32]{1,0:T(1,128)S(1)} %copy-done.9, s32[16]{0:T(128)S(1)} %copy-done.10, bf16[32,128,128]{2,1,0:T(8,128)(2,1)S(1)} %bitcast.94, f32[20,128,128]{2,1,0:T(8,128)S(1)} %get-tuple-element.76.refs_5_, ...), custom_call_target="tpu_custom_call" | custom-call | flops 134217728 | bytes 5636096 | tf_op jit(solution)/shard_map/pallas_call | solution.py:50
  (76 shorter events, 18.5 us)
Async XLA Ops:
  3.1 14.0 %collective-permute-start.4 = (bf16[1296,128]{1,0:T(8,128)(2,1)}, bf16[1296,128]{1,0:T(8,128)(2,1)S(1)}, u32[]{:S(2)}, u32[]{:S(2)}) collective-permute-start(bf16[1296,128]{1,0:T(8,128)(2,1)} %get-tuple-element.60), channel_id=1, source_target_pairs={{0,8},{8,16},{16,24},{24,0},{1,9},{9,17},{17,25},{25,1},{2,10},{10... | collective-permute-start | bytes 995336 | tf_op jit(solution)/shard_map/ppermute | solution.py:27
  6.1 16.1 %collective-permute-start.5 = (bf16[1296,128]{1,0:T(8,128)(2,1)}, bf16[1296,128]{1,0:T(8,128)(2,1)S(1)}, u32[]{:S(2)}, u32[]{:S(2)}) collective-permute-start(bf16[1296,128]{1,0:T(8,128)(2,1)} %get-tuple-element.61), channel_id=1, source_target_pairs={{0,16},{8,24},{16,0},{24,8},{1,17},{9,25},{17,1},{25,9},{2,18},{10... | collective-permute-start | bytes 995336 | tf_op jit(solution)/shard_map/ppermute | solution.py:27
  7.6 14.8 %collective-permute-start.6 = (bf16[1296,128]{1,0:T(8,128)(2,1)}, bf16[1296,128]{1,0:T(8,128)(2,1)S(1)}, u32[]{:S(2)}, u32[]{:S(2)}) collective-permute-start(bf16[1296,128]{1,0:T(8,128)(2,1)} %get-tuple-element.62), channel_id=1, source_target_pairs={{0,24},{8,0},{16,8},{24,16},{1,25},{9,1},{17,9},{25,17},{2,26},{10... | collective-permute-start | bytes 995336 | tf_op jit(solution)/shard_map/ppermute | solution.py:27
  13.4 13.0 %collective-permute-start.3 = (bf16[2,128,128]{2,1,0:T(8,128)(2,1)S(1)}, bf16[2,128,128]{2,1,0:T(8,128)(2,1)S(1)}, u32[]{:S(2)}, u32[]{:S(2)}) collective-permute-start(bf16[2,128,128]{2,1,0:T(8,128)(2,1)S(1)} %get-tuple-element.94), channel_id=1, source_target_pairs={{0,6},{1,7},{2,4},{3,5},{4,2},{5,3},{6,0},{7,1},{8,14},{9,15},{10,... | collective-permute-start | bytes 196616 | tf_op jit(solution)/shard_map/ppermute | solution.py:37
  17.1 9.6 %collective-permute-start.2 = (bf16[2,128,128]{2,1,0:T(8,128)(2,1)S(1)}, bf16[2,128,128]{2,1,0:T(8,128)(2,1)S(1)}, u32[]{:S(2)}, u32[]{:S(2)}) collective-permute-start(bf16[2,128,128]{2,1,0:T(8,128)(2,1)S(1)} %get-tuple-element.95), channel_id=1, source_target_pairs={{0,2},{1,3},{2,0},{3,1},{4,6},{5,7},{6,4},{7,5},{8,10},{9,11},{10,... | collective-permute-start | bytes 196616 | tf_op jit(solution)/shard_map/ppermute | solution.py:37
  17.1 9.6 %collective-permute-start.1 = (bf16[2,128,128]{2,1,0:T(8,128)(2,1)S(1)}, bf16[2,128,128]{2,1,0:T(8,128)(2,1)S(1)}, u32[]{:S(2)}, u32[]{:S(2)}) collective-permute-start(bf16[2,128,128]{2,1,0:T(8,128)(2,1)S(1)} %get-tuple-element.96), channel_id=1, source_target_pairs={{0,4},{1,5},{2,6},{3,7},{4,0},{5,1},{6,2},{7,3},{8,12},{9,13},{10,... | collective-permute-start | bytes 196616 | tf_op jit(solution)/shard_map/ppermute | solution.py:37
  23.2 13.3 %collective-permute-start.10 = (bf16[640,128]{1,0:T(8,128)(2,1)S(1)}, bf16[640,128]{1,0:T(8,128)(2,1)S(1)}, u32[]{:S(2)}, u32[]{:S(2)}) collective-permute-start(bf16[640,128]{1,0:T(8,128)(2,1)S(1)} %get-tuple-element.64), channel_id=1, source_target_pairs={{0,24},{8,0},{16,8},{24,16},{1,25},{9,1},{17,9},{25,17},{2,26},{10... | collective-permute-start | bytes 491528 | tf_op jit(solution)/shard_map/ppermute | solution.py:27
  24.8 11.7 %collective-permute-start.11 = (bf16[640,128]{1,0:T(8,128)(2,1)S(1)}, bf16[640,128]{1,0:T(8,128)(2,1)S(1)}, u32[]{:S(2)}, u32[]{:S(2)}) collective-permute-start(bf16[640,128]{1,0:T(8,128)(2,1)S(1)} %get-tuple-element.65), channel_id=1, source_target_pairs={{0,16},{8,24},{16,0},{24,8},{1,17},{9,25},{17,1},{25,9},{2,18},{10... | collective-permute-start | bytes 491528 | tf_op jit(solution)/shard_map/ppermute | solution.py:27
  26.4 10.1 %collective-permute-start.12 = (bf16[640,128]{1,0:T(8,128)(2,1)S(1)}, bf16[640,128]{1,0:T(8,128)(2,1)S(1)}, u32[]{:S(2)}, u32[]{:S(2)}) collective-permute-start(bf16[640,128]{1,0:T(8,128)(2,1)S(1)} %get-tuple-element.66), channel_id=1, source_target_pairs={{0,8},{8,16},{16,24},{24,0},{1,9},{9,17},{17,25},{25,1},{2,10},{10... | collective-permute-start | bytes 491528 | tf_op jit(solution)/shard_map/ppermute | solution.py:27
  26.9 5.3 %collective-permute-start.7 = (bf16[256,128]{1,0:T(8,128)(2,1)S(1)}, bf16[256,128]{1,0:T(8,128)(2,1)S(1)}, u32[]{:S(2)}, u32[]{:S(2)}) collective-permute-start(bf16[256,128]{1,0:T(8,128)(2,1)S(1)} %fusion.16), channel_id=1, source_target_pairs={{0,4},{1,5},{2,6},{3,7},{4,0},{5,1},{6,2},{7,3},{8,12},{9,13},{10,... | collective-permute-start | bytes 196616 | tf_op jit(solution)/shard_map/ppermute | solution.py:37
  29.5 4.6 %collective-permute-start.8 = (bf16[256,128]{1,0:T(8,128)(2,1)S(1)}, bf16[256,128]{1,0:T(8,128)(2,1)S(1)}, u32[]{:S(2)}, u32[]{:S(2)}) collective-permute-start(bf16[256,128]{1,0:T(8,128)(2,1)S(1)} %fusion.16), channel_id=1, source_target_pairs={{0,2},{1,3},{2,0},{3,1},{4,6},{5,7},{6,4},{7,5},{8,10},{9,11},{10,... | collective-permute-start | bytes 196616 | tf_op jit(solution)/shard_map/ppermute | solution.py:37
  32.2 4.3 %collective-permute-start.9 = (bf16[256,128]{1,0:T(8,128)(2,1)S(1)}, bf16[256,128]{1,0:T(8,128)(2,1)S(1)}, u32[]{:S(2)}, u32[]{:S(2)}) collective-permute-start(bf16[256,128]{1,0:T(8,128)(2,1)S(1)} %collective-permute-done.7), channel_id=1, source_target_pairs={{0,2},{1,3},{2,0},{3,1},{4,6},{5,7},{6,4},{7,5},{8,10},{9,11},{10,... | collective-permute-start | bytes 196616 | tf_op jit(solution)/shard_map/ppermute | solution.py:37
  42.2 8.0 %collective-permute-start.18 = (bf16[640,128]{1,0:T(8,128)(2,1)S(1)}, bf16[640,128]{1,0:T(8,128)(2,1)S(1)}, u32[]{:S(2)}, u32[]{:S(2)}) collective-permute-start(bf16[640,128]{1,0:T(8,128)(2,1)S(1)} %bitcast.86), channel_id=1, source_target_pairs={{0,8},{8,16},{16,24},{24,0},{1,9},{9,17},{17,25},{25,1},{2,10},{10... | collective-permute-start | bytes 491528 | tf_op jit(solution)/shard_map/ppermute | solution.py:27
  43.7 9.4 %collective-permute-start.19 = (bf16[640,128]{1,0:T(8,128)(2,1)S(1)}, bf16[640,128]{1,0:T(8,128)(2,1)S(1)}, u32[]{:S(2)}, u32[]{:S(2)}) collective-permute-start(bf16[640,128]{1,0:T(8,128)(2,1)S(1)} %bitcast.85), channel_id=1, source_target_pairs={{0,16},{8,24},{16,0},{24,8},{1,17},{9,25},{17,1},{25,9},{2,18},{10... | collective-permute-start | bytes 491528 | tf_op jit(solution)/shard_map/ppermute | solution.py:27
  45.4 7.7 %collective-permute-start.20 = (bf16[640,128]{1,0:T(8,128)(2,1)S(1)}, bf16[640,128]{1,0:T(8,128)(2,1)S(1)}, u32[]{:S(2)}, u32[]{:S(2)}) collective-permute-start(bf16[640,128]{1,0:T(8,128)(2,1)S(1)} %bitcast.84), channel_id=1, source_target_pairs={{0,24},{8,0},{16,8},{24,16},{1,25},{9,1},{17,9},{25,17},{2,26},{10... | collective-permute-start | bytes 491528 | tf_op jit(solution)/shard_map/ppermute | solution.py:27
  45.8 11.1 %collective-permute-start.17 = (bf16[2,128,128]{2,1,0:T(8,128)(2,1)S(1)}, bf16[2,128,128]{2,1,0:T(8,128)(2,1)S(1)}, u32[]{:S(2)}, u32[]{:S(2)}) collective-permute-start(bf16[2,128,128]{2,1,0:T(8,128)(2,1)S(1)} %get-tuple-element.91), channel_id=1, source_target_pairs={{0,6},{1,7},{2,4},{3,5},{4,2},{5,3},{6,0},{7,1},{8,14},{9,15},{10,... | collective-permute-start | bytes 196616 | tf_op jit(solution)/shard_map/ppermute | solution.py:37
  50.0 6.9 %collective-permute-start.16 = (bf16[2,128,128]{2,1,0:T(8,128)(2,1)S(1)}, bf16[2,128,128]{2,1,0:T(8,128)(2,1)S(1)}, u32[]{:S(2)}, u32[]{:S(2)}) collective-permute-start(bf16[2,128,128]{2,1,0:T(8,128)(2,1)S(1)} %get-tuple-element.92), channel_id=1, source_target_pairs={{0,2},{1,3},{2,0},{3,1},{4,6},{5,7},{6,4},{7,5},{8,10},{9,11},{10,... | collective-permute-start | bytes 196616 | tf_op jit(solution)/shard_map/ppermute | solution.py:37
  50.2 6.8 %collective-permute-start.15 = (bf16[2,128,128]{2,1,0:T(8,128)(2,1)S(1)}, bf16[2,128,128]{2,1,0:T(8,128)(2,1)S(1)}, u32[]{:S(2)}, u32[]{:S(2)}) collective-permute-start(bf16[2,128,128]{2,1,0:T(8,128)(2,1)S(1)} %get-tuple-element.93), channel_id=1, source_target_pairs={{0,4},{1,5},{2,6},{3,7},{4,0},{5,1},{6,2},{7,3},{8,12},{9,13},{10,... | collective-permute-start | bytes 196616 | tf_op jit(solution)/shard_map/ppermute | solution.py:37
  53.8 13.3 %collective-permute-start.21 = (bf16[1280,128]{1,0:T(8,128)(2,1)S(1)}, bf16[1280,128]{1,0:T(8,128)(2,1)S(1)}, u32[]{:S(2)}, u32[]{:S(2)}) collective-permute-start(bf16[1280,128]{1,0:T(8,128)(2,1)S(1)} %get-tuple-element.82), channel_id=1, source_target_pairs={{0,24},{8,0},{16,8},{24,16},{1,25},{9,1},{17,9},{25,17},{2,26},{10... | collective-permute-start | bytes 983048 | tf_op jit(solution)/shard_map/ppermute | solution.py:27
  55.6 15.7 %collective-permute-start.22 = (bf16[1280,128]{1,0:T(8,128)(2,1)S(1)}, bf16[1280,128]{1,0:T(8,128)(2,1)S(1)}, u32[]{:S(2)}, u32[]{:S(2)}) collective-permute-start(bf16[1280,128]{1,0:T(8,128)(2,1)S(1)} %get-tuple-element.83), channel_id=1, source_target_pairs={{0,16},{8,24},{16,0},{24,8},{1,17},{9,25},{17,1},{25,9},{2,18},{10... | collective-permute-start | bytes 983048 | tf_op jit(solution)/shard_map/ppermute | solution.py:27
  56.9 14.3 %collective-permute-start.23 = (bf16[1280,128]{1,0:T(8,128)(2,1)S(1)}, bf16[1280,128]{1,0:T(8,128)(2,1)S(1)}, u32[]{:S(2)}, u32[]{:S(2)}) collective-permute-start(bf16[1280,128]{1,0:T(8,128)(2,1)S(1)} %get-tuple-element.84), channel_id=1, source_target_pairs={{0,8},{8,16},{16,24},{24,0},{1,9},{9,17},{17,25},{25,1},{2,10},{10... | collective-permute-start | bytes 983048 | tf_op jit(solution)/shard_map/ppermute | solution.py:27
  57.1 5.7 %collective-permute-start.24 = (bf16[256,128]{1,0:T(8,128)(2,1)S(1)}, bf16[256,128]{1,0:T(8,128)(2,1)S(1)}, u32[]{:S(2)}, u32[]{:S(2)}) collective-permute-start(bf16[256,128]{1,0:T(8,128)(2,1)S(1)} %fusion.17), channel_id=1, source_target_pairs={{0,4},{1,5},{2,6},{3,7},{4,0},{5,1},{6,2},{7,3},{8,12},{9,13},{10,... | collective-permute-start | bytes 196616 | tf_op jit(solution)/shard_map/ppermute | solution.py:37
  60.2 4.4 %collective-permute-start.25 = (bf16[256,128]{1,0:T(8,128)(2,1)S(1)}, bf16[256,128]{1,0:T(8,128)(2,1)S(1)}, u32[]{:S(2)}, u32[]{:S(2)}) collective-permute-start(bf16[256,128]{1,0:T(8,128)(2,1)S(1)} %fusion.17), channel_id=1, source_target_pairs={{0,2},{1,3},{2,0},{3,1},{4,6},{5,7},{6,4},{7,5},{8,10},{9,11},{10,... | collective-permute-start | bytes 196616 | tf_op jit(solution)/shard_map/ppermute | solution.py:37
  62.8 4.3 %collective-permute-start.26 = (bf16[256,128]{1,0:T(8,128)(2,1)S(1)}, bf16[256,128]{1,0:T(8,128)(2,1)S(1)}, u32[]{:S(2)}, u32[]{:S(2)}) collective-permute-start(bf16[256,128]{1,0:T(8,128)(2,1)S(1)} %collective-permute-done.24), channel_id=1, source_target_pairs={{0,2},{1,3},{2,0},{3,1},{4,6},{5,7},{6,4},{7,5},{8,10},{9,11},{10,... | collective-permute-start | bytes 196616 | tf_op jit(solution)/shard_map/ppermute | solution.py:37
  (15 other events, 119.3 us)

commit v4 on v3

--- a/solution.py
+++ b/solution.py
@@ -46,12 +46,12 @@
     return lax.optimization_barrier((*values, *others))[: len(values)]
 
 
-def call(kernel, outs, scratch, flops, moved, *args, smem=0):
+def call(kernel, outs, scratch, flops, moved, *args, smem=0, spec=VMEM):
     return pl.pallas_call(
         kernel,
         out_shape=outs,
         in_specs=[SMEM] * smem + [VMEM] * (len(args) - smem),
-        out_specs=jax.tree.map(lambda _: VMEM, outs),
+        out_specs=jax.tree.map(lambda _: spec, outs),
         scratch_shapes=scratch,
         compiler_params=pltpu.CompilerParams(vmem_limit_bytes=LIMIT),
         cost_estimate=pl.CostEstimate(flops=flops, bytes_accessed=moved, transcendentals=0),
@@ -119,35 +119,39 @@
     return half + away * owned + inner
 
 
-def pull_slots(shape, row, col, live, place, tiles, half, acc):
-    slots = tiles.shape[0]
-    blocks = acc.shape[0] - 1
+def list_slots(shape, rows, row, col, live, place, slots):
+    def step(k, carry):
+        block = block_slot(place, col, k, shape)
+        alive = live[0, k] == 1
+        slots[0, k] = block
+        slots[1, k] = jnp.where(alive, block, CORES * shape[0] * shape[1])
+        slots[2, k] = row[0, k]
+        slots[3, k] = jnp.where(alive, row[0, k], rows)
+        return carry
+
+    lax.fori_loop(0, slots.shape[1], step, 0)
+
+
+def pull_slots(slots, tiles, half, acc):
     acc[...] = jnp.zeros_like(acc)
 
     def step(k, carry):
-        there = jnp.where(live[0, k] == 1, block_slot(place, col, k, shape), blocks)
-        acc[there] += lax.dot_general(
-            tiles[k], half[row[0, k]], (((0,), (0,)), ((), ())), preferred_element_type=F32
+        acc[slots[1, k]] += lax.dot_general(
+            tiles[k], half[slots[2, k]], (((0,), (0,)), ((), ())), preferred_element_type=F32
         )
         return carry
 
-    lax.fori_loop(0, slots, step, 0, unroll=8)
-
-
-def push_slots(shape, row, col, live, place, tiles, blocks, acc):
-    slots = tiles.shape[0]
-    spare = acc.shape[0] - 1
-
+    lax.fori_loop(0, tiles.shape[0], step, 0, unroll=min(32, tiles.shape[0]))
+
+
+def push_slots(slots, tiles, blocks, acc):
     def step(k, carry):
-        there = jnp.where(live[0, k] == 1, row[0, k], spare)
-        acc[there] += jnp.dot(
-            tiles[k],
-            blocks[block_slot(place, col, k, shape)],
-            preferred_element_type=F32,
+        acc[slots[3, k]] += jnp.dot(
+            tiles[k], blocks[slots[0, k]], preferred_element_type=F32
         )
         return carry
 
-    lax.fori_loop(0, slots, step, 0, unroll=8)
+    lax.fori_loop(0, tiles.shape[0], step, 0, unroll=min(32, tiles.shape[0]))
 
 
 def give_partials(acc, keep, send):
@@ -156,17 +160,21 @@
     send[...] = acc[n : 2 * n].astype(BF)
 
 
-def pull_kernel(shape, row, col, live, place, tiles, duals, keep, send, *scratch):
-    half, acc = scratch if len(scratch) == 2 else (duals, scratch[0])
-    if len(scratch) == 2:
-        half[...] = duals[...].astype(BF)
-    pull_slots(shape, row, col, live, place, tiles, half, acc)
+def first_pull_kernel(shape, row, col, live, place, tiles, duals, keep, send, slots, half, acc):
+    list_slots(shape, duals.shape[0], row, col, live, place, slots)
+    half[...] = duals[...].astype(BF)
+    pull_slots(slots, tiles, half, acc)
     give_partials(acc, keep, send)
 
 
-def step_duals(shape, parts, size, refs, blocks, acc):
-    row, col, live, place, tiles, duals, demand, near, far = refs[:9]
-    combined = refs[9:]
+def pull_kernel(slots, tiles, half, keep, send, acc):
+    pull_slots(slots, tiles, half, acc)
+    give_partials(acc, keep, send)
+
+
+def step_duals(parts, size, refs, blocks, acc):
+    slots, tiles, duals, demand, near, far = refs[:6]
+    combined = refs[6:]
     n = near.shape[0]
     blocks[0:n] = near[...]
     blocks[n : 2 * n] = far[...]
@@ -179,14 +187,14 @@
             + (STEP_DUAL * 0.25) * demand[rows].astype(F32)
             - STEP_DUAL * combined[r][0:size].astype(F32).reshape(pieces, *duals.shape[1:])
         )
-    push_slots(shape, row, col, live, place, tiles, blocks, acc)
-
-
-def push_step_kernel(shape, parts, size, *refs):
-    ins, (next_duals, half), packets = refs[: 9 + parts], refs[9 + parts : 11 + parts], refs[11 + parts : -2]
-    blocks, acc = refs[-2:]
-    tile = ins[4].shape[1]
-    step_duals(shape, parts, size, ins, blocks, acc)
+    push_slots(slots, tiles, blocks, acc)
+
+
+def push_step_kernel(parts, size, *refs):
+    ins, next_duals, half = refs[: 6 + parts], refs[6 + parts], refs[7 + parts]
+    packets, blocks, acc = refs[8 + parts : -2], refs[-2], refs[-1]
+    tile = ins[1].shape[1]
+    step_duals(parts, size, ins, blocks, acc)
     n = next_duals.shape[0]
     next_duals[...] = acc[0:n]
     half[...] = acc[0:n].astype(BF)
@@ -202,11 +210,13 @@
         out[quarter_rows(r, parts, size), :] = refs[r][size:].astype(F32)
 
 
-def last_push_kernel(shape, parts, size, *refs):
-    ins = refs[: 9 + parts]
-    next_duals, blocks, acc = refs[9 + parts :]
-    step_duals(shape, parts, size, ins, blocks, acc)
-    next_duals[...] = acc[0 : next_duals.shape[0]]
+def last_push_kernel(parts, size, *refs):
+    ins = refs[: 6 + parts]
+    next_duals, blocks, acc, sem = refs[6 + parts :]
+    step_duals(parts, size, ins, blocks, acc)
+    copy = pltpu.make_async_copy(acc.at[pl.ds(0, next_duals.shape[0])], next_duals, sem)
+    copy.start()
+    copy.wait()
 
 
 def own_rows(size, tile, i):
@@ -299,7 +309,6 @@
     flows2 = flows.reshape(owned * tile, scenarios)
     duals3 = duals.reshape(band_tiles, tile, scenarios)
     demand3 = demand.reshape(band_tiles, tile, scenarios)
-    where = (tile_row, tile_col, tile_live, block_place)
     flops = 2 * slots * tile * tile * scenarios
     quarter = jax.ShapeDtypeStruct((size, scenarios), BF)
     quarter3 = jax.ShapeDtypeStruct((size // tile, tile, scenarios), BF)
@@ -392,41 +401,38 @@
         *packets,
     )
 
-    def pull(value, scratch):
-        keep, send = call(
-            functools.partial(pull_kernel, shape),
-            [half_blocks, half_blocks],
-            scratch,
-            flops,
-            2 * rows * scenarios + 2 * slots * tile * tile,
-            *where,
-            tiles,
-            value,
-            smem=4,
-        )
-        return keep, swap_core(send)
-
-    keep, send = apart(lambda value: pull(value, pull_scratch), duals3)
+    def first_pull(value):
+        keep, send, slots_of = pl.pallas_call(
+            functools.partial(first_pull_kernel, shape),
+            out_shape=[half_blocks, half_blocks, jax.ShapeDtypeStruct((4, slots), jnp.int32)],
+            in_specs=[SMEM] * 4 + [VMEM] * 2,
+            out_specs=[VMEM, VMEM, SMEM],
+            scratch_shapes=pull_scratch,
+            compiler_params=pltpu.CompilerParams(vmem_limit_bytes=LIMIT),
+        )(tile_row, tile_col, tile_live, block_place, tiles, value)
+        return keep, swap_core(send), slots_of
+
+    keep, send, slots_of = apart(first_pull, duals3)
     pulled = collect(keep, send, combined)
     flows1, bar1 = step_flows(flows2, pulled)
     combined = [combined[0]] + [rotate(combined[r], "section", -r) for r in range(1, parts)]
     near, far = spread(bar1, combined)
 
     duals1, half, *halves = call(
-        functools.partial(push_step_kernel, shape, parts, size),
+        functools.partial(push_step_kernel, parts, size),
         [jax.ShapeDtypeStruct((band_tiles, tile, scenarios), F32), whole_half]
         + [quarter3] * (parts - 1),
         push_scratch,
         flops,
         16 * rows * scenarios + 2 * slots * tile * tile,
-        *where,
+        slots_of,
         tiles,
         duals3,
         demand3,
         near,
         far,
         *combined,
-        smem=4,
+        smem=1,
     )
     halves = [rotate(halves[r - 1].reshape(size, scenarios), "section", r) for r in range(1, parts)]
     outs = call(
@@ -441,25 +447,37 @@
         stocks,
         *halves,
     )
-    keep, send = pull(half, pull_scratch[1:])
+    keep, send = call(
+        pull_kernel,
+        [half_blocks, half_blocks],
+        pull_scratch[1:],
+        flops,
+        2 * rows * scenarios + 2 * slots * tile * tile,
+        slots_of,
+        tiles,
+        half,
+        smem=1,
+    )
+    send = swap_core(send)
     pulled = collect(keep, send, outs)
     outs = [outs[0]] + [rotate(outs[r], "section", -r) for r in range(1, parts)]
     flows2_out, bar2 = step_flows(flows1, pulled)
     near, far = spread(bar2, outs)
     duals_out = call(
-        functools.partial(last_push_kernel, shape, parts, size),
+        functools.partial(last_push_kernel, parts, size),
         jax.ShapeDtypeStruct((band_tiles, tile, scenarios), F32),
-        push_scratch,
+        [*push_scratch, pltpu.SemaphoreType.DMA(())],
         flops,
         14 * rows * scenarios + 2 * slots * tile * tile,
-        *where,
+        slots_of,
         tiles,
         duals1,
         demand3,
         near,
         far,
         *outs,
-        smem=4,
+        smem=1,
+        spec=pl.BlockSpec(memory_space=pltpu.HBM),
     )
     stock_out = call(
         functools.partial(place_kernel, parts, size),

time: 76.5 us -> 75 us (0.980)
    pallas_call x7 -> x6, Pallas kernels: 11.9 us -> 7.9 us  [call(): pl.pallas_call(kernel, out_shape=outs, in_specs=[SMEM] * smem + [VMEM] *...]
    pallas_call x0 -> x1, Pallas kernels: none -> 3.25 us  [first_pull(): pl.pallas_call(functools.partial(first_pull_kernel, shape), out_shape=[ha...]
  transfers between devices with their start and end apart: 28 -> 28, of which waited for: 13 -> 13; matrix products, arithmetic and copies ran while one was open for 2% -> 2% of each run, Pallas kernels for 7% -> 8%
where the time goes in v4:
time: 75 us; the launch traced here: 74.8 us
  starting transfers between devices  40.5 us (54%)
  waiting for transfers between devices  18.3 us (24%)
  Pallas kernels  13.6 us (18%)
  other arithmetic  1.32 us (2%)
  between operations  0.96 us (1%)
    ppermute x12, starting transfers between devices, flip_chip(): lax.ppermute(value, 'zone', [(i, i ^ by * CORES) for i in range(size)])  23.9 us
    ppermute x12, starting transfers between devices, rotate(): lax.ppermute(value, axis, [(i, (i + by) % size) for i in range(size)])  16.2 us
    ppermute x12, waiting for transfers between devices, rotate(): lax.ppermute(value, axis, [(i, (i + by) % size) for i in range(size)])  7.93 us
    pallas_call x6, Pallas kernels, call(): pl.pallas_call(kernel, out_shape=outs, in_specs=[SMEM] * smem + [VMEM] *...  7.9 us
    ppermute x12, waiting for transfers between devices, flip_chip(): lax.ppermute(value, 'zone', [(i, i ^ by * CORES) for i in range(size)])  7.41 us
    pallas_call x1, Pallas kernels, first_pull(): pl.pallas_call(functools.partial(first_pull_kernel, shape), out_shape=[ha...  3.25 us
    ppermute x4, waiting for transfers between devices, swap_core(): return lax.ppermute(value, 'zone', [(i, i ^ 1) for i in range(size)])  3 us
    pallas_call x1, Pallas kernels, per_device(): pl.pallas_call(functools.partial(pack_kernel, parts, size), out_shape=pac...  2.42 us
  transfers between devices with their start and end apart: 28, of which 13 were waited for; matrix products, arithmetic and copies ran while one was open for 2% of the time, Pallas kernels for 8%

profile of v4, /device:TPU:0, one launch (start us, length us, event | category | flops | bytes accessed | tf_op | source)
XLA Modules:
  0.0 74.8 jit_solution(17878512400487526212)
XLA Ops:
  0.7 2.4 %shard_map.136 = (bf16[1296,128]{1,0:T(8,128)(2,1)}, bf16[1296,128]{1,0:T(8,128)(2,1)}, bf16[1296,128]{1,0:T(8,128)(2,1)}) custom-call(f32[2560,128]{1,0:T(8,128)} %bitcast.87, f32[2560,128]{1,0:T(8,128)} %bitcast.75, f32[1,2560]{1,0:T(1,128)} %refs_1_.1), custom_call_target="tpu_custom_call" | custom-call | bytes 3932160 | tf_op jit(solution)/shard_map/pallas_call | solution.py:369
  3.1 3.0 %collective-permute-start.4 = (bf16[1296,128]{1,0:T(8,128)(2,1)}, bf16[1296,128]{1,0:T(8,128)(2,1)S(1)}, u32[]{:S(2)}, u32[]{:S(2)}) collective-permute-start(bf16[1296,128]{1,0:T(8,128)(2,1)} %get-tuple-element.62), channel_id=1, source_target_pairs={{0,8},{8,16},{16,24},{24,0},{1,9},{9,17},{17,25},{25,1},{2,10},{10... | collective-permute-start | bytes 995336 | tf_op jit(solution)/shard_map/ppermute | solution.py:27
  6.1 1.5 %collective-permute-start.5 = (bf16[1296,128]{1,0:T(8,128)(2,1)}, bf16[1296,128]{1,0:T(8,128)(2,1)S(1)}, u32[]{:S(2)}, u32[]{:S(2)}) collective-permute-start(bf16[1296,128]{1,0:T(8,128)(2,1)} %get-tuple-element.63), channel_id=1, source_target_pairs={{0,16},{8,24},{16,0},{24,8},{1,17},{9,25},{17,1},{25,9},{2,18},{10... | collective-permute-start | bytes 995336 | tf_op jit(solution)/shard_map/ppermute | solution.py:27
  9.1 4.9 %conditional.1 = (s32[4,32]{1,0:T(4,128)S(1)}, f32[8,128,128]{2,1,0:T(8,128)S(1)}, f32[8,128,128]{2,1,0:T(8,128)S(1)}) conditional(s32[]{:T(128)} %bitcast.1, () %tuple.24, (s32[1,32]{1,0:T(1,128)S(1)}, s32[1,32]{1,0:T(1,128)S(1)}, s32[1,32]{1,0:T(1,128)S(1)}, s32[16]{0:T(128)S(1)}, bf16[32,128,128]{2,1,0:T(8,128)(2,1)}, ...), branch_computations={%region_0.0_spmd, %region_1.0_spmd} | conditional | flops 262144 | bytes 2621504 | solution.py:334
  9.2 3.2 %branch_1_fun.1 = (bf16[8,128,128]{2,1,0:T(8,128)(2,1)S(1)}, bf16[8,128,128]{2,1,0:T(8,128)(2,1)S(1)}, s32[4,32]{1,0:T(4,128)S(1)}) custom-call(s32[1,32]{1,0:T(1,128)S(1)} %get-tuple-element.97.row, s32[1,32]{1,0:T(1,128)S(1)} %get-tuple-element.98.col, s32[1,32]{1,0:T(1,128)S(1)} %get-tuple-element.99.live, s32[16]{0:T(128)S(1)} %get-tuple-element.17.place, ...), custom_call_target="tpu_custom_call" | custom-call | tf_op jit(solution)/shard_map/cond/branch_1_fun/pallas_call | solution.py:405
  14.2 3.7 %collective-permute-start.3 = (bf16[2,128,128]{2,1,0:T(8,128)(2,1)S(1)}, bf16[2,128,128]{2,1,0:T(8,128)(2,1)S(1)}, u32[]{:S(2)}, u32[]{:S(2)}) collective-permute-start(bf16[2,128,128]{2,1,0:T(8,128)(2,1)S(1)} %get-tuple-element.103), channel_id=1, source_target_pairs={{0,6},{1,7},{2,4},{3,5},{4,2},{5,3},{6,0},{7,1},{8,14},{9,15},{10,... | collective-permute-start | bytes 196616 | tf_op jit(solution)/shard_map/ppermute | solution.py:37
  19.0 3.1 %collective-permute-done.5.refs_4_.refs_3_ = bf16[1296,128]{1,0:T(8,128)(2,1)S(1)} collective-permute-done((bf16[1296,128]{1,0:T(8,128)(2,1)}, bf16[1296,128]{1,0:T(8,128)(2,1)S(1)}, u32[]{:S(2)}, u32[]{:S(2)}) %collective-permute-start.5) | collective-permute-done | bytes 331808 | tf_op jit(solution)/shard_map/ppermute | solution.py:27
  23.2 1.6 %collective-permute-start.10 = (bf16[640,128]{1,0:T(8,128)(2,1)S(1)}, bf16[640,128]{1,0:T(8,128)(2,1)S(1)}, u32[]{:S(2)}, u32[]{:S(2)}) collective-permute-start(bf16[640,128]{1,0:T(8,128)(2,1)S(1)} %get-tuple-element.66), channel_id=1, source_target_pairs={{0,24},{8,0},{16,8},{24,16},{1,25},{9,1},{17,9},{25,17},{2,26},{10... | collective-permute-start | bytes 491528 | tf_op jit(solution)/shard_map/ppermute | solution.py:27
  24.8 1.6 %collective-permute-start.11 = (bf16[640,128]{1,0:T(8,128)(2,1)S(1)}, bf16[640,128]{1,0:T(8,128)(2,1)S(1)}, u32[]{:S(2)}, u32[]{:S(2)}) collective-permute-start(bf16[640,128]{1,0:T(8,128)(2,1)S(1)} %get-tuple-element.67), channel_id=1, source_target_pairs={{0,16},{8,24},{16,0},{24,8},{1,17},{9,25},{17,1},{25,9},{2,18},{10... | collective-permute-start | bytes 491528 | tf_op jit(solution)/shard_map/ppermute | solution.py:27
  26.9 2.7 %collective-permute-start.7 = (bf16[256,128]{1,0:T(8,128)(2,1)S(1)}, bf16[256,128]{1,0:T(8,128)(2,1)S(1)}, u32[]{:S(2)}, u32[]{:S(2)}) collective-permute-start(bf16[256,128]{1,0:T(8,128)(2,1)S(1)} %fusion.16), channel_id=1, source_target_pairs={{0,4},{1,5},{2,6},{3,7},{4,0},{5,1},{6,2},{7,3},{8,12},{9,13},{10,... | collective-permute-start | bytes 196616 | tf_op jit(solution)/shard_map/ppermute | solution.py:37
  29.5 1.6 %collective-permute-start.8 = (bf16[256,128]{1,0:T(8,128)(2,1)S(1)}, bf16[256,128]{1,0:T(8,128)(2,1)S(1)}, u32[]{:S(2)}, u32[]{:S(2)}) collective-permute-start(bf16[256,128]{1,0:T(8,128)(2,1)S(1)} %fusion.16), channel_id=1, source_target_pairs={{0,2},{1,3},{2,0},{3,1},{4,6},{5,7},{6,4},{7,5},{8,10},{9,11},{10,... | collective-permute-start | bytes 196616 | tf_op jit(solution)/shard_map/ppermute | solution.py:37
  34.1 2.3 %collective-permute-done.9 = bf16[256,128]{1,0:T(8,128)(2,1)S(1)} collective-permute-done((bf16[256,128]{1,0:T(8,128)(2,1)S(1)}, bf16[256,128]{1,0:T(8,128)(2,1)S(1)}, u32[]{:S(2)}, u32[]{:S(2)}) %collective-permute-start.9) | collective-permute-done | bytes 65568 | tf_op jit(solution)/shard_map/ppermute | solution.py:37
  36.6 1.5 %collective-permute-done.13.refs_5_ = bf16[8,128,128]{2,1,0:T(8,128)(2,1)S(1)} collective-permute-done((bf16[8,128,128]{2,1,0:T(8,128)(2,1)S(1)}, bf16[8,128,128]{2,1,0:T(8,128)(2,1)S(1)}, u32[]{:S(2)}, u32[]{:S(2)}) %collective-permute-start.13) | collective-permute-done | bytes 262176 | tf_op jit(solution)/shard_map/ppermute | solution.py:42
  38.1 1.7 %shard_map.138 = (f32[20,128,128]{2,1,0:T(8,128)S(1)}, bf16[20,128,128]{2,1,0:T(8,128)(2,1)S(1)}, bf16[5,128,128]{2,1,0:T(8,128)(2,1)S(1)}, bf16[5,128,128]{2,1,0:T(8,128)(2,1)S(1)}, bf16[5,128,128]{2,1,0:T(8,128)(2,1)S(1)}) custom-call(s32[4,32]{1,0:T(4,128)S(1)} %get-tuple-element.72.refs_0_.slots, bf16[32,128,128]{2,1,0:T(8,128)(2,1)S(1)} %bitcast.92, ...), custom_call_target="tpu_custom_call" | custom-call | flops 134217728 | bytes 6291456 | tf_op jit(solution)/shard_map/pallas_call | solution.py:50
  42.7 1.6 %collective-permute-start.19 = (bf16[640,128]{1,0:T(8,128)(2,1)S(1)}, bf16[640,128]{1,0:T(8,128)(2,1)S(1)}, u32[]{:S(2)}, u32[]{:S(2)}) collective-permute-start(bf16[640,128]{1,0:T(8,128)(2,1)S(1)} %bitcast.85), channel_id=1, source_target_pairs={{0,16},{8,24},{16,0},{24,8},{1,17},{9,25},{17,1},{25,9},{2,18},{10... | collective-permute-start | bytes 491528 | tf_op jit(solution)/shard_map/ppermute | solution.py:27
  44.8 4.2 %collective-permute-start.17 = (bf16[2,128,128]{2,1,0:T(8,128)(2,1)S(1)}, bf16[2,128,128]{2,1,0:T(8,128)(2,1)S(1)}, u32[]{:S(2)}, u32[]{:S(2)}) collective-permute-start(bf16[2,128,128]{2,1,0:T(8,128)(2,1)S(1)} %get-tuple-element.100), channel_id=1, source_target_pairs={{0,6},{1,7},{2,4},{3,5},{4,2},{5,3},{6,0},{7,1},{8,14},{9,15},{10,... | collective-permute-start | bytes 196616 | tf_op jit(solution)/shard_map/ppermute | solution.py:37
  49.2 2.7 %collective-permute-start.15 = (bf16[2,128,128]{2,1,0:T(8,128)(2,1)S(1)}, bf16[2,128,128]{2,1,0:T(8,128)(2,1)S(1)}, u32[]{:S(2)}, u32[]{:S(2)}) collective-permute-start(bf16[2,128,128]{2,1,0:T(8,128)(2,1)S(1)} %get-tuple-element.102), channel_id=1, source_target_pairs={{0,4},{1,5},{2,6},{3,7},{4,0},{5,1},{6,2},{7,3},{8,12},{9,13},{10,... | collective-permute-start | bytes 196616 | tf_op jit(solution)/shard_map/ppermute | solution.py:37
  52.7 1.8 %collective-permute-start.21 = (bf16[1280,128]{1,0:T(8,128)(2,1)S(1)}, bf16[1280,128]{1,0:T(8,128)(2,1)S(1)}, u32[]{:S(2)}, u32[]{:S(2)}) collective-permute-start(bf16[1280,128]{1,0:T(8,128)(2,1)S(1)} %get-tuple-element.85), channel_id=1, source_target_pairs={{0,24},{8,0},{16,8},{24,16},{1,25},{9,1},{17,9},{25,17},{2,26},{10... | collective-permute-start | bytes 983048 | tf_op jit(solution)/shard_map/ppermute | solution.py:27
  56.1 3.1 %collective-permute-start.24 = (bf16[256,128]{1,0:T(8,128)(2,1)S(1)}, bf16[256,128]{1,0:T(8,128)(2,1)S(1)}, u32[]{:S(2)}, u32[]{:S(2)}) collective-permute-start(bf16[256,128]{1,0:T(8,128)(2,1)S(1)} %fusion.17), channel_id=1, source_target_pairs={{0,4},{1,5},{2,6},{3,7},{4,0},{5,1},{6,2},{7,3},{8,12},{9,13},{10,... | collective-permute-start | bytes 196616 | tf_op jit(solution)/shard_map/ppermute | solution.py:37
  59.2 1.8 %collective-permute-start.25 = (bf16[256,128]{1,0:T(8,128)(2,1)S(1)}, bf16[256,128]{1,0:T(8,128)(2,1)S(1)}, u32[]{:S(2)}, u32[]{:S(2)}) collective-permute-start(bf16[256,128]{1,0:T(8,128)(2,1)S(1)} %fusion.17), channel_id=1, source_target_pairs={{0,2},{1,3},{2,0},{3,1},{4,6},{5,7},{6,4},{7,5},{8,10},{9,11},{10,... | collective-permute-start | bytes 196616 | tf_op jit(solution)/shard_map/ppermute | solution.py:37
  61.8 1.5 %collective-permute-start.26 = (bf16[256,128]{1,0:T(8,128)(2,1)S(1)}, bf16[256,128]{1,0:T(8,128)(2,1)S(1)}, u32[]{:S(2)}, u32[]{:S(2)}) collective-permute-start(bf16[256,128]{1,0:T(8,128)(2,1)S(1)} %collective-permute-done.24), channel_id=1, source_target_pairs={{0,2},{1,3},{2,0},{3,1},{4,6},{5,7},{6,4},{7,5},{8,10},{9,11},{10,... | collective-permute-start | bytes 196616 | tf_op jit(solution)/shard_map/ppermute | solution.py:37
  63.6 2.4 %collective-permute-done.26 = bf16[256,128]{1,0:T(8,128)(2,1)S(1)} collective-permute-done((bf16[256,128]{1,0:T(8,128)(2,1)S(1)}, bf16[256,128]{1,0:T(8,128)(2,1)S(1)}, u32[]{:S(2)}, u32[]{:S(2)}) %collective-permute-start.26) | collective-permute-done | bytes 65568 | tf_op jit(solution)/shard_map/ppermute | solution.py:37
  66.0 4.2 %collective-permute-done.22.refs_2_.refs_8_ = bf16[1280,128]{1,0:T(8,128)(2,1)S(1)} collective-permute-done((bf16[1280,128]{1,0:T(8,128)(2,1)S(1)}, bf16[1280,128]{1,0:T(8,128)(2,1)S(1)}, u32[]{:S(2)}, u32[]{:S(2)}) %collective-permute-start.22) | collective-permute-done | bytes 327712 | tf_op jit(solution)/shard_map/ppermute | solution.py:27
  72.2 2.6 %shard_map.142 = f32[20,128,128]{2,1,0:T(8,128)} custom-call(s32[4,32]{1,0:T(4,128)S(1)} %get-tuple-element.72.refs_0_.slots, bf16[32,128,128]{2,1,0:T(8,128)(2,1)S(1)} %bitcast.94, f32[20,128,128]{2,1,0:T(8,128)S(1)} %get-tuple-element.79.refs_2_, s32[20,128,128]{2,1,0:T(8,128)S(1)} %bitcast.79, bf16[8,128,128]{2,1,0:T(8,128)(2,1)S(1)} %bitcast.83, ...), custom_call_target="tpu_custom_call" | custom-call | flops 134217728 | bytes 5636096 | tf_op jit(solution)/shard_map/pallas_call | solution.py:50
  (76 shorter events, 17.8 us)
Async XLA Ops:
  3.1 14.7 %collective-permute-start.4 = (bf16[1296,128]{1,0:T(8,128)(2,1)}, bf16[1296,128]{1,0:T(8,128)(2,1)S(1)}, u32[]{:S(2)}, u32[]{:S(2)}) collective-permute-start(bf16[1296,128]{1,0:T(8,128)(2,1)} %get-tuple-element.62), channel_id=1, source_target_pairs={{0,8},{8,16},{16,24},{24,0},{1,9},{9,17},{17,25},{25,1},{2,10},{10... | collective-permute-start | bytes 995336 | tf_op jit(solution)/shard_map/ppermute | solution.py:27
  6.1 16.1 %collective-permute-start.5 = (bf16[1296,128]{1,0:T(8,128)(2,1)}, bf16[1296,128]{1,0:T(8,128)(2,1)S(1)}, u32[]{:S(2)}, u32[]{:S(2)}) collective-permute-start(bf16[1296,128]{1,0:T(8,128)(2,1)} %get-tuple-element.63), channel_id=1, source_target_pairs={{0,16},{8,24},{16,0},{24,8},{1,17},{9,25},{17,1},{25,9},{2,18},{10... | collective-permute-start | bytes 995336 | tf_op jit(solution)/shard_map/ppermute | solution.py:27
  7.6 14.8 %collective-permute-start.6 = (bf16[1296,128]{1,0:T(8,128)(2,1)}, bf16[1296,128]{1,0:T(8,128)(2,1)S(1)}, u32[]{:S(2)}, u32[]{:S(2)}) collective-permute-start(bf16[1296,128]{1,0:T(8,128)(2,1)} %get-tuple-element.64), channel_id=1, source_target_pairs={{0,24},{8,0},{16,8},{24,16},{1,25},{9,1},{17,9},{25,17},{2,26},{10... | collective-permute-start | bytes 995336 | tf_op jit(solution)/shard_map/ppermute | solution.py:27
  14.2 12.2 %collective-permute-start.3 = (bf16[2,128,128]{2,1,0:T(8,128)(2,1)S(1)}, bf16[2,128,128]{2,1,0:T(8,128)(2,1)S(1)}, u32[]{:S(2)}, u32[]{:S(2)}) collective-permute-start(bf16[2,128,128]{2,1,0:T(8,128)(2,1)S(1)} %get-tuple-element.103), channel_id=1, source_target_pairs={{0,6},{1,7},{2,4},{3,5},{4,2},{5,3},{6,0},{7,1},{8,14},{9,15},{10,... | collective-permute-start | bytes 196616 | tf_op jit(solution)/shard_map/ppermute | solution.py:37
  17.8 8.8 %collective-permute-start.2 = (bf16[2,128,128]{2,1,0:T(8,128)(2,1)S(1)}, bf16[2,128,128]{2,1,0:T(8,128)(2,1)S(1)}, u32[]{:S(2)}, u32[]{:S(2)}) collective-permute-start(bf16[2,128,128]{2,1,0:T(8,128)(2,1)S(1)} %get-tuple-element.104), channel_id=1, source_target_pairs={{0,2},{1,3},{2,0},{3,1},{4,6},{5,7},{6,4},{7,5},{8,10},{9,11},{10,... | collective-permute-start | bytes 196616 | tf_op jit(solution)/shard_map/ppermute | solution.py:37
  17.9 8.8 %collective-permute-start.1 = (bf16[2,128,128]{2,1,0:T(8,128)(2,1)S(1)}, bf16[2,128,128]{2,1,0:T(8,128)(2,1)S(1)}, u32[]{:S(2)}, u32[]{:S(2)}) collective-permute-start(bf16[2,128,128]{2,1,0:T(8,128)(2,1)S(1)} %get-tuple-element.105), channel_id=1, source_target_pairs={{0,4},{1,5},{2,6},{3,7},{4,0},{5,1},{6,2},{7,3},{8,12},{9,13},{10,... | collective-permute-start | bytes 196616 | tf_op jit(solution)/shard_map/ppermute | solution.py:37
  23.2 13.3 %collective-permute-start.10 = (bf16[640,128]{1,0:T(8,128)(2,1)S(1)}, bf16[640,128]{1,0:T(8,128)(2,1)S(1)}, u32[]{:S(2)}, u32[]{:S(2)}) collective-permute-start(bf16[640,128]{1,0:T(8,128)(2,1)S(1)} %get-tuple-element.66), channel_id=1, source_target_pairs={{0,24},{8,0},{16,8},{24,16},{1,25},{9,1},{17,9},{25,17},{2,26},{10... | collective-permute-start | bytes 491528 | tf_op jit(solution)/shard_map/ppermute | solution.py:27
  24.8 11.7 %collective-permute-start.11 = (bf16[640,128]{1,0:T(8,128)(2,1)S(1)}, bf16[640,128]{1,0:T(8,128)(2,1)S(1)}, u32[]{:S(2)}, u32[]{:S(2)}) collective-permute-start(bf16[640,128]{1,0:T(8,128)(2,1)S(1)} %get-tuple-element.67), channel_id=1, source_target_pairs={{0,16},{8,24},{16,0},{24,8},{1,17},{9,25},{17,1},{25,9},{2,18},{10... | collective-permute-start | bytes 491528 | tf_op jit(solution)/shard_map/ppermute | solution.py:27
  26.4 10.1 %collective-permute-start.12 = (bf16[640,128]{1,0:T(8,128)(2,1)S(1)}, bf16[640,128]{1,0:T(8,128)(2,1)S(1)}, u32[]{:S(2)}, u32[]{:S(2)}) collective-permute-start(bf16[640,128]{1,0:T(8,128)(2,1)S(1)} %get-tuple-element.68), channel_id=1, source_target_pairs={{0,8},{8,16},{16,24},{24,0},{1,9},{9,17},{17,25},{25,1},{2,10},{10... | collective-permute-start | bytes 491528 | tf_op jit(solution)/shard_map/ppermute | solution.py:27
  26.9 5.3 %collective-permute-start.7 = (bf16[256,128]{1,0:T(8,128)(2,1)S(1)}, bf16[256,128]{1,0:T(8,128)(2,1)S(1)}, u32[]{:S(2)}, u32[]{:S(2)}) collective-permute-start(bf16[256,128]{1,0:T(8,128)(2,1)S(1)} %fusion.16), channel_id=1, source_target_pairs={{0,4},{1,5},{2,6},{3,7},{4,0},{5,1},{6,2},{7,3},{8,12},{9,13},{10,... | collective-permute-start | bytes 196616 | tf_op jit(solution)/shard_map/ppermute | solution.py:37
  29.5 4.6 %collective-permute-start.8 = (bf16[256,128]{1,0:T(8,128)(2,1)S(1)}, bf16[256,128]{1,0:T(8,128)(2,1)S(1)}, u32[]{:S(2)}, u32[]{:S(2)}) collective-permute-start(bf16[256,128]{1,0:T(8,128)(2,1)S(1)} %fusion.16), channel_id=1, source_target_pairs={{0,2},{1,3},{2,0},{3,1},{4,6},{5,7},{6,4},{7,5},{8,10},{9,11},{10,... | collective-permute-start | bytes 196616 | tf_op jit(solution)/shard_map/ppermute | solution.py:37
  32.2 4.3 %collective-permute-start.9 = (bf16[256,128]{1,0:T(8,128)(2,1)S(1)}, bf16[256,128]{1,0:T(8,128)(2,1)S(1)}, u32[]{:S(2)}, u32[]{:S(2)}) collective-permute-start(bf16[256,128]{1,0:T(8,128)(2,1)S(1)} %collective-permute-done.7), channel_id=1, source_target_pairs={{0,2},{1,3},{2,0},{3,1},{4,6},{5,7},{6,4},{7,5},{8,10},{9,11},{10,... | collective-permute-start | bytes 196616 | tf_op jit(solution)/shard_map/ppermute | solution.py:37
  41.2 8.0 %collective-permute-start.18 = (bf16[640,128]{1,0:T(8,128)(2,1)S(1)}, bf16[640,128]{1,0:T(8,128)(2,1)S(1)}, u32[]{:S(2)}, u32[]{:S(2)}) collective-permute-start(bf16[640,128]{1,0:T(8,128)(2,1)S(1)} %bitcast.86), channel_id=1, source_target_pairs={{0,8},{8,16},{16,24},{24,0},{1,9},{9,17},{17,25},{25,1},{2,10},{10... | collective-permute-start | bytes 491528 | tf_op jit(solution)/shard_map/ppermute | solution.py:27
  42.7 9.4 %collective-permute-start.19 = (bf16[640,128]{1,0:T(8,128)(2,1)S(1)}, bf16[640,128]{1,0:T(8,128)(2,1)S(1)}, u32[]{:S(2)}, u32[]{:S(2)}) collective-permute-start(bf16[640,128]{1,0:T(8,128)(2,1)S(1)} %bitcast.85), channel_id=1, source_target_pairs={{0,16},{8,24},{16,0},{24,8},{1,17},{9,25},{17,1},{25,9},{2,18},{10... | collective-permute-start | bytes 491528 | tf_op jit(solution)/shard_map/ppermute | solution.py:27
  44.3 7.7 %collective-permute-start.20 = (bf16[640,128]{1,0:T(8,128)(2,1)S(1)}, bf16[640,128]{1,0:T(8,128)(2,1)S(1)}, u32[]{:S(2)}, u32[]{:S(2)}) collective-permute-start(bf16[640,128]{1,0:T(8,128)(2,1)S(1)} %bitcast.84), channel_id=1, source_target_pairs={{0,24},{8,0},{16,8},{24,16},{1,25},{9,1},{17,9},{25,17},{2,26},{10... | collective-permute-start | bytes 491528 | tf_op jit(solution)/shard_map/ppermute | solution.py:27
  44.8 11.1 %collective-permute-start.17 = (bf16[2,128,128]{2,1,0:T(8,128)(2,1)S(1)}, bf16[2,128,128]{2,1,0:T(8,128)(2,1)S(1)}, u32[]{:S(2)}, u32[]{:S(2)}) collective-permute-start(bf16[2,128,128]{2,1,0:T(8,128)(2,1)S(1)} %get-tuple-element.100), channel_id=1, source_target_pairs={{0,6},{1,7},{2,4},{3,5},{4,2},{5,3},{6,0},{7,1},{8,14},{9,15},{10,... | collective-permute-start | bytes 196616 | tf_op jit(solution)/shard_map/ppermute | solution.py:37
  49.0 6.9 %collective-permute-start.16 = (bf16[2,128,128]{2,1,0:T(8,128)(2,1)S(1)}, bf16[2,128,128]{2,1,0:T(8,128)(2,1)S(1)}, u32[]{:S(2)}, u32[]{:S(2)}) collective-permute-start(bf16[2,128,128]{2,1,0:T(8,128)(2,1)S(1)} %get-tuple-element.101), channel_id=1, source_target_pairs={{0,2},{1,3},{2,0},{3,1},{4,6},{5,7},{6,4},{7,5},{8,10},{9,11},{10,... | collective-permute-start | bytes 196616 | tf_op jit(solution)/shard_map/ppermute | solution.py:37
  49.2 6.8 %collective-permute-start.15 = (bf16[2,128,128]{2,1,0:T(8,128)(2,1)S(1)}, bf16[2,128,128]{2,1,0:T(8,128)(2,1)S(1)}, u32[]{:S(2)}, u32[]{:S(2)}) collective-permute-start(bf16[2,128,128]{2,1,0:T(8,128)(2,1)S(1)} %get-tuple-element.102), channel_id=1, source_target_pairs={{0,4},{1,5},{2,6},{3,7},{4,0},{5,1},{6,2},{7,3},{8,12},{9,13},{10,... | collective-permute-start | bytes 196616 | tf_op jit(solution)/shard_map/ppermute | solution.py:37
  52.7 13.3 %collective-permute-start.21 = (bf16[1280,128]{1,0:T(8,128)(2,1)S(1)}, bf16[1280,128]{1,0:T(8,128)(2,1)S(1)}, u32[]{:S(2)}, u32[]{:S(2)}) collective-permute-start(bf16[1280,128]{1,0:T(8,128)(2,1)S(1)} %get-tuple-element.85), channel_id=1, source_target_pairs={{0,24},{8,0},{16,8},{24,16},{1,25},{9,1},{17,9},{25,17},{2,26},{10... | collective-permute-start | bytes 983048 | tf_op jit(solution)/shard_map/ppermute | solution.py:27
  54.5 15.7 %collective-permute-start.22 = (bf16[1280,128]{1,0:T(8,128)(2,1)S(1)}, bf16[1280,128]{1,0:T(8,128)(2,1)S(1)}, u32[]{:S(2)}, u32[]{:S(2)}) collective-permute-start(bf16[1280,128]{1,0:T(8,128)(2,1)S(1)} %get-tuple-element.86), channel_id=1, source_target_pairs={{0,16},{8,24},{16,0},{24,8},{1,17},{9,25},{17,1},{25,9},{2,18},{10... | collective-permute-start | bytes 983048 | tf_op jit(solution)/shard_map/ppermute | solution.py:27
  55.9 14.3 %collective-permute-start.23 = (bf16[1280,128]{1,0:T(8,128)(2,1)S(1)}, bf16[1280,128]{1,0:T(8,128)(2,1)S(1)}, u32[]{:S(2)}, u32[]{:S(2)}) collective-permute-start(bf16[1280,128]{1,0:T(8,128)(2,1)S(1)} %get-tuple-element.87), channel_id=1, source_target_pairs={{0,8},{8,16},{16,24},{24,0},{1,9},{9,17},{17,25},{25,1},{2,10},{10... | collective-permute-start | bytes 983048 | tf_op jit(solution)/shard_map/ppermute | solution.py:27
  56.1 5.7 %collective-permute-start.24 = (bf16[256,128]{1,0:T(8,128)(2,1)S(1)}, bf16[256,128]{1,0:T(8,128)(2,1)S(1)}, u32[]{:S(2)}, u32[]{:S(2)}) collective-permute-start(bf16[256,128]{1,0:T(8,128)(2,1)S(1)} %fusion.17), channel_id=1, source_target_pairs={{0,4},{1,5},{2,6},{3,7},{4,0},{5,1},{6,2},{7,3},{8,12},{9,13},{10,... | collective-permute-start | bytes 196616 | tf_op jit(solution)/shard_map/ppermute | solution.py:37
  59.2 4.4 %collective-permute-start.25 = (bf16[256,128]{1,0:T(8,128)(2,1)S(1)}, bf16[256,128]{1,0:T(8,128)(2,1)S(1)}, u32[]{:S(2)}, u32[]{:S(2)}) collective-permute-start(bf16[256,128]{1,0:T(8,128)(2,1)S(1)} %fusion.17), channel_id=1, source_target_pairs={{0,2},{1,3},{2,0},{3,1},{4,6},{5,7},{6,4},{7,5},{8,10},{9,11},{10,... | collective-permute-start | bytes 196616 | tf_op jit(solution)/shard_map/ppermute | solution.py:37
  61.8 4.3 %collective-permute-start.26 = (bf16[256,128]{1,0:T(8,128)(2,1)S(1)}, bf16[256,128]{1,0:T(8,128)(2,1)S(1)}, u32[]{:S(2)}, u32[]{:S(2)}) collective-permute-start(bf16[256,128]{1,0:T(8,128)(2,1)S(1)} %collective-permute-done.24), channel_id=1, source_target_pairs={{0,2},{1,3},{2,0},{3,1},{4,6},{5,7},{6,4},{7,5},{8,10},{9,11},{10,... | collective-permute-start | bytes 196616 | tf_op jit(solution)/shard_map/ppermute | solution.py:37
  (15 other events, 116.4 us)

commit v5 on v4

--- a/solution.py
+++ b/solution.py
@@ -210,13 +210,31 @@
         out[quarter_rows(r, parts, size), :] = refs[r][size:].astype(F32)
 
 
-def last_push_kernel(parts, size, *refs):
-    ins = refs[: 6 + parts]
-    next_duals, blocks, acc, sem = refs[6 + parts :]
-    step_duals(parts, size, ins, blocks, acc)
-    copy = pltpu.make_async_copy(acc.at[pl.ds(0, next_duals.shape[0])], next_duals, sem)
-    copy.start()
-    copy.wait()
+def push_kernel(slots, tiles, duals, demand, *refs):
+    parts_of, (base, blocks, acc) = refs[:-3], refs[-3:]
+    first = 0
+    for part in parts_of:
+        blocks[first : first + part.shape[0]] = part[...]
+        first += part.shape[0]
+    n = base.shape[0]
+    acc[0:n] = duals[...] + (STEP_DUAL * 0.25) * demand[...].astype(F32)
+    push_slots(slots, tiles, blocks, acc)
+    base[...] = acc[0:n]
+
+
+def final_kernel(parts, size, *refs):
+    base, outs, (duals_out, stock_out) = refs[0], refs[1 : 1 + parts], refs[1 + parts : 3 + parts]
+    duals, stock, sems = refs[3 + parts :]
+    copies = []
+    for r in range(parts):
+        rows = quarter_rows(r, parts, size)
+        duals[rows, :] = base[rows, :] - STEP_DUAL * outs[r][0:size].astype(F32)
+        stock[rows, :] = outs[r][size:].astype(F32)
+        for i, (held, out) in enumerate(((duals, duals_out), (stock, stock_out))):
+            copies.append(pltpu.make_async_copy(held.at[rows], out.at[rows], sems.at[2 * r + i]))
+            copies[-1].start()
+    for copy in copies:
+        copy.wait()
 
 
 def own_rows(size, tile, i):
@@ -349,16 +367,22 @@
             total = total + value.astype(F32)
         return total.reshape(owned * tile, scenarios)
 
-    def spread(value, others):
+    def spread(value, others, early=0, pieces=1):
         own = [value]
         step = chips // 2
         while step:
-            own = own + [flip_chip(v, step) for v in own]
+            if early and step == 1:
+                first = flip_chip(value[:early], step)
+                rest = flip_chip(jnp.concatenate([value[early:], *own[1:]], axis=0), step)
+                own = own + [first, rest]
+            else:
+                own = own + [flip_chip(v, step) for v in own]
             step //= 2
         own = own[1:]
         own = after(own, others)
         near = jnp.concatenate([value, *own], axis=0).reshape(blocks // 2, tile, scenarios)
-        return near, swap_core(near)
+        piece = near.shape[0] // pieces
+        return near, *(swap_core(near[i * piece : (i + 1) * piece]) for i in range(pieces))
 
     def step_flows(now, pulled):
         new = jnp.maximum(now - STEP_PRIMAL * (flow_cost[0][:, None] - pulled), 0.0)
@@ -416,7 +440,7 @@
     pulled = collect(keep, send, combined)
     flows1, bar1 = step_flows(flows2, pulled)
     combined = [combined[0]] + [rotate(combined[r], "section", -r) for r in range(1, parts)]
-    near, far = spread(bar1, combined)
+    near, far = spread(bar1, combined, tile // 2)
 
     duals1, half, *halves = call(
         functools.partial(push_step_kernel, parts, size),
@@ -462,31 +486,35 @@
     pulled = collect(keep, send, outs)
     outs = [outs[0]] + [rotate(outs[r], "section", -r) for r in range(1, parts)]
     flows2_out, bar2 = step_flows(flows1, pulled)
-    near, far = spread(bar2, outs)
-    duals_out = call(
-        functools.partial(last_push_kernel, parts, size),
+    bar2, flows2_out = lax.optimization_barrier((bar2, flows2_out))
+    near, *far = spread(bar2, [], pieces=4)
+    base = call(
+        push_kernel,
         jax.ShapeDtypeStruct((band_tiles, tile, scenarios), F32),
-        [*push_scratch, pltpu.SemaphoreType.DMA(())],
-        flops,
-        14 * rows * scenarios + 2 * slots * tile * tile,
+        push_scratch,
+        0,
+        0,
         slots_of,
         tiles,
         duals1,
         demand3,
         near,
-        far,
-        *outs,
+        *far,
         smem=1,
-        spec=pl.BlockSpec(memory_space=pltpu.HBM),
-    )
-    stock_out = call(
-        functools.partial(place_kernel, parts, size),
-        jax.ShapeDtypeStruct((rows, scenarios), F32),
-        [],
-        0,
-        6 * rows * scenarios,
-        *outs,
-    )
+    )
+    whole = jax.ShapeDtypeStruct((rows, scenarios), F32)
+    duals_out, stock_out = pl.pallas_call(
+        functools.partial(final_kernel, parts, size),
+        out_shape=[whole, whole],
+        in_specs=[VMEM] * (parts + 1),
+        out_specs=[pl.BlockSpec(memory_space=pltpu.HBM)] * 2,
+        scratch_shapes=[pltpu.VMEM((rows, scenarios), F32)] * 2
+        + [pltpu.SemaphoreType.DMA((2 * parts,))],
+        compiler_params=pltpu.CompilerParams(vmem_limit_bytes=LIMIT),
+        cost_estimate=pl.CostEstimate(
+            flops=0, bytes_accessed=12 * rows * scenarios, transcendentals=0
+        ),
+    )(base.reshape(rows, scenarios), *outs)
     return (
         flows2_out.reshape(flows.shape),
         stock_out.reshape(stock.shape),

time: 75 us -> 72 us (0.960)
  starting transfers between devices: 40.5 us -> 34.9 us
  waiting for transfers between devices: 18.3 us -> 21.5 us
    ppermute x12, starting transfers between devices: 23.9 us -> 17.2 us  [flip_chip(): lax.ppermute(value, 'zone', [(i, i ^ by * CORES) for i in range(size)])]
    pallas_call x6 -> x5, Pallas kernels: 7.9 us -> 5.74 us  [call(): pl.pallas_call(kernel, out_shape=outs, in_specs=[SMEM] * smem + [VMEM] *...]
    ppermute x4 -> x7, waiting for transfers between devices: 3 us -> 4.81 us  [swap_core(): return lax.ppermute(value, 'zone', [(i, i ^ 1) for i in range(size)])]
    pallas_call x0 -> x1, Pallas kernels: none -> 1.59 us  [per_device(): pl.pallas_call(functools.partial(final_kernel, parts, size), out_shape=[w...]
    ppermute x12, waiting for transfers between devices: 7.41 us -> 8.78 us  [flip_chip(): lax.ppermute(value, 'zone', [(i, i ^ by * CORES) for i in range(size)])]
  transfers between devices with their start and end apart: 28 -> 31, of which waited for: 13 -> 14; matrix products, arithmetic and copies ran while one was open for 2% -> 2% of each run, Pallas kernels for 8% -> 8%
where the time goes in v5:
time: 72 us; the launch traced here: 71.8 us
  starting transfers between devices  34.9 us (48%)
  waiting for transfers between devices  21.5 us (30%)
  Pallas kernels  13 us (18%)
  other arithmetic  1.33 us (2%)
  between operations  1 us (1%)
    ppermute x12, starting transfers between devices, flip_chip(): lax.ppermute(value, 'zone', [(i, i ^ by * CORES) for i in range(size)])  17.2 us
    ppermute x12, starting transfers between devices, rotate(): lax.ppermute(value, axis, [(i, (i + by) % size) for i in range(size)])  16.7 us
    ppermute x12, waiting for transfers between devices, flip_chip(): lax.ppermute(value, 'zone', [(i, i ^ by * CORES) for i in range(size)])  8.78 us
    ppermute x12, waiting for transfers between devices, rotate(): lax.ppermute(value, axis, [(i, (i + by) % size) for i in range(size)])  7.95 us
    pallas_call x5, Pallas kernels, call(): pl.pallas_call(kernel, out_shape=outs, in_specs=[SMEM] * smem + [VMEM] *...  5.74 us
    ppermute x7, waiting for transfers between devices, swap_core(): return lax.ppermute(value, 'zone', [(i, i ^ 1) for i in range(size)])  4.81 us
    pallas_call x1, Pallas kernels, first_pull(): pl.pallas_call(functools.partial(first_pull_kernel, shape), out_shape=[ha...  3.24 us
    pallas_call x1, Pallas kernels, per_device(): pl.pallas_call(functools.partial(pack_kernel, parts, size), out_shape=pac...  2.41 us
  transfers between devices with their start and end apart: 31, of which 14 were waited for; matrix products, arithmetic and copies ran while one was open for 2% of the time, Pallas kernels for 8%

profile of v5, /device:TPU:0, one launch (start us, length us, event | category | flops | bytes accessed | tf_op | source)
XLA Modules:
  0.0 71.8 jit_solution(6815819635446537585)
XLA Ops:
  0.7 2.4 %shard_map.133 = (bf16[1296,128]{1,0:T(8,128)(2,1)}, bf16[1296,128]{1,0:T(8,128)(2,1)}, bf16[1296,128]{1,0:T(8,128)(2,1)}) custom-call(f32[2560,128]{1,0:T(8,128)} %bitcast.75, f32[2560,128]{1,0:T(8,128)} %bitcast.65, f32[1,2560]{1,0:T(1,128)} %refs_1_.1), custom_call_target="tpu_custom_call" | custom-call | bytes 3932160 | tf_op jit(solution)/shard_map/pallas_call | solution.py:393
  3.1 3.0 %collective-permute-start.4 = (bf16[1296,128]{1,0:T(8,128)(2,1)}, bf16[1296,128]{1,0:T(8,128)(2,1)S(1)}, u32[]{:S(2)}, u32[]{:S(2)}) collective-permute-start(bf16[1296,128]{1,0:T(8,128)(2,1)} %get-tuple-element.66), channel_id=1, source_target_pairs={{0,8},{8,16},{16,24},{24,0},{1,9},{9,17},{17,25},{25,1},{2,10},{10... | collective-permute-start | bytes 995336 | tf_op jit(solution)/shard_map/ppermute | solution.py:27
  6.1 1.5 %collective-permute-start.5 = (bf16[1296,128]{1,0:T(8,128)(2,1)}, bf16[1296,128]{1,0:T(8,128)(2,1)S(1)}, u32[]{:S(2)}, u32[]{:S(2)}) collective-permute-start(bf16[1296,128]{1,0:T(8,128)(2,1)} %get-tuple-element.67), channel_id=1, source_target_pairs={{0,16},{8,24},{16,0},{24,8},{1,17},{9,25},{17,1},{25,9},{2,18},{10... | collective-permute-start | bytes 995336 | tf_op jit(solution)/shard_map/ppermute | solution.py:27
  9.1 4.9 %conditional.1 = (s32[4,32]{1,0:T(4,128)S(1)}, f32[8,128,128]{2,1,0:T(8,128)S(1)}, f32[8,128,128]{2,1,0:T(8,128)S(1)}) conditional(s32[]{:T(128)} %bitcast.2, () %tuple.25, (s32[1,32]{1,0:T(1,128)S(1)}, s32[1,32]{1,0:T(1,128)S(1)}, s32[1,32]{1,0:T(1,128)S(1)}, s32[16]{0:T(128)S(1)}, bf16[32,128,128]{2,1,0:T(8,128)(2,1)}, ...), branch_computations={%region_0.0_spmd, %region_1.0_spmd} | conditional | flops 262144 | bytes 2621504 | solution.py:352
  9.2 3.2 %branch_1_fun.1 = (bf16[8,128,128]{2,1,0:T(8,128)(2,1)S(1)}, bf16[8,128,128]{2,1,0:T(8,128)(2,1)S(1)}, s32[4,32]{1,0:T(4,128)S(1)}) custom-call(s32[1,32]{1,0:T(1,128)S(1)} %get-tuple-element.105.row, s32[1,32]{1,0:T(1,128)S(1)} %get-tuple-element.106.col, s32[1,32]{1,0:T(1,128)S(1)} %get-tuple-element.107.live, s32[16]{0:T(128)S(1)} %get-tuple-element.17.place, ...), custom_call_target="tpu_custom_call" | custom-call | tf_op jit(solution)/shard_map/cond/branch_1_fun/pallas_call | solution.py:429
  14.2 3.7 %collective-permute-start.3 = (bf16[2,128,128]{2,1,0:T(8,128)(2,1)S(1)}, bf16[2,128,128]{2,1,0:T(8,128)(2,1)S(1)}, u32[]{:S(2)}, u32[]{:S(2)}) collective-permute-start(bf16[2,128,128]{2,1,0:T(8,128)(2,1)S(1)} %get-tuple-element.111), channel_id=1, source_target_pairs={{0,6},{1,7},{2,4},{3,5},{4,2},{5,3},{6,0},{7,1},{8,14},{9,15},{10,... | collective-permute-start | bytes 196616 | tf_op jit(solution)/shard_map/ppermute | solution.py:37
  19.0 3.1 %collective-permute-done.5.refs_4_.refs_3_ = bf16[1296,128]{1,0:T(8,128)(2,1)S(1)} collective-permute-done((bf16[1296,128]{1,0:T(8,128)(2,1)}, bf16[1296,128]{1,0:T(8,128)(2,1)S(1)}, u32[]{:S(2)}, u32[]{:S(2)}) %collective-permute-start.5) | collective-permute-done | bytes 331808 | tf_op jit(solution)/shard_map/ppermute | solution.py:27
  24.0 2.0 %collective-permute-start.7 = (bf16[256,128]{1,0:T(8,128)(2,1)S(1)}, bf16[256,128]{1,0:T(8,128)(2,1)S(1)}, u32[]{:S(2)}, u32[]{:S(2)}) collective-permute-start(bf16[256,128]{1,0:T(8,128)(2,1)S(1)} %fusion.8), channel_id=1, source_target_pairs={{0,4},{1,5},{2,6},{3,7},{4,0},{5,1},{6,2},{7,3},{8,12},{9,13},{10,... | collective-permute-start | bytes 196616 | tf_op jit(solution)/shard_map/ppermute | solution.py:37
  26.0 1.7 %collective-permute-start.10 = (bf16[640,128]{1,0:T(8,128)(2,1)S(1)}, bf16[640,128]{1,0:T(8,128)(2,1)S(1)}, u32[]{:S(2)}, u32[]{:S(2)}) collective-permute-start(bf16[640,128]{1,0:T(8,128)(2,1)S(1)} %get-tuple-element.70), channel_id=1, source_target_pairs={{0,24},{8,0},{16,8},{24,16},{1,25},{9,1},{17,9},{25,17},{2,26},{10... | collective-permute-start | bytes 491528 | tf_op jit(solution)/shard_map/ppermute | solution.py:27
  27.7 1.5 %collective-permute-start.11 = (bf16[640,128]{1,0:T(8,128)(2,1)S(1)}, bf16[640,128]{1,0:T(8,128)(2,1)S(1)}, u32[]{:S(2)}, u32[]{:S(2)}) collective-permute-start(bf16[640,128]{1,0:T(8,128)(2,1)S(1)} %get-tuple-element.71), channel_id=1, source_target_pairs={{0,16},{8,24},{16,0},{24,8},{1,17},{9,25},{17,1},{25,9},{2,18},{10... | collective-permute-start | bytes 491528 | tf_op jit(solution)/shard_map/ppermute | solution.py:27
  29.5 1.6 %collective-permute-start.9 = (bf16[448,128]{1,0:T(8,128)(2,1)S(1)}, bf16[448,128]{1,0:T(8,128)(2,1)S(1)}, u32[]{:S(2)}, u32[]{:S(2)}) collective-permute-start(bf16[448,128]{1,0:T(8,128)(2,1)S(1)} %pad_maximum_fusion.2), channel_id=1, source_target_pairs={{0,2},{1,3},{2,0},{3,1},{4,6},{5,7},{6,4},{7,5},{8,10},{9,11},{10,... | collective-permute-start | bytes 344072 | tf_op jit(solution)/shard_map/ppermute | solution.py:37
  31.6 3.3 %collective-permute-done.8 = bf16[64,128]{1,0:T(8,128)(2,1)S(1)} collective-permute-done((bf16[64,128]{1,0:T(8,128)(2,1)S(1)}, bf16[64,128]{1,0:T(8,128)(2,1)S(1)}, u32[]{:S(2)}, u32[]{:S(2)}) %collective-permute-start.8) | collective-permute-done | bytes 16416 | tf_op jit(solution)/shard_map/ppermute | solution.py:37
  34.9 1.6 %collective-permute-done.11.refs_8_ = bf16[640,128]{1,0:T(8,128)(2,1)S(1)} collective-permute-done((bf16[640,128]{1,0:T(8,128)(2,1)S(1)}, bf16[640,128]{1,0:T(8,128)(2,1)S(1)}, u32[]{:S(2)}, u32[]{:S(2)}) %collective-permute-start.11) | collective-permute-done | bytes 163872 | tf_op jit(solution)/shard_map/ppermute | solution.py:27
  36.6 1.5 %collective-permute-done.13.refs_5_ = bf16[8,128,128]{2,1,0:T(8,128)(2,1)S(1)} collective-permute-done((bf16[8,128,128]{2,1,0:T(8,128)(2,1)S(1)}, bf16[8,128,128]{2,1,0:T(8,128)(2,1)S(1)}, u32[]{:S(2)}, u32[]{:S(2)}) %collective-permute-start.13) | collective-permute-done | bytes 262176 | tf_op jit(solution)/shard_map/ppermute | solution.py:42
  38.1 1.7 %shard_map.135 = (f32[20,128,128]{2,1,0:T(8,128)S(1)}, bf16[20,128,128]{2,1,0:T(8,128)(2,1)S(1)}, bf16[5,128,128]{2,1,0:T(8,128)(2,1)S(1)}, bf16[5,128,128]{2,1,0:T(8,128)(2,1)S(1)}, bf16[5,128,128]{2,1,0:T(8,128)(2,1)S(1)}) custom-call(s32[4,32]{1,0:T(4,128)S(1)} %get-tuple-element.76.refs_0_.slots, bf16[32,128,128]{2,1,0:T(8,128)(2,1)S(1)} %bitcast.80, ...), custom_call_target="tpu_custom_call" | custom-call | flops 134217728 | bytes 6291456 | tf_op jit(solution)/shard_map/pallas_call | solution.py:50
  42.9 2.4 %collective-permute-start.20 = (bf16[640,128]{1,0:T(8,128)(2,1)S(1)}, bf16[640,128]{1,0:T(8,128)(2,1)S(1)}, u32[]{:S(2)}, u32[]{:S(2)}) collective-permute-start(bf16[640,128]{1,0:T(8,128)(2,1)S(1)} %bitcast.72), channel_id=1, source_target_pairs={{0,24},{8,0},{16,8},{24,16},{1,25},{9,1},{17,9},{25,17},{2,26},{10... | collective-permute-start | bytes 491528 | tf_op jit(solution)/shard_map/ppermute | solution.py:27
  45.4 2.5 %collective-permute-start.17 = (bf16[2,128,128]{2,1,0:T(8,128)(2,1)S(1)}, bf16[2,128,128]{2,1,0:T(8,128)(2,1)S(1)}, u32[]{:S(2)}, u32[]{:S(2)}) collective-permute-start(bf16[2,128,128]{2,1,0:T(8,128)(2,1)S(1)} %get-tuple-element.108), channel_id=1, source_target_pairs={{0,6},{1,7},{2,4},{3,5},{4,2},{5,3},{6,0},{7,1},{8,14},{9,15},{10,... | collective-permute-start | bytes 196616 | tf_op jit(solution)/shard_map/ppermute | solution.py:37
  52.5 2.1 %collective-permute-start.28 = (bf16[1280,128]{1,0:T(8,128)(2,1)S(1)}, bf16[1280,128]{1,0:T(8,128)(2,1)S(1)}, u32[]{:S(2)}, u32[]{:S(2)}) collective-permute-start(bf16[1280,128]{1,0:T(8,128)(2,1)S(1)} %get-tuple-element.89), channel_id=1, source_target_pairs={{0,24},{8,0},{16,8},{24,16},{1,25},{9,1},{17,9},{25,17},{2,26},{10... | collective-permute-start | bytes 983048 | tf_op jit(solution)/shard_map/ppermute | solution.py:27
  56.6 1.6 %collective-permute-start.21 = (bf16[256,128]{1,0:T(8,128)(2,1)S(1)}, bf16[256,128]{1,0:T(8,128)(2,1)S(1)}, u32[]{:S(2)}, u32[]{:S(2)}) collective-permute-start(bf16[256,128]{1,0:T(8,128)(2,1)S(1)} %fusion.7), channel_id=1, source_target_pairs={{0,4},{1,5},{2,6},{3,7},{4,0},{5,1},{6,2},{7,3},{8,12},{9,13},{10,... | collective-permute-start | bytes 196616 | tf_op jit(solution)/shard_map/ppermute | solution.py:37
  59.7 2.2 %collective-permute-done.21 = bf16[256,128]{1,0:T(8,128)(2,1)S(1)} collective-permute-done((bf16[256,128]{1,0:T(8,128)(2,1)S(1)}, bf16[256,128]{1,0:T(8,128)(2,1)S(1)}, u32[]{:S(2)}, u32[]{:S(2)}) %collective-permute-start.21) | collective-permute-done | bytes 65568 | tf_op jit(solution)/shard_map/ppermute | solution.py:37
  61.9 1.6 %collective-permute-start.23 = (bf16[256,128]{1,0:T(8,128)(2,1)S(1)}, bf16[256,128]{1,0:T(8,128)(2,1)S(1)}, u32[]{:S(2)}, u32[]{:S(2)}) collective-permute-start(bf16[256,128]{1,0:T(8,128)(2,1)S(1)} %collective-permute-done.21), channel_id=1, source_target_pairs={{0,2},{1,3},{2,0},{3,1},{4,6},{5,7},{6,4},{7,5},{8,10},{9,11},{10,... | collective-permute-start | bytes 196616 | tf_op jit(solution)/shard_map/ppermute | solution.py:37
  63.5 2.7 %collective-permute-done.23 = bf16[256,128]{1,0:T(8,128)(2,1)S(1)} collective-permute-done((bf16[256,128]{1,0:T(8,128)(2,1)S(1)}, bf16[256,128]{1,0:T(8,128)(2,1)S(1)}, u32[]{:S(2)}, u32[]{:S(2)}) %collective-permute-start.23) | collective-permute-done | bytes 65568 | tf_op jit(solution)/shard_map/ppermute | solution.py:37
  68.7 1.5 %shard_map.138 = f32[20,128,128]{2,1,0:T(8,128)S(1)} custom-call(s32[4,32]{1,0:T(4,128)S(1)} %get-tuple-element.76.refs_0_.slots, bf16[32,128,128]{2,1,0:T(8,128)(2,1)S(1)} %bitcast.82, f32[20,128,128]{2,1,0:T(8,128)S(1)} %get-tuple-element.83.duals, s32[20,128,128]{2,1,0:T(8,128)S(1)} %bitcast.68, bf16[8,128,128]{2,1,0:T(8,128)(2,1)S(1)} %bitcast.71, ...), custom_call_target="tpu_custom_call" | custom-call | tf_op jit(solution)/shard_map/pallas_call | solution.py:50
  70.2 1.6 %shard_map.139 = (f32[2560,128]{1,0:T(8,128)}, f32[2560,128]{1,0:T(8,128)}) custom-call(f32[2560,128]{1,0:T(8,128)S(1)} %bitcast.64, bf16[1280,128]{1,0:T(8,128)(2,1)S(1)} %get-tuple-element.88.refs_1_, bf16[1280,128]{1,0:T(8,128)(2,1)S(1)} %collective-permute-done.28.refs_2_, bf16[1280,128]{1,0:T(8,128)(2,1)S(1)} %collective-permute-done.29.refs_3_, ...), custom_call_target="tpu_custom_call" | custom-call | bytes 3932160 | tf_op jit(solution)/shard_map/pallas_call | solution.py:506
  (85 shorter events, 20.7 us)
Async XLA Ops:
  3.1 14.7 %collective-permute-start.4 = (bf16[1296,128]{1,0:T(8,128)(2,1)}, bf16[1296,128]{1,0:T(8,128)(2,1)S(1)}, u32[]{:S(2)}, u32[]{:S(2)}) collective-permute-start(bf16[1296,128]{1,0:T(8,128)(2,1)} %get-tuple-element.66), channel_id=1, source_target_pairs={{0,8},{8,16},{16,24},{24,0},{1,9},{9,17},{17,25},{25,1},{2,10},{10... | collective-permute-start | bytes 995336 | tf_op jit(solution)/shard_map/ppermute | solution.py:27
  6.1 16.1 %collective-permute-start.5 = (bf16[1296,128]{1,0:T(8,128)(2,1)}, bf16[1296,128]{1,0:T(8,128)(2,1)S(1)}, u32[]{:S(2)}, u32[]{:S(2)}) collective-permute-start(bf16[1296,128]{1,0:T(8,128)(2,1)} %get-tuple-element.67), channel_id=1, source_target_pairs={{0,16},{8,24},{16,0},{24,8},{1,17},{9,25},{17,1},{25,9},{2,18},{10... | collective-permute-start | bytes 995336 | tf_op jit(solution)/shard_map/ppermute | solution.py:27
  7.6 14.8 %collective-permute-start.6 = (bf16[1296,128]{1,0:T(8,128)(2,1)}, bf16[1296,128]{1,0:T(8,128)(2,1)S(1)}, u32[]{:S(2)}, u32[]{:S(2)}) collective-permute-start(bf16[1296,128]{1,0:T(8,128)(2,1)} %get-tuple-element.68), channel_id=1, source_target_pairs={{0,24},{8,0},{16,8},{24,16},{1,25},{9,1},{17,9},{25,17},{2,26},{10... | collective-permute-start | bytes 995336 | tf_op jit(solution)/shard_map/ppermute | solution.py:27
  14.2 9.0 %collective-permute-start.3 = (bf16[2,128,128]{2,1,0:T(8,128)(2,1)S(1)}, bf16[2,128,128]{2,1,0:T(8,128)(2,1)S(1)}, u32[]{:S(2)}, u32[]{:S(2)}) collective-permute-start(bf16[2,128,128]{2,1,0:T(8,128)(2,1)S(1)} %get-tuple-element.111), channel_id=1, source_target_pairs={{0,6},{1,7},{2,4},{3,5},{4,2},{5,3},{6,0},{7,1},{8,14},{9,15},{10,... | collective-permute-start | bytes 196616 | tf_op jit(solution)/shard_map/ppermute | solution.py:37
  17.8 5.3 %collective-permute-start.2 = (bf16[2,128,128]{2,1,0:T(8,128)(2,1)S(1)}, bf16[2,128,128]{2,1,0:T(8,128)(2,1)S(1)}, u32[]{:S(2)}, u32[]{:S(2)}) collective-permute-start(bf16[2,128,128]{2,1,0:T(8,128)(2,1)S(1)} %get-tuple-element.112), channel_id=1, source_target_pairs={{0,2},{1,3},{2,0},{3,1},{4,6},{5,7},{6,4},{7,5},{8,10},{9,11},{10,... | collective-permute-start | bytes 196616 | tf_op jit(solution)/shard_map/ppermute | solution.py:37
  17.9 5.9 %collective-permute-start.1 = (bf16[2,128,128]{2,1,0:T(8,128)(2,1)S(1)}, bf16[2,128,128]{2,1,0:T(8,128)(2,1)S(1)}, u32[]{:S(2)}, u32[]{:S(2)}) collective-permute-start(bf16[2,128,128]{2,1,0:T(8,128)(2,1)S(1)} %get-tuple-element.113), channel_id=1, source_target_pairs={{0,4},{1,5},{2,6},{3,7},{4,0},{5,1},{6,2},{7,3},{8,12},{9,13},{10,... | collective-permute-start | bytes 196616 | tf_op jit(solution)/shard_map/ppermute | solution.py:37
  24.0 5.5 %collective-permute-start.7 = (bf16[256,128]{1,0:T(8,128)(2,1)S(1)}, bf16[256,128]{1,0:T(8,128)(2,1)S(1)}, u32[]{:S(2)}, u32[]{:S(2)}) collective-permute-start(bf16[256,128]{1,0:T(8,128)(2,1)S(1)} %fusion.8), channel_id=1, source_target_pairs={{0,4},{1,5},{2,6},{3,7},{4,0},{5,1},{6,2},{7,3},{8,12},{9,13},{10,... | collective-permute-start | bytes 196616 | tf_op jit(solution)/shard_map/ppermute | solution.py:37
  26.0 8.9 %collective-permute-start.10 = (bf16[640,128]{1,0:T(8,128)(2,1)S(1)}, bf16[640,128]{1,0:T(8,128)(2,1)S(1)}, u32[]{:S(2)}, u32[]{:S(2)}) collective-permute-start(bf16[640,128]{1,0:T(8,128)(2,1)S(1)} %get-tuple-element.70), channel_id=1, source_target_pairs={{0,24},{8,0},{16,8},{24,16},{1,25},{9,1},{17,9},{25,17},{2,26},{10... | collective-permute-start | bytes 491528 | tf_op jit(solution)/shard_map/ppermute | solution.py:27
  27.7 8.8 %collective-permute-start.11 = (bf16[640,128]{1,0:T(8,128)(2,1)S(1)}, bf16[640,128]{1,0:T(8,128)(2,1)S(1)}, u32[]{:S(2)}, u32[]{:S(2)}) collective-permute-start(bf16[640,128]{1,0:T(8,128)(2,1)S(1)} %get-tuple-element.71), channel_id=1, source_target_pairs={{0,16},{8,24},{16,0},{24,8},{1,17},{9,25},{17,1},{25,9},{2,18},{10... | collective-permute-start | bytes 491528 | tf_op jit(solution)/shard_map/ppermute | solution.py:27
  29.2 7.3 %collective-permute-start.12 = (bf16[640,128]{1,0:T(8,128)(2,1)S(1)}, bf16[640,128]{1,0:T(8,128)(2,1)S(1)}, u32[]{:S(2)}, u32[]{:S(2)}) collective-permute-start(bf16[640,128]{1,0:T(8,128)(2,1)S(1)} %get-tuple-element.72), channel_id=1, source_target_pairs={{0,8},{8,16},{16,24},{24,0},{1,9},{9,17},{17,25},{25,1},{2,10},{10... | collective-permute-start | bytes 491528 | tf_op jit(solution)/shard_map/ppermute | solution.py:27
  29.5 7.0 %collective-permute-start.9 = (bf16[448,128]{1,0:T(8,128)(2,1)S(1)}, bf16[448,128]{1,0:T(8,128)(2,1)S(1)}, u32[]{:S(2)}, u32[]{:S(2)}) collective-permute-start(bf16[448,128]{1,0:T(8,128)(2,1)S(1)} %pad_maximum_fusion.2), channel_id=1, source_target_pairs={{0,2},{1,3},{2,0},{3,1},{4,6},{5,7},{6,4},{7,5},{8,10},{9,11},{10,... | collective-permute-start | bytes 344072 | tf_op jit(solution)/shard_map/ppermute | solution.py:37
  41.0 4.2 %collective-permute-start.14 = (bf16[8,128,128]{2,1,0:T(8,128)(2,1)S(1)}, bf16[8,128,128]{2,1,0:T(8,128)(2,1)S(1)}, u32[]{:S(2)}, u32[]{:S(2)}) collective-permute-start(bf16[8,128,128]{2,1,0:T(8,128)(2,1)S(1)} %get-tuple-element.82), channel_id=1, source_target_pairs={{0,1},{1,0},{2,3},{3,2},{4,5},{5,4},{6,7},{7,6},{8,9},{9,8},{10,11... | collective-permute-start | bytes 786440 | tf_op jit(solution)/shard_map/ppermute | solution.py:42
  41.3 8.0 %collective-permute-start.18 = (bf16[640,128]{1,0:T(8,128)(2,1)S(1)}, bf16[640,128]{1,0:T(8,128)(2,1)S(1)}, u32[]{:S(2)}, u32[]{:S(2)}) collective-permute-start(bf16[640,128]{1,0:T(8,128)(2,1)S(1)} %bitcast.74), channel_id=1, source_target_pairs={{0,8},{8,16},{16,24},{24,0},{1,9},{9,17},{17,25},{25,1},{2,10},{10... | collective-permute-start | bytes 491528 | tf_op jit(solution)/shard_map/ppermute | solution.py:27
  41.5 9.8 %collective-permute-start.19 = (bf16[640,128]{1,0:T(8,128)(2,1)S(1)}, bf16[640,128]{1,0:T(8,128)(2,1)S(1)}, u32[]{:S(2)}, u32[]{:S(2)}) collective-permute-start(bf16[640,128]{1,0:T(8,128)(2,1)S(1)} %bitcast.73), channel_id=1, source_target_pairs={{0,16},{8,24},{16,0},{24,8},{1,17},{9,25},{17,1},{25,9},{2,18},{10... | collective-permute-start | bytes 491528 | tf_op jit(solution)/shard_map/ppermute | solution.py:27
  42.9 8.9 %collective-permute-start.20 = (bf16[640,128]{1,0:T(8,128)(2,1)S(1)}, bf16[640,128]{1,0:T(8,128)(2,1)S(1)}, u32[]{:S(2)}, u32[]{:S(2)}) collective-permute-start(bf16[640,128]{1,0:T(8,128)(2,1)S(1)} %bitcast.72), channel_id=1, source_target_pairs={{0,24},{8,0},{16,8},{24,16},{1,25},{9,1},{17,9},{25,17},{2,26},{10... | collective-permute-start | bytes 491528 | tf_op jit(solution)/shard_map/ppermute | solution.py:27
  45.4 10.3 %collective-permute-start.17 = (bf16[2,128,128]{2,1,0:T(8,128)(2,1)S(1)}, bf16[2,128,128]{2,1,0:T(8,128)(2,1)S(1)}, u32[]{:S(2)}, u32[]{:S(2)}) collective-permute-start(bf16[2,128,128]{2,1,0:T(8,128)(2,1)S(1)} %get-tuple-element.108), channel_id=1, source_target_pairs={{0,6},{1,7},{2,4},{3,5},{4,2},{5,3},{6,0},{7,1},{8,14},{9,15},{10,... | collective-permute-start | bytes 196616 | tf_op jit(solution)/shard_map/ppermute | solution.py:37
  47.9 7.8 %collective-permute-start.16 = (bf16[2,128,128]{2,1,0:T(8,128)(2,1)S(1)}, bf16[2,128,128]{2,1,0:T(8,128)(2,1)S(1)}, u32[]{:S(2)}, u32[]{:S(2)}) collective-permute-start(bf16[2,128,128]{2,1,0:T(8,128)(2,1)S(1)} %get-tuple-element.109), channel_id=1, source_target_pairs={{0,2},{1,3},{2,0},{3,1},{4,6},{5,7},{6,4},{7,5},{8,10},{9,11},{10,... | collective-permute-start | bytes 196616 | tf_op jit(solution)/shard_map/ppermute | solution.py:37
  49.2 6.5 %collective-permute-start.15 = (bf16[2,128,128]{2,1,0:T(8,128)(2,1)S(1)}, bf16[2,128,128]{2,1,0:T(8,128)(2,1)S(1)}, u32[]{:S(2)}, u32[]{:S(2)}) collective-permute-start(bf16[2,128,128]{2,1,0:T(8,128)(2,1)S(1)} %get-tuple-element.110), channel_id=1, source_target_pairs={{0,4},{1,5},{2,6},{3,7},{4,0},{5,1},{6,2},{7,3},{8,12},{9,13},{10,... | collective-permute-start | bytes 196616 | tf_op jit(solution)/shard_map/ppermute | solution.py:37
  52.5 17.8 %collective-permute-start.28 = (bf16[1280,128]{1,0:T(8,128)(2,1)S(1)}, bf16[1280,128]{1,0:T(8,128)(2,1)S(1)}, u32[]{:S(2)}, u32[]{:S(2)}) collective-permute-start(bf16[1280,128]{1,0:T(8,128)(2,1)S(1)} %get-tuple-element.89), channel_id=1, source_target_pairs={{0,24},{8,0},{16,8},{24,16},{1,25},{9,1},{17,9},{25,17},{2,26},{10... | collective-permute-start | bytes 983048 | tf_op jit(solution)/shard_map/ppermute | solution.py:27
  54.6 15.6 %collective-permute-start.29 = (bf16[1280,128]{1,0:T(8,128)(2,1)S(1)}, bf16[1280,128]{1,0:T(8,128)(2,1)S(1)}, u32[]{:S(2)}, u32[]{:S(2)}) collective-permute-start(bf16[1280,128]{1,0:T(8,128)(2,1)S(1)} %get-tuple-element.90), channel_id=1, source_target_pairs={{0,16},{8,24},{16,0},{24,8},{1,17},{9,25},{17,1},{25,9},{2,18},{10... | collective-permute-start | bytes 983048 | tf_op jit(solution)/shard_map/ppermute | solution.py:27
  55.7 14.6 %collective-permute-start.30 = (bf16[1280,128]{1,0:T(8,128)(2,1)S(1)}, bf16[1280,128]{1,0:T(8,128)(2,1)S(1)}, u32[]{:S(2)}, u32[]{:S(2)}) collective-permute-start(bf16[1280,128]{1,0:T(8,128)(2,1)S(1)} %get-tuple-element.91), channel_id=1, source_target_pairs={{0,8},{8,16},{16,24},{24,0},{1,9},{9,17},{17,25},{25,1},{2,10},{10... | collective-permute-start | bytes 983048 | tf_op jit(solution)/shard_map/ppermute | solution.py:27
  56.6 5.2 %collective-permute-start.21 = (bf16[256,128]{1,0:T(8,128)(2,1)S(1)}, bf16[256,128]{1,0:T(8,128)(2,1)S(1)}, u32[]{:S(2)}, u32[]{:S(2)}) collective-permute-start(bf16[256,128]{1,0:T(8,128)(2,1)S(1)} %fusion.7), channel_id=1, source_target_pairs={{0,4},{1,5},{2,6},{3,7},{4,0},{5,1},{6,2},{7,3},{8,12},{9,13},{10,... | collective-permute-start | bytes 196616 | tf_op jit(solution)/shard_map/ppermute | solution.py:37
  58.2 5.3 %collective-permute-start.22 = (bf16[256,128]{1,0:T(8,128)(2,1)S(1)}, bf16[256,128]{1,0:T(8,128)(2,1)S(1)}, u32[]{:S(2)}, u32[]{:S(2)}) collective-permute-start(bf16[256,128]{1,0:T(8,128)(2,1)S(1)} %fusion.7), channel_id=1, source_target_pairs={{0,2},{1,3},{2,0},{3,1},{4,6},{5,7},{6,4},{7,5},{8,10},{9,11},{10,... | collective-permute-start | bytes 196616 | tf_op jit(solution)/shard_map/ppermute | solution.py:37
  61.9 4.3 %collective-permute-start.23 = (bf16[256,128]{1,0:T(8,128)(2,1)S(1)}, bf16[256,128]{1,0:T(8,128)(2,1)S(1)}, u32[]{:S(2)}, u32[]{:S(2)}) collective-permute-start(bf16[256,128]{1,0:T(8,128)(2,1)S(1)} %collective-permute-done.21), channel_id=1, source_target_pairs={{0,2},{1,3},{2,0},{3,1},{4,6},{5,7},{6,4},{7,5},{8,10},{9,11},{10,... | collective-permute-start | bytes 196616 | tf_op jit(solution)/shard_map/ppermute | solution.py:37
  (18 other events, 115.3 us)

commit v6 on v5

--- a/solution.py
+++ b/solution.py
@@ -167,11 +167,6 @@
     give_partials(acc, keep, send)
 
 
-def pull_kernel(slots, tiles, half, keep, send, acc):
-    pull_slots(slots, tiles, half, acc)
-    give_partials(acc, keep, send)
-
-
 def step_duals(parts, size, refs, blocks, acc):
     slots, tiles, duals, demand, near, far = refs[:6]
     combined = refs[6:]
@@ -190,24 +185,20 @@
     push_slots(slots, tiles, blocks, acc)
 
 
-def push_step_kernel(parts, size, *refs):
-    ins, next_duals, half = refs[: 6 + parts], refs[6 + parts], refs[7 + parts]
-    packets, blocks, acc = refs[8 + parts : -2], refs[-2], refs[-1]
-    tile = ins[1].shape[1]
+def push_pull_kernel(parts, size, *refs):
+    ins, (next_duals, keep, send) = refs[: 6 + parts], refs[6 + parts : 9 + parts]
+    packets, (blocks, half, acc, partials) = refs[9 + parts : -4], refs[-4:]
+    slots, tiles = ins[:2]
     step_duals(parts, size, ins, blocks, acc)
     n = next_duals.shape[0]
     next_duals[...] = acc[0:n]
     half[...] = acc[0:n].astype(BF)
-    pieces = size // tile
+    pieces = n // parts
     for r in range(1, parts):
         part = lax.rem(lax.axis_index("section") + r, parts)
         packets[r - 1][...] = half[pl.ds(part * pieces, pieces)]
-
-
-def place_kernel(parts, size, *refs):
-    out = refs[parts]
-    for r in range(parts):
-        out[quarter_rows(r, parts, size), :] = refs[r][size:].astype(F32)
+    pull_slots(slots, tiles, half, partials)
+    give_partials(partials, keep, send)
 
 
 def push_kernel(slots, tiles, duals, demand, *refs):
@@ -330,7 +321,6 @@
     flops = 2 * slots * tile * tile * scenarios
     quarter = jax.ShapeDtypeStruct((size, scenarios), BF)
     quarter3 = jax.ShapeDtypeStruct((size // tile, tile, scenarios), BF)
-    whole_half = jax.ShapeDtypeStruct((band_tiles, tile, scenarios), BF)
     half_blocks = jax.ShapeDtypeStruct((blocks // 2, tile, scenarios), BF)
     pull_scratch = [
         pltpu.VMEM((band_tiles, tile, scenarios), BF),
@@ -442,11 +432,11 @@
     combined = [combined[0]] + [rotate(combined[r], "section", -r) for r in range(1, parts)]
     near, far = spread(bar1, combined, tile // 2)
 
-    duals1, half, *halves = call(
-        functools.partial(push_step_kernel, parts, size),
-        [jax.ShapeDtypeStruct((band_tiles, tile, scenarios), F32), whole_half]
+    duals1, keep, send, *halves = call(
+        functools.partial(push_pull_kernel, parts, size),
+        [jax.ShapeDtypeStruct((band_tiles, tile, scenarios), F32), half_blocks, half_blocks]
         + [quarter3] * (parts - 1),
-        push_scratch,
+        [push_scratch[0], pull_scratch[0], push_scratch[1], pull_scratch[1]],
         flops,
         16 * rows * scenarios + 2 * slots * tile * tile,
         slots_of,
@@ -470,17 +460,6 @@
         *packets,
         stocks,
         *halves,
-    )
-    keep, send = call(
-        pull_kernel,
-        [half_blocks, half_blocks],
-        pull_scratch[1:],
-        flops,
-        2 * rows * scenarios + 2 * slots * tile * tile,
-        slots_of,
-        tiles,
-        half,
-        smem=1,
     )
     send = swap_core(send)
     pulled = collect(keep, send, outs)

time: 72 us -> 71.6 us (level)
  starting transfers between devices: 34.9 us -> 36.3 us
  waiting for transfers between devices: 21.5 us -> 20.3 us
    ppermute x12, waiting for transfers between devices: 7.95 us -> 5.12 us  [rotate(): lax.ppermute(value, axis, [(i, (i + by) % size) for i in range(size)])]
    ppermute x12, waiting for transfers between devices: 8.78 us -> 10.4 us  [flip_chip(): lax.ppermute(value, 'zone', [(i, i ^ by * CORES) for i in range(size)])]
    ppermute x12, starting transfers between devices: 17.2 us -> 18.7 us  [flip_chip(): lax.ppermute(value, 'zone', [(i, i ^ by * CORES) for i in range(size)])]
    pallas_call x5 -> x4, Pallas kernels: 5.74 us -> 5.11 us  [call(): pl.pallas_call(kernel, out_shape=outs, in_specs=[SMEM] * smem + [VMEM] *...]
  transfers between devices with their start and end apart: 31 -> 31, of which waited for: 14 -> 15; matrix products, arithmetic and copies ran while one was open for 2% -> 2% of each run, Pallas kernels for 8% -> 9%
where the time goes in v6:
time: 71.6 us; the launch traced here: 71.4 us
  starting transfers between devices  36.3 us (51%)
  waiting for transfers between devices  20.3 us (28%)
  Pallas kernels  12.4 us (17%)
  other arithmetic  1.32 us (2%)
  between operations  0.98 us (1%)
    ppermute x12, starting transfers between devices, flip_chip(): lax.ppermute(value, 'zone', [(i, i ^ by * CORES) for i in range(size)])  18.7 us
    ppermute x12, starting transfers between devices, rotate(): lax.ppermute(value, axis, [(i, (i + by) % size) for i in range(size)])  16.6 us
    ppermute x12, waiting for transfers between devices, flip_chip(): lax.ppermute(value, 'zone', [(i, i ^ by * CORES) for i in range(size)])  10.4 us
    ppermute x12, waiting for transfers between devices, rotate(): lax.ppermute(value, axis, [(i, (i + by) % size) for i in range(size)])  5.12 us
    pallas_call x4, Pallas kernels, call(): pl.pallas_call(kernel, out_shape=outs, in_specs=[SMEM] * smem + [VMEM] *...  5.11 us
    ppermute x7, waiting for transfers between devices, swap_core(): return lax.ppermute(value, 'zone', [(i, i ^ 1) for i in range(size)])  4.81 us
    pallas_call x1, Pallas kernels, first_pull(): pl.pallas_call(functools.partial(first_pull_kernel, shape), out_shape=[ha...  3.25 us
    pallas_call x1, Pallas kernels, per_device(): pl.pallas_call(functools.partial(pack_kernel, parts, size), out_shape=pac...  2.42 us
  transfers between devices with their start and end apart: 31, of which 15 were waited for; matrix products, arithmetic and copies ran while one was open for 2% of the time, Pallas kernels for 9%

profile of v6, /device:TPU:0, one launch (start us, length us, event | category | flops | bytes accessed | tf_op | source)
XLA Modules:
  0.0 71.4 jit_solution(17111311131782198840)
XLA Ops:
  0.7 2.4 %shard_map.133 = (bf16[1296,128]{1,0:T(8,128)(2,1)}, bf16[1296,128]{1,0:T(8,128)(2,1)}, bf16[1296,128]{1,0:T(8,128)(2,1)}) custom-call(f32[2560,128]{1,0:T(8,128)} %bitcast.75, f32[2560,128]{1,0:T(8,128)} %bitcast.65, f32[1,2560]{1,0:T(1,128)} %refs_1_.1), custom_call_target="tpu_custom_call" | custom-call | bytes 3932160 | tf_op jit(solution)/shard_map/pallas_call | solution.py:383
  3.1 3.0 %collective-permute-start.4 = (bf16[1296,128]{1,0:T(8,128)(2,1)}, bf16[1296,128]{1,0:T(8,128)(2,1)S(1)}, u32[]{:S(2)}, u32[]{:S(2)}) collective-permute-start(bf16[1296,128]{1,0:T(8,128)(2,1)} %get-tuple-element.65), channel_id=1, source_target_pairs={{0,8},{8,16},{16,24},{24,0},{1,9},{9,17},{17,25},{25,1},{2,10},{10... | collective-permute-start | bytes 995336 | tf_op jit(solution)/shard_map/ppermute | solution.py:27
  6.1 1.5 %collective-permute-start.5 = (bf16[1296,128]{1,0:T(8,128)(2,1)}, bf16[1296,128]{1,0:T(8,128)(2,1)S(1)}, u32[]{:S(2)}, u32[]{:S(2)}) collective-permute-start(bf16[1296,128]{1,0:T(8,128)(2,1)} %get-tuple-element.66), channel_id=1, source_target_pairs={{0,16},{8,24},{16,0},{24,8},{1,17},{9,25},{17,1},{25,9},{2,18},{10... | collective-permute-start | bytes 995336 | tf_op jit(solution)/shard_map/ppermute | solution.py:27
  9.1 4.9 %conditional.1 = (s32[4,32]{1,0:T(4,128)S(1)}, f32[8,128,128]{2,1,0:T(8,128)S(1)}, f32[8,128,128]{2,1,0:T(8,128)S(1)}) conditional(s32[]{:T(128)} %bitcast.2, () %tuple.25, (s32[1,32]{1,0:T(1,128)S(1)}, s32[1,32]{1,0:T(1,128)S(1)}, s32[1,32]{1,0:T(1,128)S(1)}, s32[16]{0:T(128)S(1)}, bf16[32,128,128]{2,1,0:T(8,128)(2,1)}, ...), branch_computations={%region_0.0_spmd, %region_1.0_spmd} | conditional | flops 262144 | bytes 2621504 | solution.py:342
  9.2 3.2 %branch_1_fun.1 = (bf16[8,128,128]{2,1,0:T(8,128)(2,1)S(1)}, bf16[8,128,128]{2,1,0:T(8,128)(2,1)S(1)}, s32[4,32]{1,0:T(4,128)S(1)}) custom-call(s32[1,32]{1,0:T(1,128)S(1)} %get-tuple-element.103.row, s32[1,32]{1,0:T(1,128)S(1)} %get-tuple-element.104.col, s32[1,32]{1,0:T(1,128)S(1)} %get-tuple-element.105.live, s32[16]{0:T(128)S(1)} %get-tuple-element.17.place, ...), custom_call_target="tpu_custom_call" | custom-call | tf_op jit(solution)/shard_map/cond/branch_1_fun/pallas_call | solution.py:419
  12.5 1.5 %collective-permute-done = bf16[8,128,128]{2,1,0:T(8,128)(2,1)S(1)} collective-permute-done((bf16[8,128,128]{2,1,0:T(8,128)(2,1)S(1)}, bf16[8,128,128]{2,1,0:T(8,128)(2,1)S(1)}, u32[]{:S(2)}, u32[]{:S(2)}) %collective-permute-start) | collective-permute-done | bytes 262176 | tf_op jit(solution)/shard_map/cond/branch_1_fun/ppermute | solution.py:42
  14.2 2.6 %collective-permute-start.1 = (bf16[2,128,128]{2,1,0:T(8,128)(2,1)S(1)}, bf16[2,128,128]{2,1,0:T(8,128)(2,1)S(1)}, u32[]{:S(2)}, u32[]{:S(2)}) collective-permute-start(bf16[2,128,128]{2,1,0:T(8,128)(2,1)S(1)} %get-tuple-element.111), channel_id=1, source_target_pairs={{0,4},{1,5},{2,6},{3,7},{4,0},{5,1},{6,2},{7,3},{8,12},{9,13},{10,... | collective-permute-start | bytes 196616 | tf_op jit(solution)/shard_map/ppermute | solution.py:37
  16.8 1.6 %collective-permute-start.2 = (bf16[2,128,128]{2,1,0:T(8,128)(2,1)S(1)}, bf16[2,128,128]{2,1,0:T(8,128)(2,1)S(1)}, u32[]{:S(2)}, u32[]{:S(2)}) collective-permute-start(bf16[2,128,128]{2,1,0:T(8,128)(2,1)S(1)} %get-tuple-element.110), channel_id=1, source_target_pairs={{0,2},{1,3},{2,0},{3,1},{4,6},{5,7},{6,4},{7,5},{8,10},{9,11},{10,... | collective-permute-start | bytes 196616 | tf_op jit(solution)/shard_map/ppermute | solution.py:37
  18.4 1.6 %collective-permute-start.3 = (bf16[2,128,128]{2,1,0:T(8,128)(2,1)S(1)}, bf16[2,128,128]{2,1,0:T(8,128)(2,1)S(1)}, u32[]{:S(2)}, u32[]{:S(2)}) collective-permute-start(bf16[2,128,128]{2,1,0:T(8,128)(2,1)S(1)} %get-tuple-element.109), channel_id=1, source_target_pairs={{0,6},{1,7},{2,4},{3,5},{4,2},{5,3},{6,0},{7,1},{8,14},{9,15},{10,... | collective-permute-start | bytes 196616 | tf_op jit(solution)/shard_map/ppermute | solution.py:37
  20.1 2.1 %collective-permute-done.5.refs_4_.refs_3_ = bf16[1296,128]{1,0:T(8,128)(2,1)S(1)} collective-permute-done((bf16[1296,128]{1,0:T(8,128)(2,1)}, bf16[1296,128]{1,0:T(8,128)(2,1)S(1)}, u32[]{:S(2)}, u32[]{:S(2)}) %collective-permute-start.5) | collective-permute-done | bytes 331808 | tf_op jit(solution)/shard_map/ppermute | solution.py:27
  24.6 1.7 %collective-permute-start.7 = (bf16[256,128]{1,0:T(8,128)(2,1)S(1)}, bf16[256,128]{1,0:T(8,128)(2,1)S(1)}, u32[]{:S(2)}, u32[]{:S(2)}) collective-permute-start(bf16[256,128]{1,0:T(8,128)(2,1)S(1)} %fusion.8), channel_id=1, source_target_pairs={{0,4},{1,5},{2,6},{3,7},{4,0},{5,1},{6,2},{7,3},{8,12},{9,13},{10,... | collective-permute-start | bytes 196616 | tf_op jit(solution)/shard_map/ppermute | solution.py:37
  27.7 1.5 %collective-permute-start.11 = (bf16[640,128]{1,0:T(8,128)(2,1)S(1)}, bf16[640,128]{1,0:T(8,128)(2,1)S(1)}, u32[]{:S(2)}, u32[]{:S(2)}) collective-permute-start(bf16[640,128]{1,0:T(8,128)(2,1)S(1)} %get-tuple-element.70), channel_id=1, source_target_pairs={{0,16},{8,24},{16,0},{24,8},{1,17},{9,25},{17,1},{25,9},{2,18},{10... | collective-permute-start | bytes 491528 | tf_op jit(solution)/shard_map/ppermute | solution.py:27
  32.4 2.9 %collective-permute-done.8 = bf16[64,128]{1,0:T(8,128)(2,1)S(1)} collective-permute-done((bf16[64,128]{1,0:T(8,128)(2,1)S(1)}, bf16[64,128]{1,0:T(8,128)(2,1)S(1)}, u32[]{:S(2)}, u32[]{:S(2)}) %collective-permute-start.8) | collective-permute-done | bytes 16416 | tf_op jit(solution)/shard_map/ppermute | solution.py:37
  36.6 1.5 %collective-permute-done.13.refs_5_ = bf16[8,128,128]{2,1,0:T(8,128)(2,1)S(1)} collective-permute-done((bf16[8,128,128]{2,1,0:T(8,128)(2,1)S(1)}, bf16[8,128,128]{2,1,0:T(8,128)(2,1)S(1)}, u32[]{:S(2)}, u32[]{:S(2)}) %collective-permute-start.13) | collective-permute-done | bytes 262176 | tf_op jit(solution)/shard_map/ppermute | solution.py:42
  38.1 2.3 %shard_map.135 = (f32[20,128,128]{2,1,0:T(8,128)S(1)}, bf16[8,128,128]{2,1,0:T(8,128)(2,1)S(1)}, bf16[8,128,128]{2,1,0:T(8,128)(2,1)S(1)}, bf16[5,128,128]{2,1,0...) custom-call(s32[4,32]{1,0:T(4,128)S(1)} %get-tuple-element.75.refs_0_.slots, ...), custom_call_target="tpu_custom_call" | custom-call | flops 134217728 | bytes 6291456 | tf_op jit(solution)/shard_map/pallas_call | solution.py:50
  42.2 2.6 %collective-permute-start.20 = (bf16[640,128]{1,0:T(8,128)(2,1)S(1)}, bf16[640,128]{1,0:T(8,128)(2,1)S(1)}, u32[]{:S(2)}, u32[]{:S(2)}) collective-permute-start(bf16[640,128]{1,0:T(8,128)(2,1)S(1)} %bitcast.72), channel_id=1, source_target_pairs={{0,24},{8,0},{16,8},{24,16},{1,25},{9,1},{17,9},{25,17},{2,26},{10... | collective-permute-start | bytes 491528 | tf_op jit(solution)/shard_map/ppermute | solution.py:27
  46.3 1.5 %collective-permute-start.16 = (bf16[2,128,128]{2,1,0:T(8,128)(2,1)S(1)}, bf16[2,128,128]{2,1,0:T(8,128)(2,1)S(1)}, u32[]{:S(2)}, u32[]{:S(2)}) collective-permute-start(bf16[2,128,128]{2,1,0:T(8,128)(2,1)S(1)} %get-tuple-element.107), channel_id=1, source_target_pairs={{0,2},{1,3},{2,0},{3,1},{4,6},{5,7},{6,4},{7,5},{8,10},{9,11},{10,... | collective-permute-start | bytes 196616 | tf_op jit(solution)/shard_map/ppermute | solution.py:37
  48.6 2.0 %collective-permute-start.17 = (bf16[2,128,128]{2,1,0:T(8,128)(2,1)S(1)}, bf16[2,128,128]{2,1,0:T(8,128)(2,1)S(1)}, u32[]{:S(2)}, u32[]{:S(2)}) collective-permute-start(bf16[2,128,128]{2,1,0:T(8,128)(2,1)S(1)} %get-tuple-element.106), channel_id=1, source_target_pairs={{0,6},{1,7},{2,4},{3,5},{4,2},{5,3},{6,0},{7,1},{8,14},{9,15},{10,... | collective-permute-start | bytes 196616 | tf_op jit(solution)/shard_map/ppermute | solution.py:37
  52.0 1.9 %collective-permute-start.28 = (bf16[1280,128]{1,0:T(8,128)(2,1)S(1)}, bf16[1280,128]{1,0:T(8,128)(2,1)S(1)}, u32[]{:S(2)}, u32[]{:S(2)}) collective-permute-start(bf16[1280,128]{1,0:T(8,128)(2,1)S(1)} %get-tuple-element.87), channel_id=1, source_target_pairs={{0,24},{8,0},{16,8},{24,16},{1,25},{9,1},{17,9},{25,17},{2,26},{10... | collective-permute-start | bytes 983048 | tf_op jit(solution)/shard_map/ppermute | solution.py:27
  57.5 1.5 %collective-permute-start.22 = (bf16[256,128]{1,0:T(8,128)(2,1)S(1)}, bf16[256,128]{1,0:T(8,128)(2,1)S(1)}, u32[]{:S(2)}, u32[]{:S(2)}) collective-permute-start(bf16[256,128]{1,0:T(8,128)(2,1)S(1)} %fusion.7), channel_id=1, source_target_pairs={{0,2},{1,3},{2,0},{3,1},{4,6},{5,7},{6,4},{7,5},{8,10},{9,11},{10,... | collective-permute-start | bytes 196616 | tf_op jit(solution)/shard_map/ppermute | solution.py:37
  59.1 2.4 %collective-permute-done.21 = bf16[256,128]{1,0:T(8,128)(2,1)S(1)} collective-permute-done((bf16[256,128]{1,0:T(8,128)(2,1)S(1)}, bf16[256,128]{1,0:T(8,128)(2,1)S(1)}, u32[]{:S(2)}, u32[]{:S(2)}) %collective-permute-start.21) | collective-permute-done | bytes 65568 | tf_op jit(solution)/shard_map/ppermute | solution.py:37
  62.8 2.9 %collective-permute-done.23 = bf16[256,128]{1,0:T(8,128)(2,1)S(1)} collective-permute-done((bf16[256,128]{1,0:T(8,128)(2,1)S(1)}, bf16[256,128]{1,0:T(8,128)(2,1)S(1)}, u32[]{:S(2)}, u32[]{:S(2)}) %collective-permute-start.23) | collective-permute-done | bytes 65568 | tf_op jit(solution)/shard_map/ppermute | solution.py:37
  68.2 1.5 %shard_map.137 = f32[20,128,128]{2,1,0:T(8,128)S(1)} custom-call(s32[4,32]{1,0:T(4,128)S(1)} %get-tuple-element.75.refs_0_.slots, bf16[32,128,128]{2,1,0:T(8,128)(2,1)S(1)} %bitcast.81, f32[20,128,128]{2,1,0:T(8,128)S(1)} %get-tuple-element.81.duals, s32[20,128,128]{2,1,0:T(8,128)S(1)} %bitcast.68, bf16[8,128,128]{2,1,0:T(8,128)(2,1)S(1)} %bitcast.71, ...), custom_call_target="tpu_custom_call" | custom-call | tf_op jit(solution)/shard_map/pallas_call | solution.py:50
  69.8 1.6 %shard_map.138 = (f32[2560,128]{1,0:T(8,128)}, f32[2560,128]{1,0:T(8,128)}) custom-call(f32[2560,128]{1,0:T(8,128)S(1)} %bitcast.64, bf16[1280,128]{1,0:T(8,128)(2,1)S(1)} %get-tuple-element.86.refs_1_, bf16[1280,128]{1,0:T(8,128)(2,1)S(1)} %collective-permute-done.28.refs_2_, bf16[1280,128]{1,0:T(8,128)(2,1)S(1)} %collective-permute-done.29.refs_3_, ...), custom_call_target="tpu_custom_call" | custom-call | bytes 3932160 | tf_op jit(solution)/shard_map/pallas_call | solution.py:485
  (84 shorter events, 22.8 us)
Async XLA Ops:
  3.1 15.3 %collective-permute-start.4 = (bf16[1296,128]{1,0:T(8,128)(2,1)}, bf16[1296,128]{1,0:T(8,128)(2,1)S(1)}, u32[]{:S(2)}, u32[]{:S(2)}) collective-permute-start(bf16[1296,128]{1,0:T(8,128)(2,1)} %get-tuple-element.65), channel_id=1, source_target_pairs={{0,8},{8,16},{16,24},{24,0},{1,9},{9,17},{17,25},{25,1},{2,10},{10... | collective-permute-start | bytes 995336 | tf_op jit(solution)/shard_map/ppermute | solution.py:27
  6.1 16.1 %collective-permute-start.5 = (bf16[1296,128]{1,0:T(8,128)(2,1)}, bf16[1296,128]{1,0:T(8,128)(2,1)S(1)}, u32[]{:S(2)}, u32[]{:S(2)}) collective-permute-start(bf16[1296,128]{1,0:T(8,128)(2,1)} %get-tuple-element.66), channel_id=1, source_target_pairs={{0,16},{8,24},{16,0},{24,8},{1,17},{9,25},{17,1},{25,9},{2,18},{10... | collective-permute-start | bytes 995336 | tf_op jit(solution)/shard_map/ppermute | solution.py:27
  7.6 14.8 %collective-permute-start.6 = (bf16[1296,128]{1,0:T(8,128)(2,1)}, bf16[1296,128]{1,0:T(8,128)(2,1)S(1)}, u32[]{:S(2)}, u32[]{:S(2)}) collective-permute-start(bf16[1296,128]{1,0:T(8,128)(2,1)} %get-tuple-element.67), channel_id=1, source_target_pairs={{0,24},{8,0},{16,8},{24,16},{1,25},{9,1},{17,9},{25,17},{2,26},{10... | collective-permute-start | bytes 995336 | tf_op jit(solution)/shard_map/ppermute | solution.py:27
  14.2 9.0 %collective-permute-start.1 = (bf16[2,128,128]{2,1,0:T(8,128)(2,1)S(1)}, bf16[2,128,128]{2,1,0:T(8,128)(2,1)S(1)}, u32[]{:S(2)}, u32[]{:S(2)}) collective-permute-start(bf16[2,128,128]{2,1,0:T(8,128)(2,1)S(1)} %get-tuple-element.111), channel_id=1, source_target_pairs={{0,4},{1,5},{2,6},{3,7},{4,0},{5,1},{6,2},{7,3},{8,12},{9,13},{10,... | collective-permute-start | bytes 196616 | tf_op jit(solution)/shard_map/ppermute | solution.py:37
  16.8 6.3 %collective-permute-start.2 = (bf16[2,128,128]{2,1,0:T(8,128)(2,1)S(1)}, bf16[2,128,128]{2,1,0:T(8,128)(2,1)S(1)}, u32[]{:S(2)}, u32[]{:S(2)}) collective-permute-start(bf16[2,128,128]{2,1,0:T(8,128)(2,1)S(1)} %get-tuple-element.110), channel_id=1, source_target_pairs={{0,2},{1,3},{2,0},{3,1},{4,6},{5,7},{6,4},{7,5},{8,10},{9,11},{10,... | collective-permute-start | bytes 196616 | tf_op jit(solution)/shard_map/ppermute | solution.py:37
  18.4 6.1 %collective-permute-start.3 = (bf16[2,128,128]{2,1,0:T(8,128)(2,1)S(1)}, bf16[2,128,128]{2,1,0:T(8,128)(2,1)S(1)}, u32[]{:S(2)}, u32[]{:S(2)}) collective-permute-start(bf16[2,128,128]{2,1,0:T(8,128)(2,1)S(1)} %get-tuple-element.109), channel_id=1, source_target_pairs={{0,6},{1,7},{2,4},{3,5},{4,2},{5,3},{6,0},{7,1},{8,14},{9,15},{10,... | collective-permute-start | bytes 196616 | tf_op jit(solution)/shard_map/ppermute | solution.py:37
  24.6 5.7 %collective-permute-start.7 = (bf16[256,128]{1,0:T(8,128)(2,1)S(1)}, bf16[256,128]{1,0:T(8,128)(2,1)S(1)}, u32[]{:S(2)}, u32[]{:S(2)}) collective-permute-start(bf16[256,128]{1,0:T(8,128)(2,1)S(1)} %fusion.8), channel_id=1, source_target_pairs={{0,4},{1,5},{2,6},{3,7},{4,0},{5,1},{6,2},{7,3},{8,12},{9,13},{10,... | collective-permute-start | bytes 196616 | tf_op jit(solution)/shard_map/ppermute | solution.py:37
  26.3 9.0 %collective-permute-start.10 = (bf16[640,128]{1,0:T(8,128)(2,1)S(1)}, bf16[640,128]{1,0:T(8,128)(2,1)S(1)}, u32[]{:S(2)}, u32[]{:S(2)}) collective-permute-start(bf16[640,128]{1,0:T(8,128)(2,1)S(1)} %get-tuple-element.69), channel_id=1, source_target_pairs={{0,24},{8,0},{16,8},{24,16},{1,25},{9,1},{17,9},{25,17},{2,26},{10... | collective-permute-start | bytes 491528 | tf_op jit(solution)/shard_map/ppermute | solution.py:27
  27.7 8.8 %collective-permute-start.11 = (bf16[640,128]{1,0:T(8,128)(2,1)S(1)}, bf16[640,128]{1,0:T(8,128)(2,1)S(1)}, u32[]{:S(2)}, u32[]{:S(2)}) collective-permute-start(bf16[640,128]{1,0:T(8,128)(2,1)S(1)} %get-tuple-element.70), channel_id=1, source_target_pairs={{0,16},{8,24},{16,0},{24,8},{1,17},{9,25},{17,1},{25,9},{2,18},{10... | collective-permute-start | bytes 491528 | tf_op jit(solution)/shard_map/ppermute | solution.py:27
  29.2 7.3 %collective-permute-start.12 = (bf16[640,128]{1,0:T(8,128)(2,1)S(1)}, bf16[640,128]{1,0:T(8,128)(2,1)S(1)}, u32[]{:S(2)}, u32[]{:S(2)}) collective-permute-start(bf16[640,128]{1,0:T(8,128)(2,1)S(1)} %get-tuple-element.71), channel_id=1, source_target_pairs={{0,8},{8,16},{16,24},{24,0},{1,9},{9,17},{17,25},{25,1},{2,10},{10... | collective-permute-start | bytes 491528 | tf_op jit(solution)/shard_map/ppermute | solution.py:27
  30.3 6.2 %collective-permute-start.9 = (bf16[448,128]{1,0:T(8,128)(2,1)S(1)}, bf16[448,128]{1,0:T(8,128)(2,1)S(1)}, u32[]{:S(2)}, u32[]{:S(2)}) collective-permute-start(bf16[448,128]{1,0:T(8,128)(2,1)S(1)} %pad_maximum_fusion.2), channel_id=1, source_target_pairs={{0,2},{1,3},{2,0},{3,1},{4,6},{5,7},{6,4},{7,5},{8,10},{9,11},{10,... | collective-permute-start | bytes 344072 | tf_op jit(solution)/shard_map/ppermute | solution.py:37
  40.4 4.4 %collective-permute-start.14 = (bf16[8,128,128]{2,1,0:T(8,128)(2,1)S(1)}, bf16[8,128,128]{2,1,0:T(8,128)(2,1)S(1)}, u32[]{:S(2)}, u32[]{:S(2)}) collective-permute-start(bf16[8,128,128]{2,1,0:T(8,128)(2,1)S(1)} %get-tuple-element.80), channel_id=1, source_target_pairs={{0,1},{1,0},{2,3},{3,2},{4,5},{5,4},{6,7},{7,6},{8,9},{9,8},{10,11... | collective-permute-start | bytes 786440 | tf_op jit(solution)/shard_map/ppermute | solution.py:42
  40.6 8.0 %collective-permute-start.18 = (bf16[640,128]{1,0:T(8,128)(2,1)S(1)}, bf16[640,128]{1,0:T(8,128)(2,1)S(1)}, u32[]{:S(2)}, u32[]{:S(2)}) collective-permute-start(bf16[640,128]{1,0:T(8,128)(2,1)S(1)} %bitcast.74), channel_id=1, source_target_pairs={{0,8},{8,16},{16,24},{24,0},{1,9},{9,17},{17,25},{25,1},{2,10},{10... | collective-permute-start | bytes 491528 | tf_op jit(solution)/shard_map/ppermute | solution.py:27
  41.2 9.7 %collective-permute-start.19 = (bf16[640,128]{1,0:T(8,128)(2,1)S(1)}, bf16[640,128]{1,0:T(8,128)(2,1)S(1)}, u32[]{:S(2)}, u32[]{:S(2)}) collective-permute-start(bf16[640,128]{1,0:T(8,128)(2,1)S(1)} %bitcast.73), channel_id=1, source_target_pairs={{0,16},{8,24},{16,0},{24,8},{1,17},{9,25},{17,1},{25,9},{2,18},{10... | collective-permute-start | bytes 491528 | tf_op jit(solution)/shard_map/ppermute | solution.py:27
  42.2 9.1 %collective-permute-start.20 = (bf16[640,128]{1,0:T(8,128)(2,1)S(1)}, bf16[640,128]{1,0:T(8,128)(2,1)S(1)}, u32[]{:S(2)}, u32[]{:S(2)}) collective-permute-start(bf16[640,128]{1,0:T(8,128)(2,1)S(1)} %bitcast.72), channel_id=1, source_target_pairs={{0,24},{8,0},{16,8},{24,16},{1,25},{9,1},{17,9},{25,17},{2,26},{10... | collective-permute-start | bytes 491528 | tf_op jit(solution)/shard_map/ppermute | solution.py:27
  44.9 10.3 %collective-permute-start.15 = (bf16[2,128,128]{2,1,0:T(8,128)(2,1)S(1)}, bf16[2,128,128]{2,1,0:T(8,128)(2,1)S(1)}, u32[]{:S(2)}, u32[]{:S(2)}) collective-permute-start(bf16[2,128,128]{2,1,0:T(8,128)(2,1)S(1)} %get-tuple-element.108), channel_id=1, source_target_pairs={{0,4},{1,5},{2,6},{3,7},{4,0},{5,1},{6,2},{7,3},{8,12},{9,13},{10,... | collective-permute-start | bytes 196616 | tf_op jit(solution)/shard_map/ppermute | solution.py:37
  46.3 9.0 %collective-permute-start.16 = (bf16[2,128,128]{2,1,0:T(8,128)(2,1)S(1)}, bf16[2,128,128]{2,1,0:T(8,128)(2,1)S(1)}, u32[]{:S(2)}, u32[]{:S(2)}) collective-permute-start(bf16[2,128,128]{2,1,0:T(8,128)(2,1)S(1)} %get-tuple-element.107), channel_id=1, source_target_pairs={{0,2},{1,3},{2,0},{3,1},{4,6},{5,7},{6,4},{7,5},{8,10},{9,11},{10,... | collective-permute-start | bytes 196616 | tf_op jit(solution)/shard_map/ppermute | solution.py:37
  48.6 6.7 %collective-permute-start.17 = (bf16[2,128,128]{2,1,0:T(8,128)(2,1)S(1)}, bf16[2,128,128]{2,1,0:T(8,128)(2,1)S(1)}, u32[]{:S(2)}, u32[]{:S(2)}) collective-permute-start(bf16[2,128,128]{2,1,0:T(8,128)(2,1)S(1)} %get-tuple-element.106), channel_id=1, source_target_pairs={{0,6},{1,7},{2,4},{3,5},{4,2},{5,3},{6,0},{7,1},{8,14},{9,15},{10,... | collective-permute-start | bytes 196616 | tf_op jit(solution)/shard_map/ppermute | solution.py:37
  52.0 17.8 %collective-permute-start.28 = (bf16[1280,128]{1,0:T(8,128)(2,1)S(1)}, bf16[1280,128]{1,0:T(8,128)(2,1)S(1)}, u32[]{:S(2)}, u32[]{:S(2)}) collective-permute-start(bf16[1280,128]{1,0:T(8,128)(2,1)S(1)} %get-tuple-element.87), channel_id=1, source_target_pairs={{0,24},{8,0},{16,8},{24,16},{1,25},{9,1},{17,9},{25,17},{2,26},{10... | collective-permute-start | bytes 983048 | tf_op jit(solution)/shard_map/ppermute | solution.py:27
  54.0 15.9 %collective-permute-start.29 = (bf16[1280,128]{1,0:T(8,128)(2,1)S(1)}, bf16[1280,128]{1,0:T(8,128)(2,1)S(1)}, u32[]{:S(2)}, u32[]{:S(2)}) collective-permute-start(bf16[1280,128]{1,0:T(8,128)(2,1)S(1)} %get-tuple-element.88), channel_id=1, source_target_pairs={{0,16},{8,24},{16,0},{24,8},{1,17},{9,25},{17,1},{25,9},{2,18},{10... | collective-permute-start | bytes 983048 | tf_op jit(solution)/shard_map/ppermute | solution.py:27
  55.2 14.6 %collective-permute-start.30 = (bf16[1280,128]{1,0:T(8,128)(2,1)S(1)}, bf16[1280,128]{1,0:T(8,128)(2,1)S(1)}, u32[]{:S(2)}, u32[]{:S(2)}) collective-permute-start(bf16[1280,128]{1,0:T(8,128)(2,1)S(1)} %get-tuple-element.89), channel_id=1, source_target_pairs={{0,8},{8,16},{16,24},{24,0},{1,9},{9,17},{17,25},{25,1},{2,10},{10... | collective-permute-start | bytes 983048 | tf_op jit(solution)/shard_map/ppermute | solution.py:27
  56.2 5.3 %collective-permute-start.21 = (bf16[256,128]{1,0:T(8,128)(2,1)S(1)}, bf16[256,128]{1,0:T(8,128)(2,1)S(1)}, u32[]{:S(2)}, u32[]{:S(2)}) collective-permute-start(bf16[256,128]{1,0:T(8,128)(2,1)S(1)} %fusion.7), channel_id=1, source_target_pairs={{0,4},{1,5},{2,6},{3,7},{4,0},{5,1},{6,2},{7,3},{8,12},{9,13},{10,... | collective-permute-start | bytes 196616 | tf_op jit(solution)/shard_map/ppermute | solution.py:37
  57.5 5.3 %collective-permute-start.22 = (bf16[256,128]{1,0:T(8,128)(2,1)S(1)}, bf16[256,128]{1,0:T(8,128)(2,1)S(1)}, u32[]{:S(2)}, u32[]{:S(2)}) collective-permute-start(bf16[256,128]{1,0:T(8,128)(2,1)S(1)} %fusion.7), channel_id=1, source_target_pairs={{0,2},{1,3},{2,0},{3,1},{4,6},{5,7},{6,4},{7,5},{8,10},{9,11},{10,... | collective-permute-start | bytes 196616 | tf_op jit(solution)/shard_map/ppermute | solution.py:37
  61.5 4.3 %collective-permute-start.23 = (bf16[256,128]{1,0:T(8,128)(2,1)S(1)}, bf16[256,128]{1,0:T(8,128)(2,1)S(1)}, u32[]{:S(2)}, u32[]{:S(2)}) collective-permute-start(bf16[256,128]{1,0:T(8,128)(2,1)S(1)} %collective-permute-done.21), channel_id=1, source_target_pairs={{0,2},{1,3},{2,0},{3,1},{4,6},{5,7},{6,4},{7,5},{8,10},{9,11},{10,... | collective-permute-start | bytes 196616 | tf_op jit(solution)/shard_map/ppermute | solution.py:37
  (18 other events, 116.3 us)

commit v7 on v6

--- a/solution.py
+++ b/solution.py
@@ -201,16 +201,23 @@
     give_partials(partials, keep, send)
 
 
-def push_kernel(slots, tiles, duals, demand, *refs):
-    parts_of, (base, blocks, acc) = refs[:-3], refs[-3:]
+def push_kernel(slots, tiles, duals, demand, now, pulled, cost, *refs):
+    parts_of, (base, flows_out, blocks) = refs[:-3], refs[-3:]
+    tile = now.shape[1]
+    eye = eye_of(tile)
+    for i in range(now.shape[0] // tile):
+        rows = slice(i * tile, (i + 1) * tile)
+        prices = jnp.sum(jnp.where(eye, cost[:, rows], 0.0), axis=1, keepdims=True)
+        flows_out[rows, :] = jnp.maximum(
+            now[rows, :] - STEP_PRIMAL * (prices - pulled[rows, :]), 0.0
+        )
     first = 0
     for part in parts_of:
         blocks[first : first + part.shape[0]] = part[...]
         first += part.shape[0]
-    n = base.shape[0]
-    acc[0:n] = duals[...] + (STEP_DUAL * 0.25) * demand[...].astype(F32)
-    push_slots(slots, tiles, blocks, acc)
-    base[...] = acc[0:n]
+    n = duals.shape[0]
+    base[0:n] = duals[...] + (STEP_DUAL * 0.25) * demand[...].astype(F32)
+    push_slots(slots, tiles, blocks, base)
 
 
 def final_kernel(parts, size, *refs):
@@ -464,19 +471,24 @@
     send = swap_core(send)
     pulled = collect(keep, send, outs)
     outs = [outs[0]] + [rotate(outs[r], "section", -r) for r in range(1, parts)]
-    flows2_out, bar2 = step_flows(flows1, pulled)
-    bar2, flows2_out = lax.optimization_barrier((bar2, flows2_out))
+    unused, bar2 = step_flows(flows1, pulled)
     near, *far = spread(bar2, [], pieces=4)
-    base = call(
+    base, flows2_out = call(
         push_kernel,
-        jax.ShapeDtypeStruct((band_tiles, tile, scenarios), F32),
-        push_scratch,
+        [
+            jax.ShapeDtypeStruct((band_tiles + 1, tile, scenarios), F32),
+            jax.ShapeDtypeStruct(flows2.shape, F32),
+        ],
+        push_scratch[:1],
         0,
         0,
         slots_of,
         tiles,
         duals1,
         demand3,
+        flows1,
+        pulled,
+        flow_cost,
         near,
         *far,
         smem=1,
@@ -493,7 +505,7 @@
         cost_estimate=pl.CostEstimate(
             flops=0, bytes_accessed=12 * rows * scenarios, transcendentals=0
         ),
-    )(base.reshape(rows, scenarios), *outs)
+    )(base.reshape(rows + tile, scenarios), *outs)
     return (
         flows2_out.reshape(flows.shape),
         stock_out.reshape(stock.shape),

time: 71.6 us -> 71.4 us (level)
    max x1 -> x0, other arithmetic: 0.76 us -> none  [step_flows(): new = jnp.maximum(now - STEP_PRIMAL * (flow_cost[0][:, None] - pulled), 0.0)]
  transfers between devices with their start and end apart: 31 -> 31, of which waited for: 15 -> 15; matrix products, arithmetic and copies ran while one was open for 2% -> 1% of each run, Pallas kernels for 9% -> 9%
where the time goes in v7:
time: 71.4 us; the launch traced here: 71.3 us
  starting transfers between devices  36.3 us (51%)
  waiting for transfers between devices  20.3 us (28%)
  Pallas kernels  12.9 us (18%)
  between operations  0.96 us (1%)
    ppermute x12, starting transfers between devices, flip_chip(): lax.ppermute(value, 'zone', [(i, i ^ by * CORES) for i in range(size)])  18.7 us
    ppermute x12, starting transfers between devices, rotate(): lax.ppermute(value, axis, [(i, (i + by) % size) for i in range(size)])  16.5 us
    ppermute x12, waiting for transfers between devices, flip_chip(): lax.ppermute(value, 'zone', [(i, i ^ by * CORES) for i in range(size)])  10.4 us
    pallas_call x4, Pallas kernels, call(): pl.pallas_call(kernel, out_shape=outs, in_specs=[SMEM] * smem + [VMEM] *...  5.67 us
    ppermute x12, waiting for transfers between devices, rotate(): lax.ppermute(value, axis, [(i, (i + by) % size) for i in range(size)])  5.12 us
    ppermute x7, waiting for transfers between devices, swap_core(): return lax.ppermute(value, 'zone', [(i, i ^ 1) for i in range(size)])  4.81 us
    pallas_call x1, Pallas kernels, first_pull(): pl.pallas_call(functools.partial(first_pull_kernel, shape), out_shape=[ha...  3.24 us
    pallas_call x1, Pallas kernels, per_device(): pl.pallas_call(functools.partial(pack_kernel, parts, size), out_shape=pac...  2.41 us
  transfers between devices with their start and end apart: 31, of which 15 were waited for; matrix products, arithmetic and copies ran while one was open for 1% of the time, Pallas kernels for 9%

profile of v7, /device:TPU:0, one launch (start us, length us, event | category | flops | bytes accessed | tf_op | source)
XLA Modules:
  0.0 71.3 jit_solution(12631017066357634456)
XLA Ops:
  0.7 2.4 %shard_map.133 = (bf16[1296,128]{1,0:T(8,128)(2,1)}, bf16[1296,128]{1,0:T(8,128)(2,1)}, bf16[1296,128]{1,0:T(8,128)(2,1)}) custom-call(f32[2560,128]{1,0:T(8,128)} %bitcast.58, f32[2560,128]{1,0:T(8,128)} %bitcast.42, f32[1,2560]{1,0:T(1,128)} %refs_1_.1), custom_call_target="tpu_custom_call" | custom-call | bytes 3932160 | tf_op jit(solution)/shard_map/pallas_call | solution.py:390
  3.1 3.0 %collective-permute-start.4 = (bf16[1296,128]{1,0:T(8,128)(2,1)}, bf16[1296,128]{1,0:T(8,128)(2,1)S(1)}, u32[]{:S(2)}, u32[]{:S(2)}) collective-permute-start(bf16[1296,128]{1,0:T(8,128)(2,1)} %get-tuple-element.66), channel_id=1, source_target_pairs={{0,8},{8,16},{16,24},{24,0},{1,9},{9,17},{17,25},{25,1},{2,10},{10... | collective-permute-start | bytes 995336 | tf_op jit(solution)/shard_map/ppermute | solution.py:27
  6.1 1.5 %collective-permute-start.5 = (bf16[1296,128]{1,0:T(8,128)(2,1)}, bf16[1296,128]{1,0:T(8,128)(2,1)S(1)}, u32[]{:S(2)}, u32[]{:S(2)}) collective-permute-start(bf16[1296,128]{1,0:T(8,128)(2,1)} %get-tuple-element.67), channel_id=1, source_target_pairs={{0,16},{8,24},{16,0},{24,8},{1,17},{9,25},{17,1},{25,9},{2,18},{10... | collective-permute-start | bytes 995336 | tf_op jit(solution)/shard_map/ppermute | solution.py:27
  9.1 4.9 %conditional.1 = (s32[4,32]{1,0:T(4,128)S(1)}, f32[8,128,128]{2,1,0:T(8,128)S(1)}, f32[8,128,128]{2,1,0:T(8,128)S(1)}) conditional(s32[]{:T(128)} %bitcast, () %tuple.24, (s32[1,32]{1,0:T(1,128)S(1)}, s32[1,32]{1,0:T(1,128)S(1)}, s32[1,32]{1,0:T(1,128)S(1)}, s32[16]{0:T(128)S(1)}, bf16[32,128,128]{2,1,0:T(8,128)(2,1)}, ...), branch_computations={%region_0.0_spmd, %region_1.0_spmd} | conditional | flops 262144 | bytes 2621504 | solution.py:349
  9.1 3.2 %branch_1_fun.1 = (bf16[8,128,128]{2,1,0:T(8,128)(2,1)S(1)}, bf16[8,128,128]{2,1,0:T(8,128)(2,1)S(1)}, s32[4,32]{1,0:T(4,128)S(1)}) custom-call(s32[1,32]{1,0:T(1,128)S(1)} %get-tuple-element.103.row, s32[1,32]{1,0:T(1,128)S(1)} %get-tuple-element.104.col, s32[1,32]{1,0:T(1,128)S(1)} %get-tuple-element.105.live, s32[16]{0:T(128)S(1)} %get-tuple-element.17.place, ...), custom_call_target="tpu_custom_call" | custom-call | tf_op jit(solution)/shard_map/cond/branch_1_fun/pallas_call | solution.py:426
  12.5 1.5 %collective-permute-done = bf16[8,128,128]{2,1,0:T(8,128)(2,1)S(1)} collective-permute-done((bf16[8,128,128]{2,1,0:T(8,128)(2,1)S(1)}, bf16[8,128,128]{2,1,0:T(8,128)(2,1)S(1)}, u32[]{:S(2)}, u32[]{:S(2)}) %collective-permute-start) | collective-permute-done | bytes 262176 | tf_op jit(solution)/shard_map/cond/branch_1_fun/ppermute | solution.py:42
  14.2 2.7 %collective-permute-start.1 = (bf16[2,128,128]{2,1,0:T(8,128)(2,1)S(1)}, bf16[2,128,128]{2,1,0:T(8,128)(2,1)S(1)}, u32[]{:S(2)}, u32[]{:S(2)}) collective-permute-start(bf16[2,128,128]{2,1,0:T(8,128)(2,1)S(1)} %get-tuple-element.115), channel_id=1, source_target_pairs={{0,4},{1,5},{2,6},{3,7},{4,0},{5,1},{6,2},{7,3},{8,12},{9,13},{10,... | collective-permute-start | bytes 196616 | tf_op jit(solution)/shard_map/ppermute | solution.py:37
  16.8 1.6 %collective-permute-start.2 = (bf16[2,128,128]{2,1,0:T(8,128)(2,1)S(1)}, bf16[2,128,128]{2,1,0:T(8,128)(2,1)S(1)}, u32[]{:S(2)}, u32[]{:S(2)}) collective-permute-start(bf16[2,128,128]{2,1,0:T(8,128)(2,1)S(1)} %get-tuple-element.114), channel_id=1, source_target_pairs={{0,2},{1,3},{2,0},{3,1},{4,6},{5,7},{6,4},{7,5},{8,10},{9,11},{10,... | collective-permute-start | bytes 196616 | tf_op jit(solution)/shard_map/ppermute | solution.py:37
  18.4 1.6 %collective-permute-start.3 = (bf16[2,128,128]{2,1,0:T(8,128)(2,1)S(1)}, bf16[2,128,128]{2,1,0:T(8,128)(2,1)S(1)}, u32[]{:S(2)}, u32[]{:S(2)}) collective-permute-start(bf16[2,128,128]{2,1,0:T(8,128)(2,1)S(1)} %get-tuple-element.113), channel_id=1, source_target_pairs={{0,6},{1,7},{2,4},{3,5},{4,2},{5,3},{6,0},{7,1},{8,14},{9,15},{10,... | collective-permute-start | bytes 196616 | tf_op jit(solution)/shard_map/ppermute | solution.py:37
  20.0 2.1 %collective-permute-done.5.refs_4_.refs_3_ = bf16[1296,128]{1,0:T(8,128)(2,1)S(1)} collective-permute-done((bf16[1296,128]{1,0:T(8,128)(2,1)}, bf16[1296,128]{1,0:T(8,128)(2,1)S(1)}, u32[]{:S(2)}, u32[]{:S(2)}) %collective-permute-start.5) | collective-permute-done | bytes 331808 | tf_op jit(solution)/shard_map/ppermute | solution.py:27
  24.6 1.7 %collective-permute-start.7 = (bf16[256,128]{1,0:T(8,128)(2,1)S(1)}, bf16[256,128]{1,0:T(8,128)(2,1)S(1)}, u32[]{:S(2)}, u32[]{:S(2)}) collective-permute-start(bf16[256,128]{1,0:T(8,128)(2,1)S(1)} %get-tuple-element.108), channel_id=1, source_target_pairs={{0,4},{1,5},{2,6},{3,7},{4,0},{5,1},{6,2},{7,3},{8,12},{9,13},{10,... | collective-permute-start | bytes 196616 | tf_op jit(solution)/shard_map/ppermute | solution.py:37
  27.7 1.5 %collective-permute-start.11 = (bf16[640,128]{1,0:T(8,128)(2,1)S(1)}, bf16[640,128]{1,0:T(8,128)(2,1)S(1)}, u32[]{:S(2)}, u32[]{:S(2)}) collective-permute-start(bf16[640,128]{1,0:T(8,128)(2,1)S(1)} %get-tuple-element.71), channel_id=1, source_target_pairs={{0,16},{8,24},{16,0},{24,8},{1,17},{9,25},{17,1},{25,9},{2,18},{10... | collective-permute-start | bytes 491528 | tf_op jit(solution)/shard_map/ppermute | solution.py:27
  32.4 2.9 %collective-permute-done.8 = bf16[64,128]{1,0:T(8,128)(2,1)S(1)} collective-permute-done((bf16[64,128]{1,0:T(8,128)(2,1)S(1)}, bf16[64,128]{1,0:T(8,128)(2,1)S(1)}, u32[]{:S(2)}, u32[]{:S(2)}) %collective-permute-start.8) | collective-permute-done | bytes 16416 | tf_op jit(solution)/shard_map/ppermute | solution.py:37
  36.6 1.5 %collective-permute-done.13.refs_5_ = bf16[8,128,128]{2,1,0:T(8,128)(2,1)S(1)} collective-permute-done((bf16[8,128,128]{2,1,0:T(8,128)(2,1)S(1)}, bf16[8,128,128]{2,1,0:T(8,128)(2,1)S(1)}, u32[]{:S(2)}, u32[]{:S(2)}) %collective-permute-start.13) | collective-permute-done | bytes 262176 | tf_op jit(solution)/shard_map/ppermute | solution.py:42
  38.1 2.3 %shard_map.135 = (f32[20,128,128]{2,1,0:T(8,128)S(1)}, bf16[8,128,128]{2,1,0:T(8,128)(2,1)S(1)}, bf16[8,128,128]{2,1,0:T(8,128)(2,1)S(1)}, bf16[5,128,128]{2,1,0...) custom-call(s32[4,32]{1,0:T(4,128)S(1)} %get-tuple-element.63.refs_0_.slots, ...), custom_call_target="tpu_custom_call" | custom-call | flops 134217728 | bytes 6291456 | tf_op jit(solution)/shard_map/pallas_call | solution.py:50
  42.2 2.6 %collective-permute-start.20 = (bf16[640,128]{1,0:T(8,128)(2,1)S(1)}, bf16[640,128]{1,0:T(8,128)(2,1)S(1)}, u32[]{:S(2)}, u32[]{:S(2)}) collective-permute-start(bf16[640,128]{1,0:T(8,128)(2,1)S(1)} %bitcast.55), channel_id=1, source_target_pairs={{0,24},{8,0},{16,8},{24,16},{1,25},{9,1},{17,9},{25,17},{2,26},{10... | collective-permute-start | bytes 491528 | tf_op jit(solution)/shard_map/ppermute | solution.py:27
  46.3 1.5 %collective-permute-start.16 = (bf16[2,128,128]{2,1,0:T(8,128)(2,1)S(1)}, bf16[2,128,128]{2,1,0:T(8,128)(2,1)S(1)}, u32[]{:S(2)}, u32[]{:S(2)}) collective-permute-start(bf16[2,128,128]{2,1,0:T(8,128)(2,1)S(1)} %get-tuple-element.111), channel_id=1, source_target_pairs={{0,2},{1,3},{2,0},{3,1},{4,6},{5,7},{6,4},{7,5},{8,10},{9,11},{10,... | collective-permute-start | bytes 196616 | tf_op jit(solution)/shard_map/ppermute | solution.py:37
  48.6 2.0 %collective-permute-start.17 = (bf16[2,128,128]{2,1,0:T(8,128)(2,1)S(1)}, bf16[2,128,128]{2,1,0:T(8,128)(2,1)S(1)}, u32[]{:S(2)}, u32[]{:S(2)}) collective-permute-start(bf16[2,128,128]{2,1,0:T(8,128)(2,1)S(1)} %get-tuple-element.110), channel_id=1, source_target_pairs={{0,6},{1,7},{2,4},{3,5},{4,2},{5,3},{6,0},{7,1},{8,14},{9,15},{10,... | collective-permute-start | bytes 196616 | tf_op jit(solution)/shard_map/ppermute | solution.py:37
  52.0 1.9 %collective-permute-start.28 = (bf16[1280,128]{1,0:T(8,128)(2,1)S(1)}, bf16[1280,128]{1,0:T(8,128)(2,1)S(1)}, u32[]{:S(2)}, u32[]{:S(2)}) collective-permute-start(bf16[1280,128]{1,0:T(8,128)(2,1)S(1)} %get-tuple-element.87), channel_id=1, source_target_pairs={{0,24},{8,0},{16,8},{24,16},{1,25},{9,1},{17,9},{25,17},{2,26},{10... | collective-permute-start | bytes 983048 | tf_op jit(solution)/shard_map/ppermute | solution.py:27
  56.8 1.5 %collective-permute-start.22 = (bf16[256,128]{1,0:T(8,128)(2,1)S(1)}, bf16[256,128]{1,0:T(8,128)(2,1)S(1)}, u32[]{:S(2)}, u32[]{:S(2)}) collective-permute-start(bf16[256,128]{1,0:T(8,128)(2,1)S(1)} %fusion.4), channel_id=1, source_target_pairs={{0,2},{1,3},{2,0},{3,1},{4,6},{5,7},{6,4},{7,5},{8,10},{9,11},{10,... | collective-permute-start | bytes 196616 | tf_op jit(solution)/shard_map/ppermute | solution.py:37
  58.4 2.4 %collective-permute-done.21 = bf16[256,128]{1,0:T(8,128)(2,1)S(1)} collective-permute-done((bf16[256,128]{1,0:T(8,128)(2,1)S(1)}, bf16[256,128]{1,0:T(8,128)(2,1)S(1)}, u32[]{:S(2)}, u32[]{:S(2)}) %collective-permute-start.21) | collective-permute-done | bytes 65568 | tf_op jit(solution)/shard_map/ppermute | solution.py:37
  62.1 2.9 %collective-permute-done.23 = bf16[256,128]{1,0:T(8,128)(2,1)S(1)} collective-permute-done((bf16[256,128]{1,0:T(8,128)(2,1)S(1)}, bf16[256,128]{1,0:T(8,128)(2,1)S(1)}, u32[]{:S(2)}, u32[]{:S(2)}) %collective-permute-start.23) | collective-permute-done | bytes 65568 | tf_op jit(solution)/shard_map/ppermute | solution.py:37
  67.5 2.1 %shard_map.137 = (f32[21,128,128]{2,1,0:T(8,128)S(1)}, f32[256,128]{1,0:T(8,128)}) custom-call(s32[4,32]{1,0:T(4,128)S(1)} %get-tuple-element.63.refs_0_.slots, bf16[32,128,128]{2,1,0:T(8,128)(2,1)S(1)} %bitcast.64, f32[20,128,128]{2,1,0:T(8,128)S(1)} %get-tuple-element.79.duals, s32[20,128,128]{2,1,0:T(8,128)S(1)} %bitcast.46, ...), custom_call_target="tpu_custom_call" | custom-call | tf_op jit(solution)/shard_map/pallas_call | solution.py:50
  69.7 1.6 %shard_map.138 = (f32[2560,128]{1,0:T(8,128)}, f32[2560,128]{1,0:T(8,128)}) custom-call(f32[2688,128]{1,0:T(8,128)S(1)} %bitcast.47, bf16[1280,128]{1,0:T(8,128)(2,1)S(1)} %get-tuple-element.86.refs_1_, bf16[1280,128]{1,0:T(8,128)(2,1)S(1)} %collective-permute-done.28.refs_2_, bf16[1280,128]{1,0:T(8,128)(2,1)S(1)} %collective-permute-done.29.refs_3_, ...), custom_call_target="tpu_custom_call" | custom-call | bytes 3932160 | tf_op jit(solution)/shard_map/pallas_call | solution.py:497
  (83 shorter events, 22.1 us)
Async XLA Ops:
  3.1 15.3 %collective-permute-start.4 = (bf16[1296,128]{1,0:T(8,128)(2,1)}, bf16[1296,128]{1,0:T(8,128)(2,1)S(1)}, u32[]{:S(2)}, u32[]{:S(2)}) collective-permute-start(bf16[1296,128]{1,0:T(8,128)(2,1)} %get-tuple-element.66), channel_id=1, source_target_pairs={{0,8},{8,16},{16,24},{24,0},{1,9},{9,17},{17,25},{25,1},{2,10},{10... | collective-permute-start | bytes 995336 | tf_op jit(solution)/shard_map/ppermute | solution.py:27
  6.1 16.1 %collective-permute-start.5 = (bf16[1296,128]{1,0:T(8,128)(2,1)}, bf16[1296,128]{1,0:T(8,128)(2,1)S(1)}, u32[]{:S(2)}, u32[]{:S(2)}) collective-permute-start(bf16[1296,128]{1,0:T(8,128)(2,1)} %get-tuple-element.67), channel_id=1, source_target_pairs={{0,16},{8,24},{16,0},{24,8},{1,17},{9,25},{17,1},{25,9},{2,18},{10... | collective-permute-start | bytes 995336 | tf_op jit(solution)/shard_map/ppermute | solution.py:27
  7.6 14.8 %collective-permute-start.6 = (bf16[1296,128]{1,0:T(8,128)(2,1)}, bf16[1296,128]{1,0:T(8,128)(2,1)S(1)}, u32[]{:S(2)}, u32[]{:S(2)}) collective-permute-start(bf16[1296,128]{1,0:T(8,128)(2,1)} %get-tuple-element.68), channel_id=1, source_target_pairs={{0,24},{8,0},{16,8},{24,16},{1,25},{9,1},{17,9},{25,17},{2,26},{10... | collective-permute-start | bytes 995336 | tf_op jit(solution)/shard_map/ppermute | solution.py:27
  14.2 9.0 %collective-permute-start.1 = (bf16[2,128,128]{2,1,0:T(8,128)(2,1)S(1)}, bf16[2,128,128]{2,1,0:T(8,128)(2,1)S(1)}, u32[]{:S(2)}, u32[]{:S(2)}) collective-permute-start(bf16[2,128,128]{2,1,0:T(8,128)(2,1)S(1)} %get-tuple-element.115), channel_id=1, source_target_pairs={{0,4},{1,5},{2,6},{3,7},{4,0},{5,1},{6,2},{7,3},{8,12},{9,13},{10,... | collective-permute-start | bytes 196616 | tf_op jit(solution)/shard_map/ppermute | solution.py:37
  16.8 6.3 %collective-permute-start.2 = (bf16[2,128,128]{2,1,0:T(8,128)(2,1)S(1)}, bf16[2,128,128]{2,1,0:T(8,128)(2,1)S(1)}, u32[]{:S(2)}, u32[]{:S(2)}) collective-permute-start(bf16[2,128,128]{2,1,0:T(8,128)(2,1)S(1)} %get-tuple-element.114), channel_id=1, source_target_pairs={{0,2},{1,3},{2,0},{3,1},{4,6},{5,7},{6,4},{7,5},{8,10},{9,11},{10,... | collective-permute-start | bytes 196616 | tf_op jit(solution)/shard_map/ppermute | solution.py:37
  18.4 6.1 %collective-permute-start.3 = (bf16[2,128,128]{2,1,0:T(8,128)(2,1)S(1)}, bf16[2,128,128]{2,1,0:T(8,128)(2,1)S(1)}, u32[]{:S(2)}, u32[]{:S(2)}) collective-permute-start(bf16[2,128,128]{2,1,0:T(8,128)(2,1)S(1)} %get-tuple-element.113), channel_id=1, source_target_pairs={{0,6},{1,7},{2,4},{3,5},{4,2},{5,3},{6,0},{7,1},{8,14},{9,15},{10,... | collective-permute-start | bytes 196616 | tf_op jit(solution)/shard_map/ppermute | solution.py:37
  24.6 5.7 %collective-permute-start.7 = (bf16[256,128]{1,0:T(8,128)(2,1)S(1)}, bf16[256,128]{1,0:T(8,128)(2,1)S(1)}, u32[]{:S(2)}, u32[]{:S(2)}) collective-permute-start(bf16[256,128]{1,0:T(8,128)(2,1)S(1)} %get-tuple-element.108), channel_id=1, source_target_pairs={{0,4},{1,5},{2,6},{3,7},{4,0},{5,1},{6,2},{7,3},{8,12},{9,13},{10,... | collective-permute-start | bytes 196616 | tf_op jit(solution)/shard_map/ppermute | solution.py:37
  26.3 9.0 %collective-permute-start.10 = (bf16[640,128]{1,0:T(8,128)(2,1)S(1)}, bf16[640,128]{1,0:T(8,128)(2,1)S(1)}, u32[]{:S(2)}, u32[]{:S(2)}) collective-permute-start(bf16[640,128]{1,0:T(8,128)(2,1)S(1)} %get-tuple-element.70), channel_id=1, source_target_pairs={{0,24},{8,0},{16,8},{24,16},{1,25},{9,1},{17,9},{25,17},{2,26},{10... | collective-permute-start | bytes 491528 | tf_op jit(solution)/shard_map/ppermute | solution.py:27
  27.7 8.8 %collective-permute-start.11 = (bf16[640,128]{1,0:T(8,128)(2,1)S(1)}, bf16[640,128]{1,0:T(8,128)(2,1)S(1)}, u32[]{:S(2)}, u32[]{:S(2)}) collective-permute-start(bf16[640,128]{1,0:T(8,128)(2,1)S(1)} %get-tuple-element.71), channel_id=1, source_target_pairs={{0,16},{8,24},{16,0},{24,8},{1,17},{9,25},{17,1},{25,9},{2,18},{10... | collective-permute-start | bytes 491528 | tf_op jit(solution)/shard_map/ppermute | solution.py:27
  29.2 7.3 %collective-permute-start.12 = (bf16[640,128]{1,0:T(8,128)(2,1)S(1)}, bf16[640,128]{1,0:T(8,128)(2,1)S(1)}, u32[]{:S(2)}, u32[]{:S(2)}) collective-permute-start(bf16[640,128]{1,0:T(8,128)(2,1)S(1)} %get-tuple-element.72), channel_id=1, source_target_pairs={{0,8},{8,16},{16,24},{24,0},{1,9},{9,17},{17,25},{25,1},{2,10},{10... | collective-permute-start | bytes 491528 | tf_op jit(solution)/shard_map/ppermute | solution.py:27
  30.3 6.2 %collective-permute-start.9 = (bf16[448,128]{1,0:T(8,128)(2,1)S(1)}, bf16[448,128]{1,0:T(8,128)(2,1)S(1)}, u32[]{:S(2)}, u32[]{:S(2)}) collective-permute-start(bf16[448,128]{1,0:T(8,128)(2,1)S(1)} %pad_maximum_fusion.2), channel_id=1, source_target_pairs={{0,2},{1,3},{2,0},{3,1},{4,6},{5,7},{6,4},{7,5},{8,10},{9,11},{10,... | collective-permute-start | bytes 344072 | tf_op jit(solution)/shard_map/ppermute | solution.py:37
  40.4 4.4 %collective-permute-start.14 = (bf16[8,128,128]{2,1,0:T(8,128)(2,1)S(1)}, bf16[8,128,128]{2,1,0:T(8,128)(2,1)S(1)}, u32[]{:S(2)}, u32[]{:S(2)}) collective-permute-start(bf16[8,128,128]{2,1,0:T(8,128)(2,1)S(1)} %get-tuple-element.81), channel_id=1, source_target_pairs={{0,1},{1,0},{2,3},{3,2},{4,5},{5,4},{6,7},{7,6},{8,9},{9,8},{10,11... | collective-permute-start | bytes 786440 | tf_op jit(solution)/shard_map/ppermute | solution.py:42
  40.6 8.0 %collective-permute-start.18 = (bf16[640,128]{1,0:T(8,128)(2,1)S(1)}, bf16[640,128]{1,0:T(8,128)(2,1)S(1)}, u32[]{:S(2)}, u32[]{:S(2)}) collective-permute-start(bf16[640,128]{1,0:T(8,128)(2,1)S(1)} %bitcast.57), channel_id=1, source_target_pairs={{0,8},{8,16},{16,24},{24,0},{1,9},{9,17},{17,25},{25,1},{2,10},{10... | collective-permute-start | bytes 491528 | tf_op jit(solution)/shard_map/ppermute | solution.py:27
  41.2 9.7 %collective-permute-start.19 = (bf16[640,128]{1,0:T(8,128)(2,1)S(1)}, bf16[640,128]{1,0:T(8,128)(2,1)S(1)}, u32[]{:S(2)}, u32[]{:S(2)}) collective-permute-start(bf16[640,128]{1,0:T(8,128)(2,1)S(1)} %bitcast.56), channel_id=1, source_target_pairs={{0,16},{8,24},{16,0},{24,8},{1,17},{9,25},{17,1},{25,9},{2,18},{10... | collective-permute-start | bytes 491528 | tf_op jit(solution)/shard_map/ppermute | solution.py:27
  42.2 9.1 %collective-permute-start.20 = (bf16[640,128]{1,0:T(8,128)(2,1)S(1)}, bf16[640,128]{1,0:T(8,128)(2,1)S(1)}, u32[]{:S(2)}, u32[]{:S(2)}) collective-permute-start(bf16[640,128]{1,0:T(8,128)(2,1)S(1)} %bitcast.55), channel_id=1, source_target_pairs={{0,24},{8,0},{16,8},{24,16},{1,25},{9,1},{17,9},{25,17},{2,26},{10... | collective-permute-start | bytes 491528 | tf_op jit(solution)/shard_map/ppermute | solution.py:27
  44.9 10.3 %collective-permute-start.15 = (bf16[2,128,128]{2,1,0:T(8,128)(2,1)S(1)}, bf16[2,128,128]{2,1,0:T(8,128)(2,1)S(1)}, u32[]{:S(2)}, u32[]{:S(2)}) collective-permute-start(bf16[2,128,128]{2,1,0:T(8,128)(2,1)S(1)} %get-tuple-element.112), channel_id=1, source_target_pairs={{0,4},{1,5},{2,6},{3,7},{4,0},{5,1},{6,2},{7,3},{8,12},{9,13},{10,... | collective-permute-start | bytes 196616 | tf_op jit(solution)/shard_map/ppermute | solution.py:37
  46.3 9.0 %collective-permute-start.16 = (bf16[2,128,128]{2,1,0:T(8,128)(2,1)S(1)}, bf16[2,128,128]{2,1,0:T(8,128)(2,1)S(1)}, u32[]{:S(2)}, u32[]{:S(2)}) collective-permute-start(bf16[2,128,128]{2,1,0:T(8,128)(2,1)S(1)} %get-tuple-element.111), channel_id=1, source_target_pairs={{0,2},{1,3},{2,0},{3,1},{4,6},{5,7},{6,4},{7,5},{8,10},{9,11},{10,... | collective-permute-start | bytes 196616 | tf_op jit(solution)/shard_map/ppermute | solution.py:37
  48.6 6.7 %collective-permute-start.17 = (bf16[2,128,128]{2,1,0:T(8,128)(2,1)S(1)}, bf16[2,128,128]{2,1,0:T(8,128)(2,1)S(1)}, u32[]{:S(2)}, u32[]{:S(2)}) collective-permute-start(bf16[2,128,128]{2,1,0:T(8,128)(2,1)S(1)} %get-tuple-element.110), channel_id=1, source_target_pairs={{0,6},{1,7},{2,4},{3,5},{4,2},{5,3},{6,0},{7,1},{8,14},{9,15},{10,... | collective-permute-start | bytes 196616 | tf_op jit(solution)/shard_map/ppermute | solution.py:37
  52.0 17.6 %collective-permute-start.28 = (bf16[1280,128]{1,0:T(8,128)(2,1)S(1)}, bf16[1280,128]{1,0:T(8,128)(2,1)S(1)}, u32[]{:S(2)}, u32[]{:S(2)}) collective-permute-start(bf16[1280,128]{1,0:T(8,128)(2,1)S(1)} %get-tuple-element.87), channel_id=1, source_target_pairs={{0,24},{8,0},{16,8},{24,16},{1,25},{9,1},{17,9},{25,17},{2,26},{10... | collective-permute-start | bytes 983048 | tf_op jit(solution)/shard_map/ppermute | solution.py:27
  54.0 15.7 %collective-permute-start.29 = (bf16[1280,128]{1,0:T(8,128)(2,1)S(1)}, bf16[1280,128]{1,0:T(8,128)(2,1)S(1)}, u32[]{:S(2)}, u32[]{:S(2)}) collective-permute-start(bf16[1280,128]{1,0:T(8,128)(2,1)S(1)} %get-tuple-element.88), channel_id=1, source_target_pairs={{0,16},{8,24},{16,0},{24,8},{1,17},{9,25},{17,1},{25,9},{2,18},{10... | collective-permute-start | bytes 983048 | tf_op jit(solution)/shard_map/ppermute | solution.py:27
  55.2 14.4 %collective-permute-start.30 = (bf16[1280,128]{1,0:T(8,128)(2,1)S(1)}, bf16[1280,128]{1,0:T(8,128)(2,1)S(1)}, u32[]{:S(2)}, u32[]{:S(2)}) collective-permute-start(bf16[1280,128]{1,0:T(8,128)(2,1)S(1)} %get-tuple-element.89), channel_id=1, source_target_pairs={{0,8},{8,16},{16,24},{24,0},{1,9},{9,17},{17,25},{25,1},{2,10},{10... | collective-permute-start | bytes 983048 | tf_op jit(solution)/shard_map/ppermute | solution.py:27
  55.5 5.3 %collective-permute-start.21 = (bf16[256,128]{1,0:T(8,128)(2,1)S(1)}, bf16[256,128]{1,0:T(8,128)(2,1)S(1)}, u32[]{:S(2)}, u32[]{:S(2)}) collective-permute-start(bf16[256,128]{1,0:T(8,128)(2,1)S(1)} %fusion.4), channel_id=1, source_target_pairs={{0,4},{1,5},{2,6},{3,7},{4,0},{5,1},{6,2},{7,3},{8,12},{9,13},{10,... | collective-permute-start | bytes 196616 | tf_op jit(solution)/shard_map/ppermute | solution.py:37
  56.8 5.3 %collective-permute-start.22 = (bf16[256,128]{1,0:T(8,128)(2,1)S(1)}, bf16[256,128]{1,0:T(8,128)(2,1)S(1)}, u32[]{:S(2)}, u32[]{:S(2)}) collective-permute-start(bf16[256,128]{1,0:T(8,128)(2,1)S(1)} %fusion.4), channel_id=1, source_target_pairs={{0,2},{1,3},{2,0},{3,1},{4,6},{5,7},{6,4},{7,5},{8,10},{9,11},{10,... | collective-permute-start | bytes 196616 | tf_op jit(solution)/shard_map/ppermute | solution.py:37
  60.8 4.3 %collective-permute-start.23 = (bf16[256,128]{1,0:T(8,128)(2,1)S(1)}, bf16[256,128]{1,0:T(8,128)(2,1)S(1)}, u32[]{:S(2)}, u32[]{:S(2)}) collective-permute-start(bf16[256,128]{1,0:T(8,128)(2,1)S(1)} %collective-permute-done.21), channel_id=1, source_target_pairs={{0,2},{1,3},{2,0},{3,1},{4,6},{5,7},{6,4},{7,5},{8,10},{9,11},{10,... | collective-permute-start | bytes 196616 | tf_op jit(solution)/shard_map/ppermute | solution.py:37
  (18 other events, 116.2 us)
